TPU v7x, 512 devices: a whole 4x4x16 slice. The times are simulated.
512 devices in a mesh: blk: 8 (over y_lo, x), dp: 64 (over y_hi, z, core).
Axes of the slice: x: 4, y: 4 (y_hi: 2, y_lo: 2; y = y_hi * 2 + y_lo), z: 16, core: 2. Of those that a mesh axis runs over, the one named last changes fastest.
Arguments:
- features: bfloat16 [8, 64, 4, 32, 512], P('blk', 'dp'), may hold values from -16 to 16
- conv_weight: bfloat16 [9, 512, 1024], P(None, None, 'blk'), may hold values from -0.09375 to 0.09375
- projection: bfloat16 [1024, 512], P('blk'), may hold values from -0.1875 to 0.1875
- text: bfloat16 [8, 64, 512], P('blk', 'dp'), may hold values from -6 to 6
- labels: int32 [8, 64], P('blk', 'dp'), may hold values from 0 to 7
Outputs:
- grad_features: bfloat16 [8, 64, 4, 32, 512], P('blk', 'dp')
- grad_weight: float32 [9, 512, 1024], P(None, 'dp', 'blk')
- grad_text: float32 [8, 64, 512], P('blk', 'dp')
Inputs may be any that keep to these rules, and one draw needn't show every extreme that they name: labels index the captions of the clip's own group.
All inputs are finite; a program needn't handle non-finite values.
Results may differ from a plain program's by a relative error of at most 0.018.
Values may be sent and summed in bfloat16 or wider, within the bound.
No kernel may reach another device: no remote copies, remote signals or barrier semaphores. Data moves between devices by JAX's collectives and lax.ppermute only.
A program may use at most 64 MiB of HBM per device.

v0:
```python
import jax
import jax.numpy as jnp
from jax import lax
from jax.sharding import PartitionSpec as P

logit_scale = 10.0
logit_bias = -2.0
loss_scale = 1024.0
norm_eps = 1e-06


def from_behind(block, axis, distance):
    devices = range(lax.axis_size(axis))
    route = [((i - distance) % len(devices), i) for i in devices]
    return lax.ppermute(block, axis, route)


def conv_forward(inputs, weights):
    clip_count, freq_bins, frames, _ = inputs.shape
    padded = jnp.pad(inputs, ((0, 0), (1, 1), (1, 1), (0, 0)))
    result = jnp.zeros((clip_count * freq_bins * frames, weights.shape[2]), jnp.float32)
    for row_shift in range(3):
        for col_shift in range(3):
            window = padded[:, col_shift : col_shift + freq_bins, row_shift : row_shift + frames, :]
            window = window.reshape(clip_count * freq_bins * frames, -1)
            result = result + jnp.dot(
                window, weights[3 * row_shift + col_shift], preferred_element_type=jnp.float32
            )
    return result.reshape(clip_count, freq_bins, frames, -1)


def weight_gradient(inputs, grads):
    clip_count, freq_bins, frames, _ = inputs.shape
    padded = jnp.pad(inputs, ((0, 0), (1, 1), (1, 1), (0, 0)))
    flat_grads = grads.reshape(clip_count * freq_bins * frames, -1)
    taps = []
    for row_shift in range(3):
        for col_shift in range(3):
            window = padded[:, col_shift : col_shift + freq_bins, row_shift : row_shift + frames, :]
            window = window.reshape(clip_count * freq_bins * frames, -1)
            taps.append(
                lax.dot_general(
                    window, flat_grads, (((0,), (0,)), ((), ())), preferred_element_type=jnp.float32
                )
            )
    return jnp.stack(taps)


def input_gradient(grads, weights):
    clip_count, freq_bins, frames, _ = grads.shape
    padded = jnp.pad(grads, ((0, 0), (1, 1), (1, 1), (0, 0)))
    result = jnp.zeros((clip_count * freq_bins * frames, weights.shape[1]), jnp.float32)
    for row_shift in range(3):
        for col_shift in range(3):
            window = padded[
                :,
                2 - col_shift : 2 - col_shift + freq_bins,
                2 - row_shift : 2 - row_shift + frames,
                :,
            ]
            window = window.reshape(clip_count * freq_bins * frames, -1)
            result = result + lax.dot_general(
                window,
                weights[3 * row_shift + col_shift],
                (((1,), (1,)), ((), ())),
                preferred_element_type=jnp.float32,
            )
    return result.reshape(clip_count, freq_bins, frames, -1)


def silu_slope(values):
    sigma = jax.nn.sigmoid(values)
    return sigma * (1.0 + values * (1.0 - sigma))


def pair_gradient(audio_unit, captions, clip_labels, first_index):
    logits = (
        logit_scale * jnp.dot(audio_unit, captions.T, precision=lax.Precision.HIGHEST) + logit_bias
    )
    columns = first_index + jnp.arange(captions.shape[0], dtype=jnp.int32)
    signs = jnp.where(clip_labels[:, None] == columns[None, :], 1.0, -1.0).astype(logits.dtype)
    return -loss_scale * signs * jax.nn.sigmoid(-signs * logits)


def shards(features, conv_weight, projection, text, labels):
    clip_count = features.shape[0]
    freq_bins = features.shape[2]
    frames = features.shape[3]
    local_clips = features[:, 0]
    gathered = lax.all_gather(local_clips, "blk", axis=0, tiled=True)
    preact = conv_forward(gathered, conv_weight)
    pooled = jnp.mean(jax.nn.silu(preact), axis=(1, 2)).astype(jnp.bfloat16)
    partial_embedding = jnp.dot(pooled, projection, preferred_element_type=jnp.float32)
    embedding = lax.psum_scatter(partial_embedding, "blk", scatter_dimension=0, tiled=True)
    inv_audio = lax.rsqrt(jnp.sum(embedding * embedding, axis=-1, keepdims=True) + norm_eps)
    audio_unit = embedding * inv_audio
    text_values = text[:, 0].astype(jnp.float32)
    inv_text = lax.rsqrt(jnp.sum(text_values * text_values, axis=-1, keepdims=True) + norm_eps)
    caption = text_values * inv_text
    clip_labels = labels[:, 0]
    position = lax.axis_index("blk")
    members = lax.axis_size("blk")

    def visit(rotation, carry_state):
        carried, audio_grad = carry_state
        source = (position - rotation) % members
        pair_grad = pair_gradient(audio_unit, carried[0], clip_labels, source * clip_count)
        audio_grad = audio_grad + logit_scale * jnp.dot(
            pair_grad, carried[0], precision=lax.Precision.HIGHEST
        )
        update = carried[1] + logit_scale * jnp.dot(
            pair_grad.T, audio_unit, precision=lax.Precision.HIGHEST
        )
        carried = from_behind(jnp.stack((carried[0], update)), "blk", 1)
        return (carried, audio_grad)

    start_state = (jnp.stack((caption, jnp.zeros_like(caption))), jnp.zeros_like(audio_unit))
    carried, audio_grad = lax.fori_loop(0, members, visit, start_state)
    caption_grad = carried[1]
    grad_text = (
        caption_grad - caption * jnp.sum(caption * caption_grad, axis=-1, keepdims=True)
    ) * inv_text
    embedding_grad = (
        (audio_grad - audio_unit * jnp.sum(audio_unit * audio_grad, axis=-1, keepdims=True))
        * inv_audio
    ).astype(jnp.bfloat16)
    group_grads = lax.all_gather(embedding_grad, "blk", axis=0, tiled=True)
    pooled_grad = lax.dot_general(
        group_grads, projection, (((1,), (1,)), ((), ())), preferred_element_type=jnp.float32
    )
    cell_count = frames * freq_bins
    pre_grad = (pooled_grad[:, None, None, :] / cell_count * silu_slope(preact)).astype(
        jnp.bfloat16
    )
    group_total = lax.axis_size("dp")
    weight_term = weight_gradient(gathered, pre_grad) / group_total
    grad_weight = lax.psum_scatter(weight_term, "dp", scatter_dimension=1, tiled=True)
    feature_sum = lax.psum_scatter(
        input_gradient(pre_grad, conv_weight).astype(jnp.bfloat16),
        "blk",
        scatter_dimension=0,
        tiled=True,
    )
    grad_features = feature_sum[:, None]
    return (grad_features, grad_weight, grad_text[:, None])


def solution(mesh):
    placed = (
        P("blk", "dp", None, None, None),
        P(None, None, "blk"),
        P("blk", None),
        P("blk", "dp", None),
        P("blk", "dp"),
    )
    return jax.shard_map(
        shards,
        mesh=mesh,
        in_specs=placed,
        out_specs=(P("blk", "dp", None, None, None), P(None, "dp", "blk"), P("blk", "dp", None)),
        check_vma=False,
    )
```

profile of v0, /device:TPU:6, one launch (start us, length us, event | category | flops | bytes accessed | tf_op | source)
XLA Modules:
  0.0 488.5 jit_solution(30386006181531581)
XLA Ops:
  8.0 1.3 multiply_reduce_fusion.5
  10.0 1.3 dynamic-slice
  11.9 47.1 %all-gather.4.cloned.1.call-done = bf16[8,1,4,32,512]{4,3,2,1,0:T(8,128)(2,1)} async-done(((bf16[1,1,4,32,512]{4,3,2,1,0:T(8,128)(2,1)}), bf16[8,1,4,32,512]{4,3,2,1,0:T(8,128)(2,1)}) %all-gather.4.cloned.1.call-update) | async-done | bytes 1048592 | tf_op jit(solution)/shard_map/all_gather | solution.py:90
  59.1 6.0 %pad_slice_fusion = (bf16[8,4,32,512]{3,2,1,0:T(8,128)(2,1)S(1)}, bf16[8,4,32,512]{3,2,1,0:T(8,128)(2,1)S(1)}, bf16[8,4,32,512]{3,2,1,0:T(8,128)(2,1)S(1)}, bf16...) fusion(bf16[8,4,32,512]{3,2,1,0:T(8,128)(2,1)} %bitcast.206), kind=kLoop, calls=%fused_computation.6 | loop fusion | bytes 9437184 | tf_op jit(solution)/shard_map/slice | solution.py:24
  69.5 30.2 %all-reduce.3 = f32[8,512]{1,0:T(8,128)S(1)} all-reduce(f32[8,512]{1,0:T(8,128)S(1)} %fusion.58), channel_id=3, replica_groups=mesh['blk'=8,'dp'=64] {'blk'}, use_global_device_ids=true, to_apply=%region_2.3.clone | all-reduce | flops 4096 | bytes 32768
  99.7 1.3 multiply_reduce_fusion.4
  102.5 78.2 %while.18 = (s32[]{:T(128)}, f32[2,1,512]{2,1,0:T(1,128)S(1)}, f32[1,512]{1,0:T(1,128)S(1)}, s32[]{:T(128)}, s32[1,1]{1,0:T(1,128)}, /*index=5*/f32[1,512]{1,0:T...) while((s32[]{:T(128)}, f32[2,1,512]{2,1,0:T(1,128)S(1)}, ...), condition=%wide.region_5.6_spmd.clone, body=%wide.region_4.5_spmd.clone.sunk | while | flops 5657 | bytes 53702 | solution.py:118
  104.7 6.3 %collective-permute-start = (f32[2,1,512]{2,1,0:T(1,128)S(1)}, f32[2,1,512]{2,1,0:T(1,128)S(1)}, u32[]{:S(2)}, u32[]{:S(2)}) collective-permute-start(f32[2,1,512]{2,1,0:T(1,128)S(1)} %pad_maximum_fusion.2), channel_id=1, source_target_pairs={{448,0},{0,64},{64,128},{128,192},{192,256},{256,320},{320,384},{3... | collective-permute-start | bytes 12296 | tf_op jit(solution)/shard_map/while/body/eval_jaxpr/ppermute | solution.py:15
  114.4 6.3 %collective-permute-start = (f32[2,1,512]{2,1,0:T(1,128)S(1)}, f32[2,1,512]{2,1,0:T(1,128)S(1)}, u32[]{:S(2)}, u32[]{:S(2)}) collective-permute-start(f32[2,1,512]{2,1,0:T(1,128)S(1)} %pad_maximum_fusion.2), channel_id=1, source_target_pairs={{448,0},{0,64},{64,128},{128,192},{192,256},{256,320},{320,384},{3... | collective-permute-start | bytes 12296 | tf_op jit(solution)/shard_map/while/body/eval_jaxpr/ppermute | solution.py:15
  120.8 1.3 collective-permute-done
  124.2 6.3 %collective-permute-start = (f32[2,1,512]{2,1,0:T(1,128)S(1)}, f32[2,1,512]{2,1,0:T(1,128)S(1)}, u32[]{:S(2)}, u32[]{:S(2)}) collective-permute-start(f32[2,1,512]{2,1,0:T(1,128)S(1)} %pad_maximum_fusion.2), channel_id=1, source_target_pairs={{448,0},{0,64},{64,128},{128,192},{192,256},{256,320},{320,384},{3... | collective-permute-start | bytes 12296 | tf_op jit(solution)/shard_map/while/body/eval_jaxpr/ppermute | solution.py:15
  130.5 1.3 collective-permute-done
  134.0 6.3 %collective-permute-start = (f32[2,1,512]{2,1,0:T(1,128)S(1)}, f32[2,1,512]{2,1,0:T(1,128)S(1)}, u32[]{:S(2)}, u32[]{:S(2)}) collective-permute-start(f32[2,1,512]{2,1,0:T(1,128)S(1)} %pad_maximum_fusion.2), channel_id=1, source_target_pairs={{448,0},{0,64},{64,128},{128,192},{192,256},{256,320},{320,384},{3... | collective-permute-start | bytes 12296 | tf_op jit(solution)/shard_map/while/body/eval_jaxpr/ppermute | solution.py:15
  140.3 1.3 collective-permute-done
  143.7 6.3 %collective-permute-start = (f32[2,1,512]{2,1,0:T(1,128)S(1)}, f32[2,1,512]{2,1,0:T(1,128)S(1)}, u32[]{:S(2)}, u32[]{:S(2)}) collective-permute-start(f32[2,1,512]{2,1,0:T(1,128)S(1)} %pad_maximum_fusion.2), channel_id=1, source_target_pairs={{448,0},{0,64},{64,128},{128,192},{192,256},{256,320},{320,384},{3... | collective-permute-start | bytes 12296 | tf_op jit(solution)/shard_map/while/body/eval_jaxpr/ppermute | solution.py:15
  153.5 6.3 %collective-permute-start = (f32[2,1,512]{2,1,0:T(1,128)S(1)}, f32[2,1,512]{2,1,0:T(1,128)S(1)}, u32[]{:S(2)}, u32[]{:S(2)}) collective-permute-start(f32[2,1,512]{2,1,0:T(1,128)S(1)} %pad_maximum_fusion.2), channel_id=1, source_target_pairs={{448,0},{0,64},{64,128},{128,192},{192,256},{256,320},{320,384},{3... | collective-permute-start | bytes 12296 | tf_op jit(solution)/shard_map/while/body/eval_jaxpr/ppermute | solution.py:15
  163.3 6.3 %collective-permute-start = (f32[2,1,512]{2,1,0:T(1,128)S(1)}, f32[2,1,512]{2,1,0:T(1,128)S(1)}, u32[]{:S(2)}, u32[]{:S(2)}) collective-permute-start(f32[2,1,512]{2,1,0:T(1,128)S(1)} %pad_maximum_fusion.2), channel_id=1, source_target_pairs={{448,0},{0,64},{64,128},{128,192},{192,256},{256,320},{320,384},{3... | collective-permute-start | bytes 12296 | tf_op jit(solution)/shard_map/while/body/eval_jaxpr/ppermute | solution.py:15
  173.1 6.3 %collective-permute-start = (f32[2,1,512]{2,1,0:T(1,128)S(1)}, f32[2,1,512]{2,1,0:T(1,128)S(1)}, u32[]{:S(2)}, u32[]{:S(2)}) collective-permute-start(f32[2,1,512]{2,1,0:T(1,128)S(1)} %pad_maximum_fusion.2), channel_id=1, source_target_pairs={{448,0},{0,64},{64,128},{128,192},{192,256},{256,320},{320,384},{3... | collective-permute-start | bytes 12296 | tf_op jit(solution)/shard_map/while/body/eval_jaxpr/ppermute | solution.py:15
  181.9 1.3 convert_bitcast_fusion
  183.2 23.9 %all-gather.1 = bf16[8,1,512]{2,1,0:T(2,128)(2,1)S(1)} all-gather(bf16[1,1,512]{2,1,0:T(2,128)(2,1)S(1)} %convert_bitcast_fusion), channel_id=1, replica_groups=mesh['blk'=8,'dp'=64] {'blk'}, dimensions={0}, use_global_device_ids=true | all-gather | bytes 9216 | tf_op jit(solution)/shard_map/all_gather | solution.py:127
  212.8 1.9 add_convert_fusion
  224.6 3.2 broadcast_multiply_fusion
  230.2 32.4 %reduce-scatter.3.cloned.1.call-done = bf16[1,4,32,512]{3,2,1,0:T(8,128)(2,1)} async-done(((bf16[8,4,32,512]{3,2,1,0:T(8,128)(2,1)}), bf16[1,4,32,512]{3,2,1,0:T(8,128)(2,1)}) %reduce-scatter.3.cloned.1.call-update) | async-done | bytes 131088 | tf_op jit(solution)/shard_map/reduce_scatter | solution.py:138
  262.6 219.3 %reduce-scatter.5.cloned.1.call-done = f32[9,8,128]{2,1,0:T(8,128)} async-done(((f32[9,512,128]{2,1,0:T(8,128)}), f32[9,8,128]{2,1,0:T(8,128)}) %reduce-scatter.5.cloned.1.call-update) | async-done | bytes 36880 | tf_op jit(solution)/shard_map/reduce_scatter | solution.py:137
  (105 shorter events, 37.7 us)
Async XLA Ops:
  7.2 62.2 %copy-start = (bf16[128,512]{1,0:T(8,128)(2,1)S(1)}, bf16[128,512]{1,0:T(8,128)(2,1)}, u32[]{:S(2)}) copy-start(bf16[128,512]{1,0:T(8,128)(2,1)} %param.9) | copy-start | bytes 393220
  7.2 51.9 %all-gather.4.cloned.1.call-start = ((), (), s32[]{:S(2)}) async-start(), calls=%async_computation.4 | async-start | bytes 1179648 | tf_op jit(solution)/shard_map/all_gather | solution.py:90
  7.9 254.7 %reduce-scatter.3.cloned.1.call-start = ((), (), s32[]{:S(2)}) async-start(), calls=%async_computation.2 | async-start | bytes 1179648 | tf_op jit(solution)/shard_map/reduce_scatter | solution.py:138
  59.1 6.0 %copy-start.2 = (bf16[9,512,128]{2,1,0:T(8,128)(2,1)S(1)}, bf16[9,512,128]{2,1,0:T(8,128)(2,1)}, u32[]{:S(2)}) copy-start(bf16[9,512,128]{2,1,0:T(8,128)(2,1)} %param.8) | copy-start | bytes 3538948
  65.9 1.2 copy-start.1
  104.7 7.6 %collective-permute-start = (f32[2,1,512]{2,1,0:T(1,128)S(1)}, f32[2,1,512]{2,1,0:T(1,128)S(1)}, u32[]{:S(2)}, u32[]{:S(2)}) collective-permute-start(f32[2,1,512]{2,1,0:T(1,128)S(1)} %pad_maximum_fusion.2), channel_id=1, source_target_pairs={{448,0},{0,64},{64,128},{128,192},{192,256},{256,320},{320,384},{3... | collective-permute-start | bytes 12296 | tf_op jit(solution)/shard_map/while/body/eval_jaxpr/ppermute | solution.py:15
  114.4 7.6 %collective-permute-start = (f32[2,1,512]{2,1,0:T(1,128)S(1)}, f32[2,1,512]{2,1,0:T(1,128)S(1)}, u32[]{:S(2)}, u32[]{:S(2)}) collective-permute-start(f32[2,1,512]{2,1,0:T(1,128)S(1)} %pad_maximum_fusion.2), channel_id=1, source_target_pairs={{448,0},{0,64},{64,128},{128,192},{192,256},{256,320},{320,384},{3... | collective-permute-start | bytes 12296 | tf_op jit(solution)/shard_map/while/body/eval_jaxpr/ppermute | solution.py:15
  124.2 7.6 %collective-permute-start = (f32[2,1,512]{2,1,0:T(1,128)S(1)}, f32[2,1,512]{2,1,0:T(1,128)S(1)}, u32[]{:S(2)}, u32[]{:S(2)}) collective-permute-start(f32[2,1,512]{2,1,0:T(1,128)S(1)} %pad_maximum_fusion.2), channel_id=1, source_target_pairs={{448,0},{0,64},{64,128},{128,192},{192,256},{256,320},{320,384},{3... | collective-permute-start | bytes 12296 | tf_op jit(solution)/shard_map/while/body/eval_jaxpr/ppermute | solution.py:15
  134.0 7.6 %collective-permute-start = (f32[2,1,512]{2,1,0:T(1,128)S(1)}, f32[2,1,512]{2,1,0:T(1,128)S(1)}, u32[]{:S(2)}, u32[]{:S(2)}) collective-permute-start(f32[2,1,512]{2,1,0:T(1,128)S(1)} %pad_maximum_fusion.2), channel_id=1, source_target_pairs={{448,0},{0,64},{64,128},{128,192},{192,256},{256,320},{320,384},{3... | collective-permute-start | bytes 12296 | tf_op jit(solution)/shard_map/while/body/eval_jaxpr/ppermute | solution.py:15
  143.7 7.6 %collective-permute-start = (f32[2,1,512]{2,1,0:T(1,128)S(1)}, f32[2,1,512]{2,1,0:T(1,128)S(1)}, u32[]{:S(2)}, u32[]{:S(2)}) collective-permute-start(f32[2,1,512]{2,1,0:T(1,128)S(1)} %pad_maximum_fusion.2), channel_id=1, source_target_pairs={{448,0},{0,64},{64,128},{128,192},{192,256},{256,320},{320,384},{3... | collective-permute-start | bytes 12296 | tf_op jit(solution)/shard_map/while/body/eval_jaxpr/ppermute | solution.py:15
  153.5 7.6 %collective-permute-start = (f32[2,1,512]{2,1,0:T(1,128)S(1)}, f32[2,1,512]{2,1,0:T(1,128)S(1)}, u32[]{:S(2)}, u32[]{:S(2)}) collective-permute-start(f32[2,1,512]{2,1,0:T(1,128)S(1)} %pad_maximum_fusion.2), channel_id=1, source_target_pairs={{448,0},{0,64},{64,128},{128,192},{192,256},{256,320},{320,384},{3... | collective-permute-start | bytes 12296 | tf_op jit(solution)/shard_map/while/body/eval_jaxpr/ppermute | solution.py:15
  163.3 7.6 %collective-permute-start = (f32[2,1,512]{2,1,0:T(1,128)S(1)}, f32[2,1,512]{2,1,0:T(1,128)S(1)}, u32[]{:S(2)}, u32[]{:S(2)}) collective-permute-start(f32[2,1,512]{2,1,0:T(1,128)S(1)} %pad_maximum_fusion.2), channel_id=1, source_target_pairs={{448,0},{0,64},{64,128},{128,192},{192,256},{256,320},{320,384},{3... | collective-permute-start | bytes 12296 | tf_op jit(solution)/shard_map/while/body/eval_jaxpr/ppermute | solution.py:15
  173.1 7.6 %collective-permute-start = (f32[2,1,512]{2,1,0:T(1,128)S(1)}, f32[2,1,512]{2,1,0:T(1,128)S(1)}, u32[]{:S(2)}, u32[]{:S(2)}) collective-permute-start(f32[2,1,512]{2,1,0:T(1,128)S(1)} %pad_maximum_fusion.2), channel_id=1, source_target_pairs={{448,0},{0,64},{64,128},{128,192},{192,256},{256,320},{320,384},{3... | collective-permute-start | bytes 12296 | tf_op jit(solution)/shard_map/while/body/eval_jaxpr/ppermute | solution.py:15
  214.8 267.2 %reduce-scatter.5.cloned.1.call-start = ((), (), s32[]{:S(2)}) async-start(), calls=%async_computation.3 | async-start | bytes 2396160 | tf_op jit(solution)/shard_map/reduce_scatter | solution.py:137
  227.8 0.7 copy-start.3
Sparse Core Ops, SparseCore 0:
  10.1 48.9 all-gather.3
  214.9 47.7 reduce-scatter.2
  267.9 214.0 reduce-scatter.4
where the time goes:
time: 489 us; the launch traced here: 488 us
  waiting for transfers between devices  310 us (63%)
  blocking collectives  54.1 us (11%)
  starting transfers between devices  50.7 us (10%)
  matrix products  20.3 us (4%)
  other arithmetic  17.6 us (4%)
  between operations  15.4 us (3%)
  loops' own time  11.9 us (2%)
  local copies, waits for them, and re-layouts  8.78 us (2%)
    reduce_scatter x1, waiting for transfers between devices, shards(): lax.psum_scatter(weight_term, 'dp', scatter_dimension=1, tiled=True)  219 us
    ppermute x8, starting transfers between devices, from_behind(): return lax.ppermute(block, axis, route)  50.4 us
    all_gather x1, waiting for transfers between devices, shards(): gathered = lax.all_gather(local_clips, 'blk', axis=0, tiled=True)  47.1 us
    reduce_scatter x1, waiting for transfers between devices, shards(): lax.psum_scatter(input_gradient(pre_grad, conv_weight).astype(jnp.bfloat1...  32.4 us
    unnamed x1, blocking collectives  30.2 us
    all_gather x1, blocking collectives, shards(): group_grads = lax.all_gather(embedding_grad, 'blk', axis=0, tiled=True)  23.9 us
    another operation x1, loops' own time, shards(): carried, audio_grad = lax.fori_loop(0, members, visit, start_state)  11.9 us
    dot_general x9, matrix products, weight_gradient(): lax.dot_general(window, flat_grads, (((0,), (0,)), ((), ())), preferred_e...  10.7 us
  transfers between devices with their start and end apart: 11, of which 11 were waited for; matrix products, arithmetic and copies ran while one was open for 4% of the time, Pallas kernels for 0%

commit v1 on v0

v1 whole, which is shorter than its diff:
```python
import functools

import jax
import jax.numpy as jnp
from jax import lax
from jax.experimental import pallas as pl
from jax.experimental.pallas import tpu as pltpu
from jax.sharding import Mesh, PartitionSpec as P

logit_scale = 10.0
logit_bias = -2.0
loss_scale = 1024.0
norm_eps = 1e-06

BLK = ("ylo", "x")
Z = "z"
f32 = jnp.float32
bf16 = jnp.bfloat16

clips = 8
freq = 4
frames = 32
cells = freq * frames
text_row = cells
label_row = cells + 1
rows = cells + 16
vmem_limit = 48 * 1024 * 1024


def call(kernel, out_shape, scratch=(), flops=0, moved=0):
    return pl.pallas_call(
        kernel,
        out_shape=out_shape,
        scratch_shapes=scratch,
        compiler_params=pltpu.CompilerParams(vmem_limit_bytes=vmem_limit),
        cost_estimate=pl.CostEstimate(flops=flops, bytes_accessed=moved, transcendentals=0),
    )


def frame_index(count):
    return lax.broadcasted_iota(jnp.int32, (count, 1), 0) % frames


def shift_rows(values, step):
    count = values.shape[0]
    frame = frame_index(count)
    if step == 1:
        return jnp.where(frame == 0, 0.0, pltpu.roll(values, 1, 0))
    return jnp.where(frame == frames - 1, 0.0, pltpu.roll(values, count - 1, 0))


def forward_kernel(group_ref, weight_ref, projection_ref, slope_ref, turned_ref, partial_ref):
    inputs = group_ref[:, :cells, :].reshape(clips * cells, -1)
    turned_ref[...] = inputs.T
    out_width = projection_ref.shape[0]
    preact = None
    for a in range(3):
        product = jnp.dot(
            inputs,
            weight_ref[:, 3 * a * out_width : 3 * (a + 1) * out_width],
            preferred_element_type=f32,
        ).reshape(clips, freq, frames, 3 * out_width)
        low = product[..., :out_width]
        mid = product[..., out_width : 2 * out_width]
        high = product[..., 2 * out_width :]
        bins = []
        for f in range(freq):
            total = mid[:, f]
            if f > 0:
                total = total + low[:, f - 1]
            if f < freq - 1:
                total = total + high[:, f + 1]
            bins.append(total[:, None])
        column = jnp.concatenate(bins, axis=1).reshape(clips * cells, out_width)
        if a == 0:
            column = shift_rows(column, 1)
        if a == 2:
            column = shift_rows(column, -1)
        preact = column if preact is None else preact + column
    sigma = jax.nn.sigmoid(preact)
    slope_ref[...] = sigma * (1.0 + preact * (1.0 - sigma))
    active = (preact * sigma).reshape(clips, cells, out_width)
    pooled = (jnp.sum(active, axis=1) * (1.0 / cells)).astype(bf16)
    partial = jnp.dot(pooled, projection_ref[...], preferred_element_type=f32)
    partial_ref[...] = jnp.broadcast_to(partial[None], partial_ref.shape)


def row_sum(values):
    return jnp.sum(values, axis=-1, keepdims=True)


def pair_column(audio_unit, caption_row, clip_labels, column):
    logits = logit_scale * row_sum(audio_unit * caption_row) + logit_bias
    signs = jnp.where(clip_labels == column, 1.0, -1.0)
    return -loss_scale * signs * jax.nn.sigmoid(-signs * logits)


def input_kernel(
    parts_ref, group_ref, slope_ref, weight_ref, projection_ref, feature_ref, text_ref, shifted_ref
):
    embedding = jnp.sum(parts_ref[...], axis=0)
    inv_audio = lax.rsqrt(row_sum(embedding * embedding) + norm_eps)
    audio_unit = embedding * inv_audio
    clip_labels = jnp.concatenate(
        [group_ref[c, cells : cells + 16, :].astype(f32)[1:2, :1] for c in range(clips)], axis=0
    ).astype(jnp.int32)
    position = lax.axis_index("ylo") * 4 + lax.axis_index("x")

    def caption_at(index):
        text_values = group_ref[index, cells : cells + 16, :].astype(f32)[:1]
        inv_text = lax.rsqrt(row_sum(text_values * text_values) + norm_eps)
        return text_values * inv_text, inv_text

    audio_grad = jnp.zeros_like(audio_unit)
    for j in range(clips):
        caption, _ = caption_at(j)
        audio_grad = audio_grad + pair_column(audio_unit, caption, clip_labels, j) * caption
    audio_grad = logit_scale * audio_grad
    caption, inv_text = caption_at(position)
    own_pairs = pair_column(audio_unit, caption, clip_labels, position)
    caption_grad = logit_scale * jnp.sum(own_pairs * audio_unit, axis=0, keepdims=True)
    text_ref[...] = (caption_grad - caption * row_sum(caption * caption_grad)) * inv_text
    embedding_grad = (
        (audio_grad - audio_unit * row_sum(audio_unit * audio_grad)) * inv_audio
    ).astype(bf16)
    pooled_grad = lax.dot_general(
        embedding_grad, projection_ref[...], (((1,), (1,)), ((), ())), preferred_element_type=f32
    )
    width = pooled_grad.shape[1]
    scaled = pooled_grad * (1.0 / cells)
    pre_grad = (scaled[:, None, :] * slope_ref[...].reshape(clips, cells, width)).astype(bf16)
    pre_grad = pre_grad.astype(f32).reshape(clips * cells, width)
    zeros = jnp.zeros((clips, frames, width), bf16)
    for a in range(3):
        moved = pre_grad
        if a == 0:
            moved = shift_rows(pre_grad, -1)
        if a == 2:
            moved = shift_rows(pre_grad, 1)
        moved = moved.astype(bf16).reshape(clips, freq, frames, width)
        for b in range(3):
            tap = 3 * a + b
            for f in range(freq):
                source = f - (b - 1)
                block = moved[:, source] if 0 <= source < freq else zeros
                shifted_ref[:, f, :, tap * width : (tap + 1) * width] = block
    shifted = shifted_ref[...].reshape(clips * cells, -1)
    result = lax.dot_general(
        shifted, weight_ref[...], (((1,), (1,)), ((), ())), preferred_element_type=f32
    )
    feature_ref[...] = result.astype(bf16).reshape(feature_ref.shape)


def weight_kernel(turned_ref, shifted_ref, kept_ref, sent_ref, total_ref):
    width = shifted_ref.shape[-1]
    shifted = shifted_ref[...].reshape(clips * cells, width)
    total_ref[...] = jnp.dot(turned_ref[...], shifted, preferred_element_type=f32).reshape(
        total_ref.shape
    )
    core = lax.axis_index("core")
    kept_ref[...] = total_ref[:, core].reshape(kept_ref.shape)
    sent_ref[...] = total_ref[:, 1 - core].reshape(sent_ref.shape).astype(bf16)


def half_kernel(kept_ref, came_ref, mine_ref, sent_ref, total_ref):
    total_ref[...] = (kept_ref[...] + came_ref[...].astype(f32)).reshape(total_ref.shape)
    side = lax.axis_index("yhi")
    mine_ref[...] = total_ref[side]
    sent_ref[...] = total_ref[1 - side].astype(bf16)


def add_kernel(kept_ref, came_ref, sent_ref):
    sent_ref[...] = (kept_ref[...] + came_ref[...].astype(f32)).astype(bf16)


def final_kernel(group_total, parts_ref, out_ref):
    total = jnp.sum(parts_ref[...].astype(f32), axis=0) * (1.0 / group_total)
    taps, _, width = out_ref.shape
    for tap in range(taps):
        out_ref[tap] = total[:, tap * width : (tap + 1) * width]


def swap(values, axis):
    return lax.ppermute(values, axis, [(0, 1), (1, 0)])


def shards(features, conv_weight, projection, text, labels):
    taps, channels, width = conv_weight.shape
    wide = taps * width
    own = jnp.concatenate(
        [
            features.reshape(cells, channels),
            text.reshape(1, channels),
            jnp.broadcast_to(labels.astype(bf16).reshape(1, 1), (1, channels)),
            jnp.zeros((rows - cells - 2, channels), bf16),
        ]
    )
    weight = jnp.transpose(conv_weight, (1, 0, 2)).reshape(channels, wide)
    group = lax.all_to_all(jnp.broadcast_to(own[None], (clips, rows, channels)), BLK, 0, 0)
    slope, turned, partial = call(
        forward_kernel,
        (
            jax.ShapeDtypeStruct((clips * cells, width), f32),
            jax.ShapeDtypeStruct((channels, clips * cells), bf16),
            jax.ShapeDtypeStruct((clips, clips, projection.shape[1]), f32),
        ),
        flops=2 * clips * cells * channels * wide,
    )(group, weight, projection)
    parts = lax.all_to_all(partial, BLK, 0, 0)
    feature_part, grad_text, shifted = call(
        input_kernel,
        (
            jax.ShapeDtypeStruct((clips, cells, channels), bf16),
            jax.ShapeDtypeStruct((1, channels), f32),
            jax.ShapeDtypeStruct((clips, freq, frames, wide), bf16),
        ),
        flops=2 * clips * cells * channels * wide,
    )(parts, group, slope, weight, projection)
    feature_sum = lax.psum_scatter(feature_part, BLK, scatter_dimension=0, tiled=True)
    half = channels // 2
    quarter = half // 2
    kept, sent = call(
        weight_kernel,
        (jax.ShapeDtypeStruct((half, wide), f32), jax.ShapeDtypeStruct((half, wide), bf16)),
        scratch=[pltpu.VMEM((channels // 16, 2, 8, wide), f32)],
        flops=2 * clips * cells * channels * wide,
    )(turned, shifted)
    came = swap(sent, "core")
    kept, sent = call(
        half_kernel,
        (jax.ShapeDtypeStruct((quarter, wide), f32), jax.ShapeDtypeStruct((quarter, wide), bf16)),
        scratch=[pltpu.VMEM((2, quarter, wide), f32)],
    )(kept, came)
    came = swap(sent, "yhi")
    sent = call(add_kernel, jax.ShapeDtypeStruct((quarter, wide), bf16))(kept, came)
    heights = lax.axis_size(Z)
    parts = lax.all_to_all(sent.reshape(heights, quarter // heights, wide), Z, 0, 0)
    group_total = heights * 4
    grad_weight = call(
        functools.partial(final_kernel, group_total),
        jax.ShapeDtypeStruct((taps, quarter // heights, width), f32),
    )(parts)
    grad_features = feature_sum.reshape(features.shape)
    return (grad_features, grad_weight, grad_text.reshape(1, 1, channels))


def solution(mesh):
    fine = Mesh(mesh.devices.reshape(2, 4, 2, 16, 2), ("ylo", "x", "yhi", "z", "core"))
    dp = ("yhi", "z", "core")
    placed = (
        P(BLK, dp, None, None, None),
        P(None, None, BLK),
        P(BLK, None),
        P(BLK, dp, None),
        P(BLK, dp),
    )
    return jax.shard_map(
        shards,
        mesh=fine,
        in_specs=placed,
        out_specs=(P(BLK, dp, None, None, None), P(None, dp, BLK), P(BLK, dp, None)),
        check_vma=False,
    )
```

time: 489 us -> 111 us (0.23)
  the two profiles are of different devices: /device:TPU:6 before, /device:TPU:16 now
where the time goes in v1:
time: 111 us; the launch traced here: 110 us
  blocking collectives  44.8 us (40%)
  waiting for transfers between devices  25.7 us (23%)
  between operations  14.7 us (13%)
  starting transfers between devices  9.74 us (9%)
  Pallas kernels  8.14 us (7%)
  local copies, waits for them, and re-layouts  6.09 us (5%)
    all_to_all x1, blocking collectives, shards(): lax.all_to_all(sent.reshape(heights, quarter // heights, wide), Z, 0, 0)  35.7 us
    all_to_all x1, waiting for transfers between devices, shards(): lax.all_to_all(jnp.broadcast_to(own[None], (clips, rows, channels)), BLK,...  13.9 us
    ppermute x2, waiting for transfers between devices, swap(): return lax.ppermute(values, axis, [(0, 1), (1, 0)])  11.8 us
    all_to_all x1, blocking collectives, shards(): parts = lax.all_to_all(partial, BLK, 0, 0)  9.1 us
    all_to_all x1, starting transfers between devices, shards(): lax.all_to_all(jnp.broadcast_to(own[None], (clips, rows, channels)), BLK,...  5.15 us
    ppermute x2, starting transfers between devices, swap(): return lax.ppermute(values, axis, [(0, 1), (1, 0)])  4.56 us
    pallas_call x1, Pallas kernels, shards(): call(input_kernel, (jax.ShapeDtypeStruct((clips, cells, channels), bf16),...  3.33 us
    unnamed x7, local copies, waits for them, and re-layouts  3.11 us
  transfers between devices with their start and end apart: 4, of which 3 were waited for; matrix products, arithmetic and copies ran while one was open for 3% of the time, Pallas kernels for 3%

profile of v1, /device:TPU:16, one launch (start us, length us, event | category | flops | bytes accessed | tf_op | source)
XLA Modules:
  0.0 110.2 jit_solution(12014602355295302845)
XLA Ops:
  7.8 0.1 pad.2.clone
  7.9 0.1 pad.3.clone
  8.0 1.0 maximum_maximum_fusion
  9.0 1.1 %broadcast_in_dim.19 = bf16[8,144,512]{2,1,0:T(8,128)(2,1)} broadcast(bf16[144,512]{1,0:T(8,128)(2,1)S(1)} %maximum_maximum_fusion), dimensions={1,2} | broadcast | bytes 1327104 | tf_op jit(solution)/shard_map/broadcast_in_dim | solution.py:199
  10.1 5.2 %all-to-all-start = ((bf16[8,144,512]{2,1,0:T(8,128)(2,1)}), bf16[8,144,512]{2,1,0:T(8,128)(2,1)S(1)}, u32[]{:S(2)}, u32[]{:S(2)}) async-start(bf16[8,144,512]{2,1,0:T(8,128)(2,1)} %broadcast_in_dim.19), calls=%async_computation | async-start | bytes 2359296 | tf_op jit(solution)/shard_map/all_to_all | solution.py:199
  15.3 0.0 reduce-scatter.2.cloned.1.call-start
  15.3 0.0 copy-done.2
  15.3 1.4 %copy.9 = bf16[9,512,128]{1,2,0:T(8,128)(2,1)} copy(bf16[9,512,128]{2,1,0:T(8,128)(2,1)S(1)} %copy-done.2) | data formatting | bytes 2359296 | tf_op args[1]
  16.8 1.7 %copy.10.weight_ref = bf16[512,1152]{1,0:T(8,128)(2,1)S(1)} copy(bf16[512,1152]{0,1:T(8,128)(2,1)} %bitcast.12) | data formatting | bytes 2359296 | tf_op jit(solution)/shard_map/reshape | solution.py:198
  18.5 13.9 %all-to-all-done.group_ref = bf16[8,144,512]{2,1,0:T(8,128)(2,1)S(1)} async-done(((bf16[8,144,512]{2,1,0:T(8,128)(2,1)}), bf16[8,144,512]{2,1,0:T(8,128)(2,1)S(1)}, u32[]{:S(2)}, u32[]{:S(2)}) %all-to-all-start) | async-done | bytes 1179680 | tf_op jit(solution)/shard_map/all_to_all | solution.py:199
  32.4 2.0 %shard_map.76 = (f32[1024,128]{1,0:T(8,128)S(1)}, bf16[512,1024]{1,0:T(8,128)(2,1)S(1)}, f32[8,8,512]{2,1,0:T(8,128)S(1)}) custom-call(bf16[8,144,512]{2,1,0:T(8,128)(2,1)S(1)} %all-to-all-done.group_ref, bf16[512,1152]{1,0:T(8,128)(2,1)S(1)} %copy.10.weight_ref, bf16[128,512]{1,0:T(8,128)(2,1)S(1)} %copy-done), custom_call_target="tpu_custom_call" | custom-call | flops 1207959552 | tf_op jit(solution)/shard_map/pallas_call | solution.py:200
  34.4 9.1 %all_to_all.15.parts_ref = f32[8,8,512]{2,1,0:T(8,128)S(1)} all-to-all(f32[8,8,512]{2,1,0:T(8,128)S(1)} %get-tuple-element.13), channel_id=1, replica_groups=mesh['ylo'=2,'x'=4,'yhi'=2,'z'=16,'core'=2] {'ylo','x'}, dimensions={0} | all-to-all | bytes 262144 | tf_op jit(solution)/shard_map/all_to_all | solution.py:209
  43.5 3.3 %shard_map.77 = (bf16[8,128,512]{2,1,0:T(8,128)(2,1)}, f32[1,512]{1,0:T(1,128)}, bf16[8,4,32,1152]{3,2,1,0:T(8,128)(2,1)}) custom-call(f32[8,8,512]{2,1,0:T(8,128)S(1)} %all_to_all.15.parts_ref, bf16[8,144,512]{2,1,0:T(8,128)(2,1)S(1)} %all-to-all-done.group_ref, f32[1024,128]{1,0:T(8,128)S(1)} %get-tuple-element.14.slope_ref, ...), custom_call_target="tpu_custom_call" | custom-call | flops 1207959552 | tf_op jit(solution)/shard_map/pallas_call | solution.py:210
  46.8 0.0 reduce-scatter.2.cloned.1.call-update
  46.8 1.7 %copy-done.1 = bf16[8,4,32,1152]{3,2,1,0:T(8,128)(2,1)S(1)} copy-done((bf16[8,4,32,1152]{3,2,1,0:T(8,128)(2,1)S(1)}, bf16[8,4,32,1152]{3,2,1,0:T(8,128)(2,1)}, u32[]{:S(2)}) %copy-start.1) | copy-done | bytes 2359320
  48.5 1.9 %shard_map.78 = (f32[256,1152]{1,0:T(8,128)S(1)}, bf16[256,1152]{1,0:T(8,128)(2,1)S(1)}) custom-call(bf16[512,1024]{1,0:T(8,128)(2,1)S(1)} %get-tuple-element.16.turned_ref, bf16[8,4,32,1152]{3,2,1,0:T(8,128)(2,1)S(1)} %copy-done.1), custom_call_target="tpu_custom_call" | custom-call | flops 1207959552 | tf_op jit(solution)/shard_map/pallas_call | solution.py:222
  50.4 1.9 %collective-permute-start = (bf16[256,1152]{1,0:T(8,128)(2,1)S(1)}, bf16[256,1152]{1,0:T(8,128)(2,1)S(1)}, u32[]{:S(2)}, u32[]{:S(2)}) collective-permute-start(bf16[256,1152]{1,0:T(8,128)(2,1)S(1)} %get-tuple-element.19), channel_id=1, source_target_pairs={{0,1},{1,0},{2,3},{3,2},{4,5},{5,4},{6,7},{7,6},{8,9},{9,8},{10,11... | collective-permute-start | bytes 1769480 | tf_op jit(solution)/shard_map/ppermute | solution.py:184
  52.3 2.0 %collective-permute-done.came_ref = bf16[256,1152]{1,0:T(8,128)(2,1)S(1)} collective-permute-done((bf16[256,1152]{1,0:T(8,128)(2,1)S(1)}, bf16[256,1152]{1,0:T(8,128)(2,1)S(1)}, u32[]{:S(2)}, u32[]{:S(2)}) %collective-permute-start) | collective-permute-done | bytes 589856 | tf_op jit(solution)/shard_map/ppermute | solution.py:184
  54.3 0.2 shard_map.79
  54.5 2.6 %collective-permute-start.1 = (bf16[128,1152]{1,0:T(8,128)(2,1)S(1)}, bf16[128,1152]{1,0:T(8,128)(2,1)S(1)}, u32[]{:S(2)}, u32[]{:S(2)}) collective-permute-start(bf16[128,1152]{1,0:T(8,128)(2,1)S(1)} %get-tuple-element.21), channel_id=1, source_target_pairs={{0,32},{32,0},{1,33},{33,1},{2,34},{34,2},{3,35},{35,3},{4,36},{36... | collective-permute-start | bytes 884744 | tf_op jit(solution)/shard_map/ppermute | solution.py:184
  57.2 9.8 %collective-permute-done.1.came_ref = bf16[128,1152]{1,0:T(8,128)(2,1)S(1)} collective-permute-done((bf16[128,1152]{1,0:T(8,128)(2,1)S(1)}, bf16[128,1152]{1,0:T(8,128)(2,1)S(1)}, u32[]{:S(2)}, u32[]{:S(2)}) %collective-permute-start.1) | collective-permute-done | bytes 294944 | tf_op jit(solution)/shard_map/ppermute | solution.py:184
  67.0 0.1 shard_map.80
  67.0 35.7 %all_to_all.16.parts_ref = bf16[16,8,1152]{2,1,0:T(8,128)(2,1)S(1)} all-to-all(bf16[16,8,1152]{2,1,0:T(8,128)(2,1)S(1)} %bitcast.11), channel_id=1, replica_groups=mesh['ylo'=2,'x'=4,'yhi'=2,'z'=16,'core'=2] {'z'}, dimensions={0} | all-to-all | bytes 589824 | tf_op jit(solution)/shard_map/all_to_all | solution.py:237
  102.7 0.7 shard_map.81
  (6 shorter events, 0.0 us)
Async XLA Ops:
  10.1 5.2 %copy-start.2 = (bf16[9,512,128]{2,1,0:T(8,128)(2,1)S(1)}, bf16[9,512,128]{2,1,0:T(8,128)(2,1)}, u32[]{:S(2)}) copy-start(bf16[9,512,128]{2,1,0:T(8,128)(2,1)} %param.6) | copy-start | bytes 3538948
  10.1 22.3 %all-to-all-start = ((bf16[8,144,512]{2,1,0:T(8,128)(2,1)}), bf16[8,144,512]{2,1,0:T(8,128)(2,1)S(1)}, u32[]{:S(2)}, u32[]{:S(2)}) async-start(bf16[8,144,512]{2,1,0:T(8,128)(2,1)} %broadcast_in_dim.19), calls=%async_computation | async-start | bytes 2359296 | tf_op jit(solution)/shard_map/all_to_all | solution.py:199
  15.3 88.1 %reduce-scatter.2.cloned.1.call-start = ((), (), s32[]{:S(2)}) async-start(), calls=%async_computation.4 | async-start | bytes 1179648 | tf_op jit(solution)/shard_map/reduce_scatter | solution.py:219
  16.8 15.6 %copy-start = (bf16[128,512]{1,0:T(8,128)(2,1)S(1)}, bf16[128,512]{1,0:T(8,128)(2,1)}, u32[]{:S(2)}) copy-start(bf16[128,512]{1,0:T(8,128)(2,1)} %projection_ref.3) | copy-start | bytes 393220
  46.8 1.7 %copy-start.1 = (bf16[8,4,32,1152]{3,2,1,0:T(8,128)(2,1)S(1)}, bf16[8,4,32,1152]{3,2,1,0:T(8,128)(2,1)}, u32[]{:S(2)}) copy-start(bf16[8,4,32,1152]{3,2,1,0:T(8,128)(2,1)} %get-tuple-element.17.shifted_ref) | copy-start | bytes 7077892
  50.4 3.9 %collective-permute-start = (bf16[256,1152]{1,0:T(8,128)(2,1)S(1)}, bf16[256,1152]{1,0:T(8,128)(2,1)S(1)}, u32[]{:S(2)}, u32[]{:S(2)}) collective-permute-start(bf16[256,1152]{1,0:T(8,128)(2,1)S(1)} %get-tuple-element.19), channel_id=1, source_target_pairs={{0,1},{1,0},{2,3},{3,2},{4,5},{5,4},{6,7},{7,6},{8,9},{9,8},{10,11... | collective-permute-start | bytes 1769480 | tf_op jit(solution)/shard_map/ppermute | solution.py:184
  54.5 12.4 %collective-permute-start.1 = (bf16[128,1152]{1,0:T(8,128)(2,1)S(1)}, bf16[128,1152]{1,0:T(8,128)(2,1)S(1)}, u32[]{:S(2)}, u32[]{:S(2)}) collective-permute-start(bf16[128,1152]{1,0:T(8,128)(2,1)S(1)} %get-tuple-element.21), channel_id=1, source_target_pairs={{0,32},{32,0},{1,33},{33,1},{2,34},{34,2},{3,35},{35,3},{4,36},{36... | collective-permute-start | bytes 884744 | tf_op jit(solution)/shard_map/ppermute | solution.py:184
Sparse Core Ops, SparseCore 0:
  47.0 48.9 reduce-scatter.1

commit v2 on v1

v2 whole, which is shorter than its diff:
```python
import functools

import jax
import jax.numpy as jnp
from jax import lax
from jax.experimental import pallas as pl
from jax.experimental.pallas import tpu as pltpu
from jax.sharding import Mesh, PartitionSpec as P

logit_scale = 10.0
logit_bias = -2.0
loss_scale = 1024.0
norm_eps = 1e-06

BLK = ("ylo", "x")
Z = "z"
f32 = jnp.float32
bf16 = jnp.bfloat16

clips = 8
freq = 4
frames = 32
cells = freq * frames
columns = 4
vmem_limit = 40 * 1024 * 1024
HBM = pl.BlockSpec(memory_space=pltpu.HBM)
VMEM = pl.BlockSpec(memory_space=pltpu.VMEM)
DMA = pltpu.SemaphoreType.DMA


def shape(dims, dtype):
    return jax.ShapeDtypeStruct(dims, dtype)


def call(kernel, out_shape, scratch=(), flops=0, **specs):
    return pl.pallas_call(
        kernel,
        out_shape=out_shape,
        scratch_shapes=scratch,
        compiler_params=pltpu.CompilerParams(vmem_limit_bytes=vmem_limit),
        cost_estimate=pl.CostEstimate(flops=flops, bytes_accessed=0, transcendentals=0),
        **specs,
    )


def copy_kernel(own_ref, out_ref, sems):
    copies = [
        pltpu.make_async_copy(own_ref.at[0], out_ref.at[c], sems.at[c]) for c in range(clips)
    ]
    for copy in copies:
        copy.start()
    for copy in copies:
        copy.wait()


def frame_index(count):
    return lax.broadcasted_iota(jnp.int32, (count, 1), 0) % frames


def shift_rows(values, step):
    count = values.shape[0]
    frame = frame_index(count)
    if step == 1:
        return jnp.where(frame == 0, 0.0, pltpu.roll(values, 1, 0))
    return jnp.where(frame == frames - 1, 0.0, pltpu.roll(values, count - 1, 0))


def forward_kernel(
    group_ref,
    weight_ref,
    projection_ref,
    caption_ref,
    label_ref,
    slope_ref,
    partial_ref,
    slope_buf,
    slope_sem,
):
    inputs = group_ref[...].reshape(clips * cells, -1)
    out_width = projection_ref.shape[0]
    preact = None
    for a in range(3):
        product = jnp.dot(
            inputs,
            weight_ref[:, 3 * a * out_width : 3 * (a + 1) * out_width],
            preferred_element_type=f32,
        ).reshape(clips, freq, frames, 3 * out_width)
        low = product[..., :out_width]
        mid = product[..., out_width : 2 * out_width]
        high = product[..., 2 * out_width :]
        bins = []
        for f in range(freq):
            total = mid[:, f]
            if f > 0:
                total = total + low[:, f - 1]
            if f < freq - 1:
                total = total + high[:, f + 1]
            bins.append(total[:, None])
        column = jnp.concatenate(bins, axis=1).reshape(clips * cells, out_width)
        if a == 0:
            column = shift_rows(column, 1)
        if a == 2:
            column = shift_rows(column, -1)
        preact = column if preact is None else preact + column
    sigma = jax.nn.sigmoid(preact)
    slope_buf[...] = sigma * (1.0 + preact * (1.0 - sigma))
    slope_copy = pltpu.make_async_copy(slope_buf, slope_ref, slope_sem)
    slope_copy.start()
    active = (preact * sigma).reshape(clips, cells, out_width)
    pooled = (jnp.sum(active, axis=1) * (1.0 / cells)).astype(bf16)
    partial = jnp.dot(pooled, projection_ref[...], preferred_element_type=f32)
    embed = partial.shape[1]
    partial_ref[:, :, :embed] = jnp.broadcast_to(partial[None], (clips, clips, embed))
    own_caption = caption_ref[...].astype(f32)
    lanes = partial_ref.shape[2] - embed
    for piece in range(embed // lanes):
        part = own_caption[:, piece * lanes : (piece + 1) * lanes]
        partial_ref[:, piece : piece + 1, embed:] = jnp.broadcast_to(
            part[None], (clips, 1, lanes)
        )
    label = jnp.full((clips, clips // 2, lanes), label_ref[0, 0], jnp.int32)
    partial_ref[:, clips // 2 :, embed:] = label.astype(f32)
    slope_copy.wait()


def turn_kernel(group_ref, turned_ref):
    channels = group_ref.shape[-1]
    inputs = group_ref[...].reshape(clips * cells, channels)
    target = lax.broadcasted_iota(jnp.int32, (channels, channels), 0)
    source = lax.broadcasted_iota(jnp.int32, (channels, channels), 1)
    half = channels // 2
    core = target // half
    within = target - core * half
    wanted = ((within // 8) * 2 + core) * 8 + within % 8
    order = jnp.where(source == wanted, 1.0, 0.0).astype(bf16)
    turned = lax.dot_general(
        order, inputs, (((1,), (1,)), ((), ())), preferred_element_type=f32
    )
    turned_ref[...] = turned.astype(bf16).reshape(turned_ref.shape)


def row_sum(values):
    return jnp.sum(values, axis=-1, keepdims=True)


def pair_column(audio_unit, caption_row, clip_labels, column):
    logits = logit_scale * row_sum(audio_unit * caption_row) + logit_bias
    signs = jnp.where(clip_labels == column, 1.0, -1.0)
    return -loss_scale * signs * jax.nn.sigmoid(-signs * logits)


def pair_kernel(
    parts_ref,
    slope_ref,
    projection_ref,
    turned_ref,
    text_ref,
    shifted_ref,
    sent_ref,
    slope_buf,
    projection_buf,
    turned_buf,
    sems,
):
    core = lax.axis_index("core")
    copies = [
        pltpu.make_async_copy(projection_ref, projection_buf, sems.at[0]),
        pltpu.make_async_copy(slope_ref, slope_buf, sems.at[1]),
        pltpu.make_async_copy(turned_ref.at[1 - core], turned_buf, sems.at[2]),
    ]
    for copy in copies:
        copy.start()
    embed = projection_ref.shape[1]
    lanes = parts_ref.shape[2] - embed
    embedding = jnp.sum(parts_ref[:, :, :embed], axis=0)
    inv_audio = lax.rsqrt(row_sum(embedding * embedding) + norm_eps)
    audio_unit = embedding * inv_audio
    clip_labels = jnp.concatenate(
        [parts_ref[c, clips - 1 :, embed : embed + 1] for c in range(clips)], axis=0
    ).astype(jnp.int32)
    position = lax.axis_index("ylo") * columns + lax.axis_index("x")

    def caption_at(index):
        text_values = jnp.concatenate(
            [parts_ref[index, p : p + 1, embed:] for p in range(embed // lanes)], axis=1
        )
        inv_text = lax.rsqrt(row_sum(text_values * text_values) + norm_eps)
        return text_values * inv_text, inv_text

    audio_grad = jnp.zeros_like(audio_unit)
    for j in range(clips):
        caption, _ = caption_at(j)
        audio_grad = audio_grad + pair_column(audio_unit, caption, clip_labels, j) * caption
    audio_grad = logit_scale * audio_grad
    caption, inv_text = caption_at(position)
    own_pairs = pair_column(audio_unit, caption, clip_labels, position)
    caption_grad = logit_scale * jnp.sum(own_pairs * audio_unit, axis=0, keepdims=True)
    text_ref[...] = (caption_grad - caption * row_sum(caption * caption_grad)) * inv_text
    embedding_grad = (
        (audio_grad - audio_unit * row_sum(audio_unit * audio_grad)) * inv_audio
    ).astype(bf16)
    copies[0].wait()
    pooled_grad = lax.dot_general(
        embedding_grad, projection_buf[...], (((1,), (1,)), ((), ())), preferred_element_type=f32
    )
    width = pooled_grad.shape[1]
    scaled = pooled_grad * (1.0 / cells)
    copies[1].wait()
    pre_grad = (scaled[:, None, :] * slope_buf[...].reshape(clips, cells, width)).astype(bf16)
    pre_grad = pre_grad.astype(f32).reshape(clips * cells, width)
    zeros = jnp.zeros((clips, frames, width), bf16)
    for a in range(3):
        moved = pre_grad
        if a == 0:
            moved = shift_rows(pre_grad, -1)
        if a == 2:
            moved = shift_rows(pre_grad, 1)
        moved = moved.astype(bf16).reshape(clips, freq, frames, width)
        for b in range(3):
            tap = 3 * a + b
            for f in range(freq):
                source = f - (b - 1)
                block = moved[:, source] if 0 <= source < freq else zeros
                shifted_ref[:, f, :, tap * width : (tap + 1) * width] = block
    shifted = shifted_ref[...].reshape(clips * cells, -1)
    copies[2].wait()
    sent_ref[...] = jnp.dot(turned_buf[...], shifted, preferred_element_type=f32).astype(bf16)


def keep_kernel(turned_ref, shifted_ref, kept_ref, turned_buf, sem):
    core = lax.axis_index("core")
    copy = pltpu.make_async_copy(turned_ref.at[core], turned_buf, sem)
    copy.start()
    copy.wait()
    shifted = shifted_ref[...].reshape(clips * cells, -1)
    kept_ref[...] = jnp.dot(turned_buf[...], shifted, preferred_element_type=f32)


def half_kernel(kept_ref, came_ref, mine_ref, sent_ref, total_ref):
    total_ref[...] = (kept_ref[...] + came_ref[...].astype(f32)).reshape(total_ref.shape)
    side = lax.axis_index("yhi")
    mine_ref[...] = total_ref[side]
    sent_ref[...] = total_ref[1 - side].astype(bf16)


def input_kernel(shifted_ref, weight_ref, after_ref, *rest):
    out_refs, total_ref = rest[:columns], rest[columns]
    shifted = shifted_ref[...].reshape(clips * cells, -1)
    result = lax.dot_general(
        shifted, weight_ref[...], (((1,), (1,)), ((), ())), preferred_element_type=f32
    )
    total_ref[...] = result.astype(bf16).reshape(total_ref.shape)
    here = lax.axis_index("x")
    for d in range(columns):
        out_refs[d][...] = total_ref[:, here ^ d]


def add_kernel(kept_ref, came_ref, after_ref, sent_ref, sent_buf, sem):
    sent_buf[...] = (kept_ref[...] + came_ref[...].astype(f32)).astype(bf16)
    copy = pltpu.make_async_copy(sent_buf, sent_ref, sem)
    copy.start()
    copy.wait()


def column_kernel(own_ref, a_ref, b_ref, c_ref, mine_ref, sent_ref, total_ref):
    total = own_ref[...].astype(f32)
    for ref in (a_ref, b_ref, c_ref):
        total = total + ref[...].astype(f32)
    total_ref[...] = total
    side = lax.axis_index("ylo")
    mine_ref[...] = total_ref[side]
    sent_ref[...] = total_ref[1 - side].astype(bf16)


def join_kernel(mine_ref, came_ref, out_ref):
    out_ref[...] = (mine_ref[...] + came_ref[...].astype(f32)).astype(bf16)


def final_kernel(group_total, parts_ref, out_ref):
    total = jnp.sum(parts_ref[...].astype(f32), axis=0) * (1.0 / group_total)
    taps, _, width = out_ref.shape
    for tap in range(taps):
        out_ref[tap] = total[:, tap * width : (tap + 1) * width]


def swap(values, axis):
    return lax.ppermute(values, axis, [(0, 1), (1, 0)])


def shards(features, conv_weight, projection, text, labels):
    taps, channels, width = conv_weight.shape
    wide = taps * width
    embed = projection.shape[1]
    half = channels // 2
    quarter = half // 2
    matmul = 2 * clips * cells * channels * wide
    weight = jnp.transpose(conv_weight, (1, 0, 2)).reshape(channels, wide)
    copies = call(
        copy_kernel,
        shape((clips, cells, channels), bf16),
        scratch=[DMA((clips,))],
        in_specs=[HBM],
        out_specs=HBM,
    )(features.reshape(1, cells, channels))
    group = lax.all_to_all(copies, BLK, 0, 0)
    slope, partial = call(
        forward_kernel,
        (shape((clips * cells, width), f32), shape((clips, clips, embed + 128), f32)),
        scratch=[pltpu.VMEM((clips * cells, width), f32), DMA],
        out_specs=(HBM, VMEM),
        flops=matmul,
    )(group, weight, projection, text.reshape(1, embed), labels)
    parts = lax.all_to_all(partial, BLK, 0, 0)
    turned = call(turn_kernel, shape((2, half, clips * cells), bf16), flops=matmul // 4)(group)
    grad_text, shifted, sent = call(
        pair_kernel,
        (
            shape((1, embed), f32),
            shape((clips, freq, frames, wide), bf16),
            shape((half, wide), bf16),
        ),
        scratch=[
            pltpu.VMEM((clips * cells, width), f32),
            pltpu.VMEM(projection.shape, bf16),
            pltpu.VMEM((half, clips * cells), bf16),
            DMA((3,)),
        ],
        in_specs=[VMEM, HBM, HBM, HBM],
        flops=matmul // 2,
    )(parts, slope, projection, turned)
    kept = call(
        keep_kernel,
        shape((half, wide), f32),
        scratch=[pltpu.VMEM((half, clips * cells), bf16), DMA],
        in_specs=[HBM, VMEM],
        flops=matmul // 2,
    )(turned, shifted)
    came = swap(sent, "core")
    kept, sent = call(
        half_kernel,
        (shape((quarter, wide), f32), shape((quarter, wide), bf16)),
        scratch=[pltpu.VMEM((2, quarter, wide), f32)],
    )(kept, came)
    columns_out = call(
        input_kernel,
        tuple(shape((2, cells, channels), bf16) for _ in range(columns)),
        scratch=[pltpu.VMEM((2, columns, cells, channels), bf16)],
        in_specs=[VMEM, VMEM, pl.BlockSpec(memory_space=pl.ANY)],
        flops=matmul,
    )(shifted, weight, kept)
    came = swap(sent, "yhi")
    sent = call(
        add_kernel,
        shape((quarter, wide), bf16),
        scratch=[pltpu.VMEM((quarter, wide), bf16), DMA],
        in_specs=[VMEM, VMEM, pl.BlockSpec(memory_space=pl.ANY)],
        out_specs=HBM,
    )(kept, came, columns_out[0])
    heights = lax.axis_size(Z)
    parts = lax.all_to_all(sent.reshape(heights, quarter // heights, wide), Z, 0, 0)
    others = [
        lax.ppermute(columns_out[d], "x", [(i, i ^ d) for i in range(columns)])
        for d in range(1, columns)
    ]
    mine, other = call(
        column_kernel,
        (shape((cells, channels), f32), shape((cells, channels), bf16)),
        scratch=[pltpu.VMEM((2, cells, channels), f32)],
        flops=int(1e10),
    )(columns_out[0], *others)
    grad_features = call(join_kernel, shape((cells, channels), bf16))(mine, swap(other, "ylo"))
    grad_weight = call(
        functools.partial(final_kernel, heights * 4),
        shape((taps, quarter // heights, width), f32),
    )(parts)
    return (
        grad_features.reshape(features.shape),
        grad_weight,
        grad_text.reshape(1, 1, embed),
    )


def solution(mesh):
    fine = Mesh(mesh.devices.reshape(2, columns, 2, 16, 2), ("ylo", "x", "yhi", "z", "core"))
    dp = ("yhi", "z", "core")
    placed = (
        P(BLK, dp, None, None, None),
        P(None, None, BLK),
        P(BLK, None),
        P(BLK, dp, None),
        P(BLK, dp),
    )
    return jax.shard_map(
        shards,
        mesh=fine,
        in_specs=placed,
        out_specs=(P(BLK, dp, None, None, None), P(None, dp, BLK), P(BLK, dp, None)),
        check_vma=False,
    )
```

time: 111 us -> 98.8 us (0.89)
  the two profiles are of different devices: /device:TPU:16 before, /device:TPU:6 now
where the time goes in v2:
time: 98.8 us; the launch traced here: 96.9 us
  starting transfers between devices  49.5 us (50%)
  waiting for transfers between devices  27.1 us (27%)
  Pallas kernels  12 us (12%)
  local copies, waits for them, and re-layouts  6.79 us (7%)
  between operations  1.48 us (1%)
    all_to_all x1, starting transfers between devices, shards(): lax.all_to_all(sent.reshape(heights, quarter // heights, wide), Z, 0, 0)  15.2 us
    all_to_all x1, waiting for transfers between devices, shards(): lax.all_to_all(sent.reshape(heights, quarter // heights, wide), Z, 0, 0)  11.3 us
    ppermute x3, starting transfers between devices, shards(): lax.ppermute(columns_out[d], 'x', [(i, i ^ d) for i in range(columns)])  10.4 us
    all_to_all x1, starting transfers between devices, shards(): group = lax.all_to_all(copies, BLK, 0, 0)  9.47 us
    ppermute x3, starting transfers between devices, swap(): return lax.ppermute(values, axis, [(0, 1), (1, 0)])  8.82 us
    all_to_all x1, waiting for transfers between devices, shards(): group = lax.all_to_all(copies, BLK, 0, 0)  6.07 us
    ppermute x3, waiting for transfers between devices, swap(): return lax.ppermute(values, axis, [(0, 1), (1, 0)])  5.83 us
    all_to_all x1, starting transfers between devices, shards(): parts = lax.all_to_all(partial, BLK, 0, 0)  5.58 us
  transfers between devices with their start and end apart: 9, of which 5 were waited for; matrix products, arithmetic and copies ran while one was open for 3% of the time, Pallas kernels for 5%

profile of v2, /device:TPU:6, one launch (start us, length us, event | category | flops | bytes accessed | tf_op | source)
XLA Modules:
  0.0 96.9 jit_solution(16843862670133987692)
XLA Ops:
  0.6 0.9 copy-done
  1.5 1.0 %shard_map.76 = bf16[8,128,512]{2,1,0:T(8,128)(2,1)} custom-call(bf16[1,128,512]{2,1,0:T(8,128)(2,1)S(1)} %bitcast.8), custom_call_target="tpu_custom_call" | custom-call | tf_op jit(solution)/shard_map/pallas_call | solution.py:298
  2.6 9.5 %all-to-all-start = ((bf16[8,128,512]{2,1,0:T(8,128)(2,1)}), bf16[8,128,512]{2,1,0:T(8,128)(2,1)S(1)}, u32[]{:S(2)}, u32[]{:S(2)}) async-start(bf16[8,128,512]{2,1,0:T(8,128)(2,1)} %shard_map.76), calls=%async_computation | async-start | bytes 2097152 | tf_op jit(solution)/shard_map/all_to_all | solution.py:305
  12.7 1.4 %copy.9 = bf16[9,512,128]{1,2,0:T(8,128)(2,1)} copy(bf16[9,512,128]{2,1,0:T(8,128)(2,1)S(1)} %copy-done.6) | data formatting | bytes 2359296 | tf_op args[1]
  14.2 1.7 %copy.10.weight_ref = bf16[512,1152]{1,0:T(8,128)(2,1)S(1)} copy(bf16[512,1152]{0,1:T(8,128)(2,1)} %bitcast.10) | data formatting | bytes 2359296 | tf_op jit(solution)/shard_map/reshape | solution.py:297
  15.9 6.1 %all-to-all-done.group_ref = bf16[8,128,512]{2,1,0:T(8,128)(2,1)S(1)} async-done(((bf16[8,128,512]{2,1,0:T(8,128)(2,1)}), bf16[8,128,512]{2,1,0:T(8,128)(2,1)S(1)}, u32[]{:S(2)}, u32[]{:S(2)}) %all-to-all-start) | async-done | bytes 1048608 | tf_op jit(solution)/shard_map/all_to_all | solution.py:305
  21.9 2.7 %shard_map.77 = (f32[1024,128]{1,0:T(8,128)S(1)}, f32[8,8,640]{2,1,0:T(8,128)}) custom-call(bf16[8,128,512]{2,1,0:T(8,128)(2,1)S(1)} %all-to-all-done.group_ref, bf16[512,1152]{1,0:T(8,128)(2,1)S(1)} %copy.10.weight_ref, bf16[128,512]{1,0:T(8,128)(2,1)S(1)} %copy-done.1, bf16[1,512]{1,0:T(2,128)(2,1)S(1)} %bitcast.9, s32[1,1]{1,0:T(1,128)S(6)} %copy.12.label_ref), custom_call_target="tpu_custom_call" | custom-call | flops 1207959552 | tf_op jit(solution)/shard_map/pallas_call | solution.py:306
  25.5 5.6 %all-to-all-start.1 = ((f32[8,8,640]{2,1,0:T(8,128)}), f32[8,8,640]{2,1,0:T(8,128)S(1)}, u32[]{:S(2)}, u32[]{:S(2)}) async-start(f32[8,8,640]{2,1,0:T(8,128)} %get-tuple-element.16), calls=%async_computation.1 | async-start | bytes 327680 | tf_op jit(solution)/shard_map/all_to_all | solution.py:313
  31.9 3.9 %all-to-all-done.1.parts_ref = f32[8,8,640]{2,1,0:T(8,128)S(1)} async-done(((f32[8,8,640]{2,1,0:T(8,128)}), f32[8,8,640]{2,1,0:T(8,128)S(1)}, u32[]{:S(2)}, u32[]{:S(2)}) %all-to-all-start.1) | async-done | bytes 163872 | tf_op jit(solution)/shard_map/all_to_all | solution.py:313
  35.9 0.9 copy-done.2
  36.8 1.0 %copy-done.5 = f32[1024,128]{1,0:T(8,128)S(1)} copy-done((f32[1024,128]{1,0:T(8,128)S(1)}, f32[1024,128]{1,0:T(8,128)}, u32[]{:S(2)}) %copy-start.5) | copy-done | bytes 524312
  37.8 2.3 %shard_map.79 = (f32[1,512]{1,0:T(1,128)}, bf16[8,4,32,1152]{3,2,1,0:T(8,128)(2,1)S(1)}, bf16[256,1152]{1,0:T(8,128)(2,1)S(1)}) custom-call(f32[8,8,640]{2,1,0:T(8,128)S(1)} %all-to-all-done.1.parts_ref, f32[1024,128]{1,0:T(8,128)S(1)} %copy-done.5, bf16[128,512]{1,0:T(8,128)(2,1)S(1)} %copy-done.2, bf16[2,256,1024]{2,1,0:T(8,128)(2,1)S(1)} %shard_map.78.turned_ref), custom_call_target="tpu_custom_call" | custom-call | flops 603979776 | tf_op jit(solution)/shard_map/pallas_call | solution.py:315
  40.1 1.9 %collective-permute-start = (bf16[256,1152]{1,0:T(8,128)(2,1)S(1)}, bf16[256,1152]{1,0:T(8,128)(2,1)S(1)}, u32[]{:S(2)}, u32[]{:S(2)}) collective-permute-start(bf16[256,1152]{1,0:T(8,128)(2,1)S(1)} %get-tuple-element.19), channel_id=1, source_target_pairs={{0,1},{1,0},{2,3},{3,2},{4,5},{5,4},{6,7},{7,6},{8,9},{9,8},{10,11... | collective-permute-start | bytes 1769480 | tf_op jit(solution)/shard_map/ppermute | solution.py:287
  42.0 0.9 shard_map.80.kept_ref
  42.9 1.1 %collective-permute-done.came_ref = bf16[256,1152]{1,0:T(8,128)(2,1)S(1)} collective-permute-done((bf16[256,1152]{1,0:T(8,128)(2,1)S(1)}, bf16[256,1152]{1,0:T(8,128)(2,1)S(1)}, u32[]{:S(2)}, u32[]{:S(2)}) %collective-permute-start) | collective-permute-done | bytes 589856 | tf_op jit(solution)/shard_map/ppermute | solution.py:287
  44.2 4.8 %collective-permute-start.5 = (bf16[128,1152]{1,0:T(8,128)(2,1)S(1)}, bf16[128,1152]{1,0:T(8,128)(2,1)S(1)}, u32[]{:S(2)}, u32[]{:S(2)}) collective-permute-start(bf16[128,1152]{1,0:T(8,128)(2,1)S(1)} %get-tuple-element.27), channel_id=1, source_target_pairs={{0,32},{32,0},{1,33},{33,1},{2,34},{34,2},{3,35},{35,3},{4,36},{36... | collective-permute-start | bytes 884744 | tf_op jit(solution)/shard_map/ppermute | solution.py:287
  49.0 1.6 %shard_map.82 = (bf16[2,128,512]{2,1,0:T(8,128)(2,1)S(1)}, bf16[2,128,512]{2,1,0:T(8,128)(2,1)S(1)}, bf16[2,128,512]{2,1,0:T(8,128)(2,1)S(1)}, bf16[2,128,512]{2,1,0:T(8,128)(2,1)S(1)}) custom-call(bf16[8,4,32,1152]{3,2,1,0:T(8,128)(2,1)S(1)} %get-tuple-element.18.shifted_ref, bf16[512,1152]{1,0:T(8,128)(2,1)S(1)} %copy.10.weight_ref, ...), custom_call_target="tpu_custom_call" | custom-call | flops 1207959552 | tf_op jit(solution)/shard_map/pallas_call | solution.py:344
  50.7 2.3 %collective-permute-start.1 = (bf16[2,128,512]{2,1,0:T(8,128)(2,1)S(1)}, bf16[2,128,512]{2,1,0:T(8,128)(2,1)S(1)}, u32[]{:S(2)}, u32[]{:S(2)}) collective-permute-start(bf16[2,128,512]{2,1,0:T(8,128)(2,1)S(1)} %get-tuple-element.22), channel_id=1, source_target_pairs={{0,64},{64,0},{128,192},{192,128},{1,65},{65,1},{129,193},{193,129... | collective-permute-start | bytes 786440 | tf_op jit(solution)/shard_map/ppermute | solution.py:362
  52.9 5.0 %collective-permute-start.2 = (bf16[2,128,512]{2,1,0:T(8,128)(2,1)S(1)}, bf16[2,128,512]{2,1,0:T(8,128)(2,1)S(1)}, u32[]{:S(2)}, u32[]{:S(2)}) collective-permute-start(bf16[2,128,512]{2,1,0:T(8,128)(2,1)S(1)} %get-tuple-element.23), channel_id=1, source_target_pairs={{0,128},{64,192},{128,0},{192,64},{1,129},{65,193},{129,1},{193,65... | collective-permute-start | bytes 786440 | tf_op jit(solution)/shard_map/ppermute | solution.py:362
  58.0 3.2 %collective-permute-start.3 = (bf16[2,128,512]{2,1,0:T(8,128)(2,1)S(1)}, bf16[2,128,512]{2,1,0:T(8,128)(2,1)S(1)}, u32[]{:S(2)}, u32[]{:S(2)}) collective-permute-start(bf16[2,128,512]{2,1,0:T(8,128)(2,1)S(1)} %get-tuple-element.24), channel_id=1, source_target_pairs={{0,192},{64,128},{128,64},{192,0},{1,193},{65,129},{129,65},{193,1... | collective-permute-start | bytes 786440 | tf_op jit(solution)/shard_map/ppermute | solution.py:362
  61.9 15.2 %all-to-all-start.2 = ((bf16[16,8,1152]{2,1,0:T(8,128)(2,1)}), bf16[16,8,1152]{2,1,0:T(8,128)(2,1)S(1)}, u32[]{:S(2)}, u32[]{:S(2)}) async-start(bf16[16,8,1152]{2,1,0:T(8,128)(2,1)} %bitcast.5), calls=%async_computation.2 | async-start | bytes 589824 | tf_op jit(solution)/shard_map/all_to_all | solution.py:360
  77.4 2.1 %collective-permute-start.4 = (bf16[128,512]{1,0:T(8,128)(2,1)S(1)}, bf16[128,512]{1,0:T(8,128)(2,1)S(1)}, u32[]{:S(2)}, u32[]{:S(2)}) collective-permute-start(bf16[128,512]{1,0:T(8,128)(2,1)S(1)} %get-tuple-element.26), channel_id=1, source_target_pairs={{0,256},{256,0},{1,257},{257,1},{2,258},{258,2},{3,259},{259,3},{4... | collective-permute-start | bytes 393224 | tf_op jit(solution)/shard_map/ppermute | solution.py:287
  79.5 4.8 %collective-permute-done.4.came_ref = bf16[128,512]{1,0:T(8,128)(2,1)S(1)} collective-permute-done((bf16[128,512]{1,0:T(8,128)(2,1)S(1)}, bf16[128,512]{1,0:T(8,128)(2,1)S(1)}, u32[]{:S(2)}, u32[]{:S(2)}) %collective-permute-start.4) | collective-permute-done | bytes 131104 | tf_op jit(solution)/shard_map/ppermute | solution.py:287
  85.0 11.3 %all-to-all-done.2.parts_ref = bf16[16,8,1152]{2,1,0:T(8,128)(2,1)S(1)} async-done(((bf16[16,8,1152]{2,1,0:T(8,128)(2,1)}), bf16[16,8,1152]{2,1,0:T(8,128)(2,1)S(1)}, u32[]{:S(2)}, u32[]{:S(2)}) %all-to-all-start.2) | async-done | bytes 294944 | tf_op jit(solution)/shard_map/all_to_all | solution.py:360
  (21 shorter events, 4.3 us)
Async XLA Ops:
  0.6 0.9 copy-start
  2.6 10.1 %copy-start.6 = (bf16[9,512,128]{2,1,0:T(8,128)(2,1)S(1)}, bf16[9,512,128]{2,1,0:T(8,128)(2,1)}, u32[]{:S(2)}) copy-start(bf16[9,512,128]{2,1,0:T(8,128)(2,1)} %param.6) | copy-start | bytes 3538948
  2.6 19.3 %all-to-all-start = ((bf16[8,128,512]{2,1,0:T(8,128)(2,1)}), bf16[8,128,512]{2,1,0:T(8,128)(2,1)S(1)}, u32[]{:S(2)}, u32[]{:S(2)}) async-start(bf16[8,128,512]{2,1,0:T(8,128)(2,1)} %shard_map.76), calls=%async_computation | async-start | bytes 2097152 | tf_op jit(solution)/shard_map/all_to_all | solution.py:305
  14.1 7.8 %copy-start.1 = (bf16[128,512]{1,0:T(8,128)(2,1)S(1)}, bf16[128,512]{1,0:T(8,128)(2,1)}, u32[]{:S(2)}) copy-start(bf16[128,512]{1,0:T(8,128)(2,1)} %projection_ref.3) | copy-start | bytes 393220
  14.1 7.8 %copy-start.3 = (bf16[1,1,512]{2,1,0:T(2,128)(2,1)S(1)}, bf16[1,1,512]{2,1,0:T(2,128)(2,1)}, u32[]{:S(2)}) copy-start(bf16[1,1,512]{2,1,0:T(2,128)(2,1)} %param.8) | copy-start | bytes 3076
  24.7 0.8 copy-start.4
  25.5 10.4 %all-to-all-start.1 = ((f32[8,8,640]{2,1,0:T(8,128)}), f32[8,8,640]{2,1,0:T(8,128)S(1)}, u32[]{:S(2)}, u32[]{:S(2)}) async-start(f32[8,8,640]{2,1,0:T(8,128)} %get-tuple-element.16), calls=%async_computation.1 | async-start | bytes 327680 | tf_op jit(solution)/shard_map/all_to_all | solution.py:313
  35.9 0.9 copy-start.2
  36.8 1.0 %copy-start.5 = (f32[1024,128]{1,0:T(8,128)S(1)}, f32[1024,128]{1,0:T(8,128)}, u32[]{:S(2)}) copy-start(f32[1024,128]{1,0:T(8,128)} %copy-done.4) | copy-start | bytes 1572868
  40.1 3.9 %collective-permute-start = (bf16[256,1152]{1,0:T(8,128)(2,1)S(1)}, bf16[256,1152]{1,0:T(8,128)(2,1)S(1)}, u32[]{:S(2)}, u32[]{:S(2)}) collective-permute-start(bf16[256,1152]{1,0:T(8,128)(2,1)S(1)} %get-tuple-element.19), channel_id=1, source_target_pairs={{0,1},{1,0},{2,3},{3,2},{4,5},{5,4},{6,7},{7,6},{8,9},{9,8},{10,11... | collective-permute-start | bytes 1769480 | tf_op jit(solution)/shard_map/ppermute | solution.py:287
  44.2 16.9 %collective-permute-start.5 = (bf16[128,1152]{1,0:T(8,128)(2,1)S(1)}, bf16[128,1152]{1,0:T(8,128)(2,1)S(1)}, u32[]{:S(2)}, u32[]{:S(2)}) collective-permute-start(bf16[128,1152]{1,0:T(8,128)(2,1)S(1)} %get-tuple-element.27), channel_id=1, source_target_pairs={{0,32},{32,0},{1,33},{33,1},{2,34},{34,2},{3,35},{35,3},{4,36},{36... | collective-permute-start | bytes 884744 | tf_op jit(solution)/shard_map/ppermute | solution.py:287
  50.7 26.5 %collective-permute-start.1 = (bf16[2,128,512]{2,1,0:T(8,128)(2,1)S(1)}, bf16[2,128,512]{2,1,0:T(8,128)(2,1)S(1)}, u32[]{:S(2)}, u32[]{:S(2)}) collective-permute-start(bf16[2,128,512]{2,1,0:T(8,128)(2,1)S(1)} %get-tuple-element.22), channel_id=1, source_target_pairs={{0,64},{64,0},{128,192},{192,128},{1,65},{65,1},{129,193},{193,129... | collective-permute-start | bytes 786440 | tf_op jit(solution)/shard_map/ppermute | solution.py:362
  52.9 24.2 %collective-permute-start.2 = (bf16[2,128,512]{2,1,0:T(8,128)(2,1)S(1)}, bf16[2,128,512]{2,1,0:T(8,128)(2,1)S(1)}, u32[]{:S(2)}, u32[]{:S(2)}) collective-permute-start(bf16[2,128,512]{2,1,0:T(8,128)(2,1)S(1)} %get-tuple-element.23), channel_id=1, source_target_pairs={{0,128},{64,192},{128,0},{192,64},{1,129},{65,193},{129,1},{193,65... | collective-permute-start | bytes 786440 | tf_op jit(solution)/shard_map/ppermute | solution.py:362
  58.0 19.2 %collective-permute-start.3 = (bf16[2,128,512]{2,1,0:T(8,128)(2,1)S(1)}, bf16[2,128,512]{2,1,0:T(8,128)(2,1)S(1)}, u32[]{:S(2)}, u32[]{:S(2)}) collective-permute-start(bf16[2,128,512]{2,1,0:T(8,128)(2,1)S(1)} %get-tuple-element.24), channel_id=1, source_target_pairs={{0,192},{64,128},{128,64},{192,0},{1,193},{65,129},{129,65},{193,1... | collective-permute-start | bytes 786440 | tf_op jit(solution)/shard_map/ppermute | solution.py:362
  61.9 34.3 %all-to-all-start.2 = ((bf16[16,8,1152]{2,1,0:T(8,128)(2,1)}), bf16[16,8,1152]{2,1,0:T(8,128)(2,1)S(1)}, u32[]{:S(2)}, u32[]{:S(2)}) async-start(bf16[16,8,1152]{2,1,0:T(8,128)(2,1)} %bitcast.5), calls=%async_computation.2 | async-start | bytes 589824 | tf_op jit(solution)/shard_map/all_to_all | solution.py:360
  77.4 6.9 %collective-permute-start.4 = (bf16[128,512]{1,0:T(8,128)(2,1)S(1)}, bf16[128,512]{1,0:T(8,128)(2,1)S(1)}, u32[]{:S(2)}, u32[]{:S(2)}) collective-permute-start(bf16[128,512]{1,0:T(8,128)(2,1)S(1)} %get-tuple-element.26), channel_id=1, source_target_pairs={{0,256},{256,0},{1,257},{257,1},{2,258},{258,2},{3,259},{259,3},{4... | collective-permute-start | bytes 393224 | tf_op jit(solution)/shard_map/ppermute | solution.py:287

commit v3 on v2

--- a/solution.py
+++ b/solution.py
@@ -43,14 +43,9 @@
     )
 
 
-def copy_kernel(own_ref, out_ref, sems):
-    copies = [
-        pltpu.make_async_copy(own_ref.at[0], out_ref.at[c], sems.at[c]) for c in range(clips)
-    ]
-    for copy in copies:
-        copy.start()
-    for copy in copies:
-        copy.wait()
+def copy_kernel(own_ref, given_ref, copies_ref, extra_ref):
+    copies_ref[...] = jnp.broadcast_to(own_ref[...][None], copies_ref.shape)
+    extra_ref[...] = given_ref[...]
 
 
 def frame_index(count):
@@ -69,20 +64,21 @@
     group_ref,
     weight_ref,
     projection_ref,
-    caption_ref,
-    label_ref,
+    extra_ref,
     slope_ref,
+    turned_ref,
     partial_ref,
-    slope_buf,
-    slope_sem,
 ):
     inputs = group_ref[...].reshape(clips * cells, -1)
+    turned = inputs.T.astype(f32).reshape(-1, 2, 8, clips * cells)
+    for core in range(2):
+        turned_ref[core] = turned[:, core].reshape(turned_ref.shape[1:]).astype(bf16)
     out_width = projection_ref.shape[0]
     preact = None
     for a in range(3):
         product = jnp.dot(
             inputs,
-            weight_ref[:, 3 * a * out_width : 3 * (a + 1) * out_width],
+            jnp.concatenate([weight_ref[3 * a + b] for b in range(3)], axis=1),
             preferred_element_type=f32,
         ).reshape(clips, freq, frames, 3 * out_width)
         low = product[..., :out_width]
@@ -103,40 +99,15 @@
             column = shift_rows(column, -1)
         preact = column if preact is None else preact + column
     sigma = jax.nn.sigmoid(preact)
-    slope_buf[...] = sigma * (1.0 + preact * (1.0 - sigma))
-    slope_copy = pltpu.make_async_copy(slope_buf, slope_ref, slope_sem)
-    slope_copy.start()
+    slope_ref[...] = sigma * (1.0 + preact * (1.0 - sigma))
     active = (preact * sigma).reshape(clips, cells, out_width)
     pooled = (jnp.sum(active, axis=1) * (1.0 / cells)).astype(bf16)
     partial = jnp.dot(pooled, projection_ref[...], preferred_element_type=f32)
     embed = partial.shape[1]
     partial_ref[:, :, :embed] = jnp.broadcast_to(partial[None], (clips, clips, embed))
-    own_caption = caption_ref[...].astype(f32)
-    lanes = partial_ref.shape[2] - embed
-    for piece in range(embed // lanes):
-        part = own_caption[:, piece * lanes : (piece + 1) * lanes]
-        partial_ref[:, piece : piece + 1, embed:] = jnp.broadcast_to(
-            part[None], (clips, 1, lanes)
-        )
-    label = jnp.full((clips, clips // 2, lanes), label_ref[0, 0], jnp.int32)
-    partial_ref[:, clips // 2 :, embed:] = label.astype(f32)
-    slope_copy.wait()
-
-
-def turn_kernel(group_ref, turned_ref):
-    channels = group_ref.shape[-1]
-    inputs = group_ref[...].reshape(clips * cells, channels)
-    target = lax.broadcasted_iota(jnp.int32, (channels, channels), 0)
-    source = lax.broadcasted_iota(jnp.int32, (channels, channels), 1)
-    half = channels // 2
-    core = target // half
-    within = target - core * half
-    wanted = ((within // 8) * 2 + core) * 8 + within % 8
-    order = jnp.where(source == wanted, 1.0, 0.0).astype(bf16)
-    turned = lax.dot_general(
-        order, inputs, (((1,), (1,)), ((), ())), preferred_element_type=f32
-    )
-    turned_ref[...] = turned.astype(bf16).reshape(turned_ref.shape)
+    partial_ref[:, :, embed:] = jnp.broadcast_to(
+        extra_ref[...][None], (clips, clips, extra_ref.shape[1])
+    )
 
 
 def row_sum(values):
@@ -157,19 +128,8 @@
     text_ref,
     shifted_ref,
     sent_ref,
-    slope_buf,
-    projection_buf,
-    turned_buf,
-    sems,
 ):
     core = lax.axis_index("core")
-    copies = [
-        pltpu.make_async_copy(projection_ref, projection_buf, sems.at[0]),
-        pltpu.make_async_copy(slope_ref, slope_buf, sems.at[1]),
-        pltpu.make_async_copy(turned_ref.at[1 - core], turned_buf, sems.at[2]),
-    ]
-    for copy in copies:
-        copy.start()
     embed = projection_ref.shape[1]
     lanes = parts_ref.shape[2] - embed
     embedding = jnp.sum(parts_ref[:, :, :embed], axis=0)
@@ -199,14 +159,12 @@
     embedding_grad = (
         (audio_grad - audio_unit * row_sum(audio_unit * audio_grad)) * inv_audio
     ).astype(bf16)
-    copies[0].wait()
     pooled_grad = lax.dot_general(
-        embedding_grad, projection_buf[...], (((1,), (1,)), ((), ())), preferred_element_type=f32
+        embedding_grad, projection_ref[...], (((1,), (1,)), ((), ())), preferred_element_type=f32
     )
     width = pooled_grad.shape[1]
     scaled = pooled_grad * (1.0 / cells)
-    copies[1].wait()
-    pre_grad = (scaled[:, None, :] * slope_buf[...].reshape(clips, cells, width)).astype(bf16)
+    pre_grad = (scaled[:, None, :] * slope_ref[...].reshape(clips, cells, width)).astype(bf16)
     pre_grad = pre_grad.astype(f32).reshape(clips * cells, width)
     zeros = jnp.zeros((clips, frames, width), bf16)
     for a in range(3):
@@ -223,17 +181,13 @@
                 block = moved[:, source] if 0 <= source < freq else zeros
                 shifted_ref[:, f, :, tap * width : (tap + 1) * width] = block
     shifted = shifted_ref[...].reshape(clips * cells, -1)
-    copies[2].wait()
-    sent_ref[...] = jnp.dot(turned_buf[...], shifted, preferred_element_type=f32).astype(bf16)
-
-
-def keep_kernel(turned_ref, shifted_ref, kept_ref, turned_buf, sem):
+    sent_ref[...] = jnp.dot(turned_ref[1 - core], shifted, preferred_element_type=f32).astype(bf16)
+
+
+def keep_kernel(turned_ref, shifted_ref, kept_ref):
     core = lax.axis_index("core")
-    copy = pltpu.make_async_copy(turned_ref.at[core], turned_buf, sem)
-    copy.start()
-    copy.wait()
     shifted = shifted_ref[...].reshape(clips * cells, -1)
-    kept_ref[...] = jnp.dot(turned_buf[...], shifted, preferred_element_type=f32)
+    kept_ref[...] = jnp.dot(turned_ref[core], shifted, preferred_element_type=f32)
 
 
 def half_kernel(kept_ref, came_ref, mine_ref, sent_ref, total_ref):
@@ -246,8 +200,9 @@
 def input_kernel(shifted_ref, weight_ref, after_ref, *rest):
     out_refs, total_ref = rest[:columns], rest[columns]
     shifted = shifted_ref[...].reshape(clips * cells, -1)
+    weight = jnp.concatenate([weight_ref[tap] for tap in range(weight_ref.shape[0])], axis=1)
     result = lax.dot_general(
-        shifted, weight_ref[...], (((1,), (1,)), ((), ())), preferred_element_type=f32
+        shifted, weight, (((1,), (1,)), ((), ())), preferred_element_type=f32
     )
     total_ref[...] = result.astype(bf16).reshape(total_ref.shape)
     here = lax.axis_index("x")
@@ -262,11 +217,12 @@
     copy.wait()
 
 
-def column_kernel(own_ref, a_ref, b_ref, c_ref, mine_ref, sent_ref, total_ref):
-    total = own_ref[...].astype(f32)
-    for ref in (a_ref, b_ref, c_ref):
-        total = total + ref[...].astype(f32)
-    total_ref[...] = total
+def near_kernel(own_ref, a_ref, b_ref, total_ref):
+    total_ref[...] = own_ref[...].astype(f32) + a_ref[...].astype(f32) + b_ref[...].astype(f32)
+
+
+def column_kernel(near_ref, c_ref, mine_ref, sent_ref, total_ref):
+    total_ref[...] = near_ref[...] + c_ref[...].astype(f32)
     side = lax.axis_index("ylo")
     mine_ref[...] = total_ref[side]
     sent_ref[...] = total_ref[1 - side].astype(bf16)
@@ -294,24 +250,26 @@
     half = channels // 2
     quarter = half // 2
     matmul = 2 * clips * cells * channels * wide
-    weight = jnp.transpose(conv_weight, (1, 0, 2)).reshape(channels, wide)
-    copies = call(
-        copy_kernel,
-        shape((clips, cells, channels), bf16),
-        scratch=[DMA((clips,))],
-        in_specs=[HBM],
-        out_specs=HBM,
-    )(features.reshape(1, cells, channels))
+    given = jnp.concatenate(
+        [
+            text.reshape(4, embed // 4).astype(f32),
+            jnp.broadcast_to(labels.astype(f32), (4, embed // 4)),
+        ]
+    )
+    copies, extra = call(
+        copy_kernel, (shape((clips, cells, channels), bf16), shape(given.shape, f32))
+    )(features.reshape(cells, channels), given)
     group = lax.all_to_all(copies, BLK, 0, 0)
-    slope, partial = call(
+    slope, turned, partial = call(
         forward_kernel,
-        (shape((clips * cells, width), f32), shape((clips, clips, embed + 128), f32)),
-        scratch=[pltpu.VMEM((clips * cells, width), f32), DMA],
-        out_specs=(HBM, VMEM),
+        (
+            shape((clips * cells, width), f32),
+            shape((2, half, clips * cells), bf16),
+            shape((clips, clips, embed + 128), f32),
+        ),
         flops=matmul,
-    )(group, weight, projection, text.reshape(1, embed), labels)
+    )(group, conv_weight, projection, extra)
     parts = lax.all_to_all(partial, BLK, 0, 0)
-    turned = call(turn_kernel, shape((2, half, clips * cells), bf16), flops=matmul // 4)(group)
     grad_text, shifted, sent = call(
         pair_kernel,
         (
@@ -319,20 +277,11 @@
             shape((clips, freq, frames, wide), bf16),
             shape((half, wide), bf16),
         ),
-        scratch=[
-            pltpu.VMEM((clips * cells, width), f32),
-            pltpu.VMEM(projection.shape, bf16),
-            pltpu.VMEM((half, clips * cells), bf16),
-            DMA((3,)),
-        ],
-        in_specs=[VMEM, HBM, HBM, HBM],
         flops=matmul // 2,
     )(parts, slope, projection, turned)
     kept = call(
         keep_kernel,
         shape((half, wide), f32),
-        scratch=[pltpu.VMEM((half, clips * cells), bf16), DMA],
-        in_specs=[HBM, VMEM],
         flops=matmul // 2,
     )(turned, shifted)
     came = swap(sent, "core")
@@ -347,7 +296,7 @@
         scratch=[pltpu.VMEM((2, columns, cells, channels), bf16)],
         in_specs=[VMEM, VMEM, pl.BlockSpec(memory_space=pl.ANY)],
         flops=matmul,
-    )(shifted, weight, kept)
+    )(shifted, conv_weight, kept)
     came = swap(sent, "yhi")
     sent = call(
         add_kernel,
@@ -362,12 +311,15 @@
         lax.ppermute(columns_out[d], "x", [(i, i ^ d) for i in range(columns)])
         for d in range(1, columns)
     ]
+    near = call(near_kernel, shape((2, cells, channels), f32), flops=int(1e10))(
+        columns_out[0], others[0], others[2]
+    )
     mine, other = call(
         column_kernel,
         (shape((cells, channels), f32), shape((cells, channels), bf16)),
         scratch=[pltpu.VMEM((2, cells, channels), f32)],
-        flops=int(1e10),
-    )(columns_out[0], *others)
+        flops=int(0),
+    )(near, others[1])
     grad_features = call(join_kernel, shape((cells, channels), bf16))(mine, swap(other, "ylo"))
     grad_weight = call(
         functools.partial(final_kernel, heights * 4),

time: 98.8 us -> 89.7 us (0.908)
  blocking collectives: 0 us -> 28.8 us
  starting transfers between devices: 49.5 us -> 34.1 us
  waiting for transfers between devices: 27.1 us -> 14.2 us
  local copies, waits for them, and re-layouts: 6.79 us -> 0.92 us
  Pallas kernels: 12 us -> 8.61 us
    all_to_all x0 -> x2, blocking collectives: none -> 28.8 us  [the longest x1 19.3 us: shards(): group = lax.all_to_all(copies, BLK, 0, 0)]
    all_to_all x2 -> x0, starting transfers between devices: 15.1 us -> none  [the longest x1 9.47 us: shards(): group = lax.all_to_all(copies, BLK, 0, 0)]
    all_to_all x1, waiting for transfers between devices: 11.3 us -> 1.18 us  [shards(): lax.all_to_all(sent.reshape(heights, quarter // heights, wide), Z, 0, 0)]
    all_to_all x2 -> x0, waiting for transfers between devices: 9.98 us -> none  [the longest x1 6.07 us: shards(): group = lax.all_to_all(copies, BLK, 0, 0)]
    ppermute x3, waiting for transfers between devices: 0.01 us -> 7.01 us  [shards(): lax.ppermute(columns_out[d], 'x', [(i, i ^ d) for i in range(columns)])]
    unnamed x15 -> x6, local copies, waits for them, and re-layouts: 5.08 us -> 0.91 us
    pallas_call x4, Pallas kernels: 5.53 us -> 3.01 us  [the longest x1 2.01 us: shards(): call(forward_kernel, (shape((clips * cells, width), f32), shape((2, half,...]
    reshape x1 -> x0, local copies, waits for them, and re-layouts: 1.71 us -> none  [shards(): weight = jnp.transpose(conv_weight, (1, 0, 2)).reshape(channels, wide)]
  transfers between devices with their start and end apart: 9 -> 7, of which waited for: 5 -> 4; matrix products, arithmetic and copies ran while one was open for 3% -> 0% of each run, Pallas kernels for 5% -> 5%
where the time goes in v3:
time: 89.7 us; the launch traced here: 88.7 us
  starting transfers between devices  34.1 us (38%)
  blocking collectives  28.8 us (32%)
  waiting for transfers between devices  14.2 us (16%)
  Pallas kernels  8.61 us (10%)
  between operations  1.41 us (2%)
  local copies, waits for them, and re-layouts  0.92 us (1%)
    all_to_all x1, blocking collectives, shards(): group = lax.all_to_all(copies, BLK, 0, 0)  19.3 us
    all_to_all x1, starting transfers between devices, shards(): lax.all_to_all(sent.reshape(heights, quarter // heights, wide), Z, 0, 0)  15.2 us
    ppermute x3, starting transfers between devices, shards(): lax.ppermute(columns_out[d], 'x', [(i, i ^ d) for i in range(columns)])  10.1 us
    all_to_all x1, blocking collectives, shards(): parts = lax.all_to_all(partial, BLK, 0, 0)  9.42 us
    ppermute x3, starting transfers between devices, swap(): return lax.ppermute(values, axis, [(0, 1), (1, 0)])  8.77 us
    ppermute x3, waiting for transfers between devices, shards(): lax.ppermute(columns_out[d], 'x', [(i, i ^ d) for i in range(columns)])  7.01 us
    ppermute x3, waiting for transfers between devices, swap(): return lax.ppermute(values, axis, [(0, 1), (1, 0)])  5.98 us
    pallas_call x1, Pallas kernels, shards(): call(forward_kernel, (shape((clips * cells, width), f32), shape((2, half,...  2.01 us
  transfers between devices with their start and end apart: 7, of which 4 were waited for; matrix products, arithmetic and copies ran while one was open for 0% of the time, Pallas kernels for 5%

profile of v3, /device:TPU:6, one launch (start us, length us, event | category | flops | bytes accessed | tf_op | source)
XLA Modules:
  0.0 88.7 jit_solution(5160243381010320830)
XLA Ops:
  1.3 0.7 convert_element_type.12
  2.0 0.9 %copy-done = bf16[1,1,4,32,512]{4,3,2,1,0:T(8,128)(2,1)S(1)} copy-done((bf16[1,1,4,32,512]{4,3,2,1,0:T(8,128)(2,1)S(1)}, bf16[1,1,4,32,512]{4,3,2,1,0:T(8,128)(2,1)}, u32[]{:S(2)}) %copy-start) | copy-done | bytes 131096
  3.0 19.3 %all_to_all.15.group_ref = bf16[8,128,512]{2,1,0:T(8,128)(2,1)S(1)} all-to-all(bf16[8,128,512]{2,1,0:T(8,128)(2,1)S(1)} %get-tuple-element.19), channel_id=1, replica_groups=mesh['ylo'=2,'x'=4,'yhi'=2,'z'=16,'core'=2] {'ylo','x'}, dimensions={0} | all-to-all | bytes 2097152 | tf_op jit(solution)/shard_map/all_to_all | solution.py:262
  22.3 2.0 %shard_map.77 = (f32[1024,128]{1,0:T(8,128)S(1)}, bf16[2,256,1024]{2,1,0:T(8,128)(2,1)S(1)}, f32[8,8,640]{2,1,0:T(8,128)S(1)}) custom-call(bf16[8,128,512]{2,1,0:T(8,128)(2,1)S(1)} %all_to_all.15.group_ref, bf16[9,512,128]{2,1,0:T(8,128)(2,1)S(1)} %copy-done.1, bf16[128,512]{1,0:T(8,128)(2,1)S(1)} %copy-done.2, f32[8,128]{1,0:T(8,128)S(1)} %get-tuple-element.20.extra_ref), custom_call_target="tpu_custom_call" | custom-call | flops 1207959552 | tf_op jit(solution)/shard_map/pallas_call | solution.py:263
  24.3 9.4 %all_to_all.16.parts_ref = f32[8,8,640]{2,1,0:T(8,128)S(1)} all-to-all(f32[8,8,640]{2,1,0:T(8,128)S(1)} %get-tuple-element.21), channel_id=1, replica_groups=mesh['ylo'=2,'x'=4,'yhi'=2,'z'=16,'core'=2] {'ylo','x'}, dimensions={0} | all-to-all | bytes 327680 | tf_op jit(solution)/shard_map/all_to_all | solution.py:272
  33.7 1.5 %shard_map.78 = (f32[1,512]{1,0:T(1,128)}, bf16[8,4,32,1152]{3,2,1,0:T(8,128)(2,1)S(1)}, bf16[256,1152]{1,0:T(8,128)(2,1)S(1)}) custom-call(f32[8,8,640]{2,1,0:T(8,128)S(1)} %all_to_all.16.parts_ref, f32[1024,128]{1,0:T(8,128)S(1)} %get-tuple-element.22.slope_ref, bf16[128,512]{1,0:T(8,128)(2,1)S(1)} %copy-done.2, ...), custom_call_target="tpu_custom_call" | custom-call | flops 603979776 | tf_op jit(solution)/shard_map/pallas_call | solution.py:273
  35.2 1.9 %collective-permute-start = (bf16[256,1152]{1,0:T(8,128)(2,1)S(1)}, bf16[256,1152]{1,0:T(8,128)(2,1)S(1)}, u32[]{:S(2)}, u32[]{:S(2)}) collective-permute-start(bf16[256,1152]{1,0:T(8,128)(2,1)S(1)} %get-tuple-element.25), channel_id=1, source_target_pairs={{0,1},{1,0},{2,3},{3,2},{4,5},{5,4},{6,7},{7,6},{8,9},{9,8},{10,11... | collective-permute-start | bytes 1769480 | tf_op jit(solution)/shard_map/ppermute | solution.py:243
  37.1 0.8 shard_map.79.kept_ref
  38.0 1.1 %collective-permute-done.came_ref = bf16[256,1152]{1,0:T(8,128)(2,1)S(1)} collective-permute-done((bf16[256,1152]{1,0:T(8,128)(2,1)S(1)}, bf16[256,1152]{1,0:T(8,128)(2,1)S(1)}, u32[]{:S(2)}, u32[]{:S(2)}) %collective-permute-start) | collective-permute-done | bytes 589856 | tf_op jit(solution)/shard_map/ppermute | solution.py:243
  39.1 0.2 shard_map.80
  39.4 4.9 %collective-permute-start.5 = (bf16[128,1152]{1,0:T(8,128)(2,1)S(1)}, bf16[128,1152]{1,0:T(8,128)(2,1)S(1)}, u32[]{:S(2)}, u32[]{:S(2)}) collective-permute-start(bf16[128,1152]{1,0:T(8,128)(2,1)S(1)} %get-tuple-element.33), channel_id=1, source_target_pairs={{0,32},{32,0},{1,33},{33,1},{2,34},{34,2},{3,35},{35,3},{4,36},{36... | collective-permute-start | bytes 884744 | tf_op jit(solution)/shard_map/ppermute | solution.py:243
  44.2 1.6 %shard_map.81 = (bf16[2,128,512]{2,1,0:T(8,128)(2,1)S(1)}, bf16[2,128,512]{2,1,0:T(8,128)(2,1)S(1)}, bf16[2,128,512]{2,1,0:T(8,128)(2,1)S(1)}, bf16[2,128,512]{2,1,0:T(8,128)(2,1)S(1)}) custom-call(bf16[8,4,32,1152]{3,2,1,0:T(8,128)(2,1)S(1)} %get-tuple-element.24.shifted_ref, bf16[9,512,128]{2,1,0:T(8,128)(2,1)S(1)} %copy-done.1, ...), custom_call_target="tpu_custom_call" | custom-call | flops 1207959552 | tf_op jit(solution)/shard_map/pallas_call | solution.py:293
  45.9 2.2 %collective-permute-start.1 = (bf16[2,128,512]{2,1,0:T(8,128)(2,1)S(1)}, bf16[2,128,512]{2,1,0:T(8,128)(2,1)S(1)}, u32[]{:S(2)}, u32[]{:S(2)}) collective-permute-start(bf16[2,128,512]{2,1,0:T(8,128)(2,1)S(1)} %get-tuple-element.28), channel_id=1, source_target_pairs={{0,64},{64,0},{128,192},{192,128},{1,65},{65,1},{129,193},{193,129... | collective-permute-start | bytes 786440 | tf_op jit(solution)/shard_map/ppermute | solution.py:311
  48.1 4.4 %collective-permute-start.2 = (bf16[2,128,512]{2,1,0:T(8,128)(2,1)S(1)}, bf16[2,128,512]{2,1,0:T(8,128)(2,1)S(1)}, u32[]{:S(2)}, u32[]{:S(2)}) collective-permute-start(bf16[2,128,512]{2,1,0:T(8,128)(2,1)S(1)} %get-tuple-element.29), channel_id=1, source_target_pairs={{0,192},{64,128},{128,64},{192,0},{1,193},{65,129},{129,65},{193,1... | collective-permute-start | bytes 786440 | tf_op jit(solution)/shard_map/ppermute | solution.py:311
  52.5 0.8 shard_map.85
  53.3 15.2 %all-to-all-start.2 = ((bf16[16,8,1152]{2,1,0:T(8,128)(2,1)}), bf16[16,8,1152]{2,1,0:T(8,128)(2,1)S(1)}, u32[]{:S(2)}, u32[]{:S(2)}) async-start(bf16[16,8,1152]{2,1,0:T(8,128)(2,1)} %bitcast.4), calls=%async_computation.2 | async-start | bytes 589824 | tf_op jit(solution)/shard_map/all_to_all | solution.py:309
  68.5 3.5 %collective-permute-start.3 = (bf16[2,128,512]{2,1,0:T(8,128)(2,1)S(1)}, bf16[2,128,512]{2,1,0:T(8,128)(2,1)S(1)}, u32[]{:S(2)}, u32[]{:S(2)}) collective-permute-start(bf16[2,128,512]{2,1,0:T(8,128)(2,1)S(1)} %get-tuple-element.30), channel_id=1, source_target_pairs={{0,128},{64,192},{128,0},{192,64},{1,129},{65,193},{129,1},{193,65... | collective-permute-start | bytes 786440 | tf_op jit(solution)/shard_map/ppermute | solution.py:311
  72.2 7.0 %collective-permute-done.3.c_ref = bf16[2,128,512]{2,1,0:T(8,128)(2,1)S(1)} collective-permute-done((bf16[2,128,512]{2,1,0:T(8,128)(2,1)S(1)}, bf16[2,128,512]{2,1,0:T(8,128)(2,1)S(1)}, u32[]{:S(2)}, u32[]{:S(2)}) %collective-permute-start.3) | collective-permute-done | bytes 262176 | tf_op jit(solution)/shard_map/ppermute | solution.py:311
  79.2 0.1 shard_map.83
  79.3 2.0 %collective-permute-start.4 = (bf16[128,512]{1,0:T(8,128)(2,1)S(1)}, bf16[128,512]{1,0:T(8,128)(2,1)S(1)}, u32[]{:S(2)}, u32[]{:S(2)}) collective-permute-start(bf16[128,512]{1,0:T(8,128)(2,1)S(1)} %get-tuple-element.32), channel_id=1, source_target_pairs={{0,256},{256,0},{1,257},{257,1},{2,258},{258,2},{3,259},{259,3},{4... | collective-permute-start | bytes 393224 | tf_op jit(solution)/shard_map/ppermute | solution.py:243
  81.3 4.9 %collective-permute-done.4.came_ref = bf16[128,512]{1,0:T(8,128)(2,1)S(1)} collective-permute-done((bf16[128,512]{1,0:T(8,128)(2,1)S(1)}, bf16[128,512]{1,0:T(8,128)(2,1)S(1)}, u32[]{:S(2)}, u32[]{:S(2)}) %collective-permute-start.4) | collective-permute-done | bytes 131104 | tf_op jit(solution)/shard_map/ppermute | solution.py:243
  86.1 0.7 shard_map.84
  86.8 1.2 %all-to-all-done.2.parts_ref = bf16[16,8,1152]{2,1,0:T(8,128)(2,1)S(1)} async-done(((bf16[16,8,1152]{2,1,0:T(8,128)(2,1)}), bf16[16,8,1152]{2,1,0:T(8,128)(2,1)S(1)}, u32[]{:S(2)}, u32[]{:S(2)}) %all-to-all-start.2) | async-done | bytes 294944 | tf_op jit(solution)/shard_map/all_to_all | solution.py:309
  88.0 0.7 shard_map.86
  (11 shorter events, 0.2 us)
Async XLA Ops:
  2.0 0.9 %copy-start = (bf16[1,1,4,32,512]{4,3,2,1,0:T(8,128)(2,1)S(1)}, bf16[1,1,4,32,512]{4,3,2,1,0:T(8,128)(2,1)}, u32[]{:S(2)}) copy-start(bf16[1,1,4,32,512]{4,3,2,1,0:T(8,128)(2,1)} %param.5) | copy-start | bytes 393220
  2.9 19.4 %copy-start.1 = (bf16[9,512,128]{2,1,0:T(8,128)(2,1)S(1)}, bf16[9,512,128]{2,1,0:T(8,128)(2,1)}, u32[]{:S(2)}) copy-start(bf16[9,512,128]{2,1,0:T(8,128)(2,1)} %weight_ref.3) | copy-start | bytes 3538948
  2.9 19.4 %copy-start.2 = (bf16[128,512]{1,0:T(8,128)(2,1)S(1)}, bf16[128,512]{1,0:T(8,128)(2,1)}, u32[]{:S(2)}) copy-start(bf16[128,512]{1,0:T(8,128)(2,1)} %projection_ref.3) | copy-start | bytes 393220
  35.2 3.9 %collective-permute-start = (bf16[256,1152]{1,0:T(8,128)(2,1)S(1)}, bf16[256,1152]{1,0:T(8,128)(2,1)S(1)}, u32[]{:S(2)}, u32[]{:S(2)}) collective-permute-start(bf16[256,1152]{1,0:T(8,128)(2,1)S(1)} %get-tuple-element.25), channel_id=1, source_target_pairs={{0,1},{1,0},{2,3},{3,2},{4,5},{5,4},{6,7},{7,6},{8,9},{9,8},{10,11... | collective-permute-start | bytes 1769480 | tf_op jit(solution)/shard_map/ppermute | solution.py:243
  39.4 13.2 %collective-permute-start.5 = (bf16[128,1152]{1,0:T(8,128)(2,1)S(1)}, bf16[128,1152]{1,0:T(8,128)(2,1)S(1)}, u32[]{:S(2)}, u32[]{:S(2)}) collective-permute-start(bf16[128,1152]{1,0:T(8,128)(2,1)S(1)} %get-tuple-element.33), channel_id=1, source_target_pairs={{0,32},{32,0},{1,33},{33,1},{2,34},{34,2},{3,35},{35,3},{4,36},{36... | collective-permute-start | bytes 884744 | tf_op jit(solution)/shard_map/ppermute | solution.py:243
  45.9 26.2 %collective-permute-start.1 = (bf16[2,128,512]{2,1,0:T(8,128)(2,1)S(1)}, bf16[2,128,512]{2,1,0:T(8,128)(2,1)S(1)}, u32[]{:S(2)}, u32[]{:S(2)}) collective-permute-start(bf16[2,128,512]{2,1,0:T(8,128)(2,1)S(1)} %get-tuple-element.28), channel_id=1, source_target_pairs={{0,64},{64,0},{128,192},{192,128},{1,65},{65,1},{129,193},{193,129... | collective-permute-start | bytes 786440 | tf_op jit(solution)/shard_map/ppermute | solution.py:311
  48.1 24.0 %collective-permute-start.2 = (bf16[2,128,512]{2,1,0:T(8,128)(2,1)S(1)}, bf16[2,128,512]{2,1,0:T(8,128)(2,1)S(1)}, u32[]{:S(2)}, u32[]{:S(2)}) collective-permute-start(bf16[2,128,512]{2,1,0:T(8,128)(2,1)S(1)} %get-tuple-element.29), channel_id=1, source_target_pairs={{0,192},{64,128},{128,64},{192,0},{1,193},{65,129},{129,65},{193,1... | collective-permute-start | bytes 786440 | tf_op jit(solution)/shard_map/ppermute | solution.py:311
  53.3 34.7 %all-to-all-start.2 = ((bf16[16,8,1152]{2,1,0:T(8,128)(2,1)}), bf16[16,8,1152]{2,1,0:T(8,128)(2,1)S(1)}, u32[]{:S(2)}, u32[]{:S(2)}) async-start(bf16[16,8,1152]{2,1,0:T(8,128)(2,1)} %bitcast.4), calls=%async_computation.2 | async-start | bytes 589824 | tf_op jit(solution)/shard_map/all_to_all | solution.py:309
  68.5 10.6 %collective-permute-start.3 = (bf16[2,128,512]{2,1,0:T(8,128)(2,1)S(1)}, bf16[2,128,512]{2,1,0:T(8,128)(2,1)S(1)}, u32[]{:S(2)}, u32[]{:S(2)}) collective-permute-start(bf16[2,128,512]{2,1,0:T(8,128)(2,1)S(1)} %get-tuple-element.30), channel_id=1, source_target_pairs={{0,128},{64,192},{128,0},{192,64},{1,129},{65,193},{129,1},{193,65... | collective-permute-start | bytes 786440 | tf_op jit(solution)/shard_map/ppermute | solution.py:311
  79.3 6.9 %collective-permute-start.4 = (bf16[128,512]{1,0:T(8,128)(2,1)S(1)}, bf16[128,512]{1,0:T(8,128)(2,1)S(1)}, u32[]{:S(2)}, u32[]{:S(2)}) collective-permute-start(bf16[128,512]{1,0:T(8,128)(2,1)S(1)} %get-tuple-element.32), channel_id=1, source_target_pairs={{0,256},{256,0},{1,257},{257,1},{2,258},{258,2},{3,259},{259,3},{4... | collective-permute-start | bytes 393224 | tf_op jit(solution)/shard_map/ppermute | solution.py:243

commit v4 on v3

--- a/solution.py
+++ b/solution.py
@@ -13,7 +13,8 @@
 norm_eps = 1e-06
 
 BLK = ("ylo", "x")
-Z = "z"
+NEAR = ("yhi", "zl")
+FAR = "z8"
 f32 = jnp.float32
 bf16 = jnp.bfloat16
 
@@ -22,6 +23,9 @@
 frames = 32
 cells = freq * frames
 columns = 4
+heights = 8
+first_far = 4
+far_order = [(first_far + p) % heights for p in range(heights)]
 vmem_limit = 40 * 1024 * 1024
 HBM = pl.BlockSpec(memory_space=pltpu.HBM)
 VMEM = pl.BlockSpec(memory_space=pltpu.VMEM)
@@ -43,9 +47,14 @@
     )
 
 
-def copy_kernel(own_ref, given_ref, copies_ref, extra_ref):
-    copies_ref[...] = jnp.broadcast_to(own_ref[...][None], copies_ref.shape)
-    extra_ref[...] = given_ref[...]
+def copy_kernel(own_ref, copies_ref, extra_ref):
+    copies_ref[...] = jnp.broadcast_to(own_ref[:cells][None], copies_ref.shape)
+    last = own_ref[cells:].astype(f32)
+    lanes = extra_ref.shape[1]
+    pieces = last.shape[1] // lanes
+    for piece in range(pieces):
+        extra_ref[piece : piece + 1, :] = last[:1, piece * lanes : (piece + 1) * lanes]
+    extra_ref[pieces:, :] = last[8 : 8 + clips - pieces, :lanes]
 
 
 def frame_index(count):
@@ -70,9 +79,15 @@
     partial_ref,
 ):
     inputs = group_ref[...].reshape(clips * cells, -1)
-    turned = inputs.T.astype(f32).reshape(-1, 2, 8, clips * cells)
+    turned = inputs.T.astype(f32).reshape(2, heights, 2, 2, 8, clips * cells)
+    turned = jnp.concatenate([turned[:, first_far:], turned[:, :first_far]], axis=1)
+    block = heights * 8
     for core in range(2):
-        turned_ref[core] = turned[:, core].reshape(turned_ref.shape[1:]).astype(bf16)
+        for yhi in range(2):
+            for zl in range(2):
+                rows = turned[yhi, :, zl, core].reshape(block, clips * cells)
+                low = (2 * yhi + zl) * block
+                turned_ref[core, low : low + block] = rows.astype(bf16)
     out_width = projection_ref.shape[0]
     preact = None
     for a in range(3):
@@ -120,14 +135,34 @@
     return -loss_scale * signs * jax.nn.sigmoid(-signs * logits)
 
 
+def shift_all(pre_grad, shifted_ref):
+    width = pre_grad.shape[1]
+    zeros = jnp.zeros((clips, frames, width), bf16)
+    for a in range(3):
+        moved = pre_grad
+        if a == 0:
+            moved = shift_rows(pre_grad, -1)
+        if a == 2:
+            moved = shift_rows(pre_grad, 1)
+        moved = moved.astype(bf16).reshape(clips, freq, frames, width)
+        for b in range(3):
+            tap = 3 * a + b
+            for f in range(freq):
+                source = f - (b - 1)
+                block = moved[:, source] if 0 <= source < freq else zeros
+                shifted_ref[:, f, :, tap * width : (tap + 1) * width] = block
+    return shifted_ref[...].reshape(clips * cells, -1)
+
+
 def pair_kernel(
     parts_ref,
     slope_ref,
     projection_ref,
     turned_ref,
     text_ref,
+    pre_ref,
+    sent_ref,
     shifted_ref,
-    sent_ref,
 ):
     core = lax.axis_index("core")
     embed = projection_ref.shape[1]
@@ -166,40 +201,16 @@
     scaled = pooled_grad * (1.0 / cells)
     pre_grad = (scaled[:, None, :] * slope_ref[...].reshape(clips, cells, width)).astype(bf16)
     pre_grad = pre_grad.astype(f32).reshape(clips * cells, width)
-    zeros = jnp.zeros((clips, frames, width), bf16)
-    for a in range(3):
-        moved = pre_grad
-        if a == 0:
-            moved = shift_rows(pre_grad, -1)
-        if a == 2:
-            moved = shift_rows(pre_grad, 1)
-        moved = moved.astype(bf16).reshape(clips, freq, frames, width)
-        for b in range(3):
-            tap = 3 * a + b
-            for f in range(freq):
-                source = f - (b - 1)
-                block = moved[:, source] if 0 <= source < freq else zeros
-                shifted_ref[:, f, :, tap * width : (tap + 1) * width] = block
-    shifted = shifted_ref[...].reshape(clips * cells, -1)
+    pre_ref[...] = pre_grad.astype(bf16)
+    shifted = shift_all(pre_grad, shifted_ref)
     sent_ref[...] = jnp.dot(turned_ref[1 - core], shifted, preferred_element_type=f32).astype(bf16)
 
 
-def keep_kernel(turned_ref, shifted_ref, kept_ref):
+def keep_kernel(turned_ref, pre_ref, weight_ref, kept_ref, *rest):
+    out_refs, total_ref, shifted_ref = rest[:columns], rest[columns], rest[columns + 1]
     core = lax.axis_index("core")
-    shifted = shifted_ref[...].reshape(clips * cells, -1)
+    shifted = shift_all(pre_ref[...].astype(f32), shifted_ref)
     kept_ref[...] = jnp.dot(turned_ref[core], shifted, preferred_element_type=f32)
-
-
-def half_kernel(kept_ref, came_ref, mine_ref, sent_ref, total_ref):
-    total_ref[...] = (kept_ref[...] + came_ref[...].astype(f32)).reshape(total_ref.shape)
-    side = lax.axis_index("yhi")
-    mine_ref[...] = total_ref[side]
-    sent_ref[...] = total_ref[1 - side].astype(bf16)
-
-
-def input_kernel(shifted_ref, weight_ref, after_ref, *rest):
-    out_refs, total_ref = rest[:columns], rest[columns]
-    shifted = shifted_ref[...].reshape(clips * cells, -1)
     weight = jnp.concatenate([weight_ref[tap] for tap in range(weight_ref.shape[0])], axis=1)
     result = lax.dot_general(
         shifted, weight, (((1,), (1,)), ((), ())), preferred_element_type=f32
@@ -210,8 +221,22 @@
         out_refs[d][...] = total_ref[:, here ^ d]
 
 
-def add_kernel(kept_ref, came_ref, after_ref, sent_ref, sent_buf, sem):
-    sent_buf[...] = (kept_ref[...] + came_ref[...].astype(f32)).astype(bf16)
+def pair_sum_kernel(kept_ref, came_ref, sent_ref, sent_buf, sems):
+    copies = []
+    count = sent_buf.shape[1]
+    for piece in range(sent_buf.shape[0]):
+        rows = slice(piece * count, (piece + 1) * count)
+        sent_buf[piece] = (kept_ref[rows] + came_ref[rows].astype(f32)).astype(bf16)
+        copies.append(
+            pltpu.make_async_copy(sent_buf.at[piece], sent_ref.at[piece], sems.at[piece])
+        )
+        copies[-1].start()
+    for copy in copies:
+        copy.wait()
+
+
+def add_kernel(parts_ref, after_ref, sent_ref, sent_buf, sem):
+    sent_buf[...] = jnp.sum(parts_ref[...].astype(f32), axis=0).astype(bf16)
     copy = pltpu.make_async_copy(sent_buf, sent_ref, sem)
     copy.start()
     copy.wait()
@@ -248,17 +273,18 @@
     wide = taps * width
     embed = projection.shape[1]
     half = channels // 2
-    quarter = half // 2
+    quarter = half // 4
     matmul = 2 * clips * cells * channels * wide
-    given = jnp.concatenate(
+    own = jnp.concatenate(
         [
-            text.reshape(4, embed // 4).astype(f32),
-            jnp.broadcast_to(labels.astype(f32), (4, embed // 4)),
+            features.reshape(cells, channels),
+            text.reshape(1, channels),
+            jnp.broadcast_to(labels.astype(bf16), (15, channels)),
         ]
     )
     copies, extra = call(
-        copy_kernel, (shape((clips, cells, channels), bf16), shape(given.shape, f32))
-    )(features.reshape(cells, channels), given)
+        copy_kernel, (shape((clips, cells, channels), bf16), shape((clips, 128), f32))
+    )(own)
     group = lax.all_to_all(copies, BLK, 0, 0)
     slope, turned, partial = call(
         forward_kernel,
@@ -270,59 +296,58 @@
         flops=matmul,
     )(group, conv_weight, projection, extra)
     parts = lax.all_to_all(partial, BLK, 0, 0)
-    grad_text, shifted, sent = call(
+    shifted_buf = pltpu.VMEM((clips, freq, frames, wide), bf16)
+    grad_text, pre, sent = call(
         pair_kernel,
         (
             shape((1, embed), f32),
-            shape((clips, freq, frames, wide), bf16),
+            shape((clips * cells, width), bf16),
             shape((half, wide), bf16),
         ),
+        scratch=[shifted_buf],
         flops=matmul // 2,
     )(parts, slope, projection, turned)
-    kept = call(
+    kept, *columns_out = call(
         keep_kernel,
-        shape((half, wide), f32),
-        flops=matmul // 2,
-    )(turned, shifted)
+        (shape((half, wide), f32),)
+        + tuple(shape((2, cells, channels), bf16) for _ in range(columns)),
+        scratch=[pltpu.VMEM((2, columns, cells, channels), bf16), shifted_buf],
+        flops=matmul + matmul // 2,
+    )(turned, pre, conv_weight)
     came = swap(sent, "core")
-    kept, sent = call(
-        half_kernel,
-        (shape((quarter, wide), f32), shape((quarter, wide), bf16)),
-        scratch=[pltpu.VMEM((2, quarter, wide), f32)],
+    sent = call(
+        pair_sum_kernel,
+        shape((4, quarter, wide), bf16),
+        scratch=[pltpu.VMEM((4, quarter, wide), bf16), DMA((4,))],
+        out_specs=HBM,
     )(kept, came)
-    columns_out = call(
-        input_kernel,
-        tuple(shape((2, cells, channels), bf16) for _ in range(columns)),
-        scratch=[pltpu.VMEM((2, columns, cells, channels), bf16)],
-        in_specs=[VMEM, VMEM, pl.BlockSpec(memory_space=pl.ANY)],
-        flops=matmul,
-    )(shifted, conv_weight, kept)
-    came = swap(sent, "yhi")
+    parts = lax.all_to_all(sent, NEAR, 0, 0)
     sent = call(
         add_kernel,
         shape((quarter, wide), bf16),
         scratch=[pltpu.VMEM((quarter, wide), bf16), DMA],
-        in_specs=[VMEM, VMEM, pl.BlockSpec(memory_space=pl.ANY)],
+        in_specs=[VMEM, pl.BlockSpec(memory_space=pl.ANY)],
         out_specs=HBM,
-    )(kept, came, columns_out[0])
-    heights = lax.axis_size(Z)
-    parts = lax.all_to_all(sent.reshape(heights, quarter // heights, wide), Z, 0, 0)
+    )(parts, columns_out[0])
+    parts = lax.all_to_all(
+        sent.reshape(heights, quarter // heights, wide), FAR, 0, 0, axis_index_groups=[far_order]
+    )
     others = [
         lax.ppermute(columns_out[d], "x", [(i, i ^ d) for i in range(columns)])
         for d in range(1, columns)
     ]
-    near = call(near_kernel, shape((2, cells, channels), f32), flops=int(1e10))(
+    near = call(near_kernel, shape((2, cells, channels), f32), flops=int(2e10))(
         columns_out[0], others[0], others[2]
     )
     mine, other = call(
         column_kernel,
         (shape((cells, channels), f32), shape((cells, channels), bf16)),
         scratch=[pltpu.VMEM((2, cells, channels), f32)],
-        flops=int(0),
+        flops=int(3e9),
     )(near, others[1])
     grad_features = call(join_kernel, shape((cells, channels), bf16))(mine, swap(other, "ylo"))
     grad_weight = call(
-        functools.partial(final_kernel, heights * 4),
+        functools.partial(final_kernel, heights * 8),
         shape((taps, quarter // heights, width), f32),
     )(parts)
     return (
@@ -333,8 +358,8 @@
 
 
 def solution(mesh):
-    fine = Mesh(mesh.devices.reshape(2, columns, 2, 16, 2), ("ylo", "x", "yhi", "z", "core"))
-    dp = ("yhi", "z", "core")
+    fine = Mesh(mesh.devices.reshape(2, columns, 2, 8, 2, 2), ("ylo", "x", "yhi", "z8", "zl", "core"))
+    dp = ("yhi", "z8", "zl", "core")
     placed = (
         P(BLK, dp, None, None, None),
         P(None, None, BLK),

time: 89.7 us -> 84.6 us (0.943)
  waiting for transfers between devices: 14.2 us -> 5.8 us
  starting transfers between devices: 34.1 us -> 36.9 us
    all_to_all x1 -> x2, starting transfers between devices: 15.2 us -> 23.1 us  [the longest x1 17.5 us: shards(): lax.all_to_all(sent.reshape(heights, quarter // heights, wide), FAR, 0, 0...]
    ppermute x3, waiting for transfers between devices: 7.01 us -> 0.01 us  [shards(): lax.ppermute(columns_out[d], 'x', [(i, i ^ d) for i in range(columns)])]
    ppermute x3 -> x2, starting transfers between devices: 8.77 us -> 4 us  [swap(): return lax.ppermute(values, axis, [(0, 1), (1, 0)])]
    ppermute x3 -> x2, waiting for transfers between devices: 5.98 us -> 4.77 us  [swap(): return lax.ppermute(values, axis, [(0, 1), (1, 0)])]
    concatenate x0 -> x1, other arithmetic: none -> 1.01 us  [shards(): jnp.concatenate([features.reshape(cells, channels), text.reshape(1, chann...]
    unnamed x6 -> x4, local copies, waits for them, and re-layouts: 0.91 us -> 0.01 us
    pallas_call x7 -> x6, Pallas kernels: 5.05 us -> 5.57 us  [the longest x1 2.39 us: shards(): call(keep_kernel, (shape((half, wide), f32),) + tuple((shape((2, cells, c...]
  transfers between devices with their start and end apart: 7 -> 7, of which waited for: 4 -> 2; matrix products, arithmetic and copies ran while one was open for 0% -> 0% of each run, Pallas kernels for 5% -> 5%
where the time goes in v4:
time: 84.6 us; the launch traced here: 83.1 us
  starting transfers between devices  36.9 us (44%)
  blocking collectives  28.8 us (34%)
  Pallas kernels  9.1 us (11%)
  waiting for transfers between devices  5.8 us (7%)
  between operations  1.43 us (2%)
  other arithmetic  1.01 us (1%)
    all_to_all x1, blocking collectives, shards(): group = lax.all_to_all(copies, BLK, 0, 0)  19.3 us
    all_to_all x1, starting transfers between devices, shards(): lax.all_to_all(sent.reshape(heights, quarter // heights, wide), FAR, 0, 0...  17.5 us
    ppermute x3, starting transfers between devices, shards(): lax.ppermute(columns_out[d], 'x', [(i, i ^ d) for i in range(columns)])  9.81 us
    all_to_all x1, blocking collectives, shards(): parts = lax.all_to_all(partial, BLK, 0, 0)  9.42 us
    all_to_all x1, starting transfers between devices, shards(): parts = lax.all_to_all(sent, NEAR, 0, 0)  5.58 us
    ppermute x2, waiting for transfers between devices, swap(): return lax.ppermute(values, axis, [(0, 1), (1, 0)])  4.77 us
    ppermute x2, starting transfers between devices, swap(): return lax.ppermute(values, axis, [(0, 1), (1, 0)])  4 us
    pallas_call x1, Pallas kernels, shards(): call(keep_kernel, (shape((half, wide), f32),) + tuple((shape((2, cells, c...  2.39 us
  transfers between devices with their start and end apart: 7, of which 2 were waited for; matrix products, arithmetic and copies ran while one was open for 0% of the time, Pallas kernels for 5%

profile of v4, /device:TPU:6, one launch (start us, length us, event | category | flops | bytes accessed | tf_op | source)
XLA Modules:
  0.0 83.1 jit_solution(12721374478376671592)
XLA Ops:
  1.3 0.1 pad.2.clone
  1.4 1.0 %maximum_maximum_fusion.own_ref = bf16[144,512]{1,0:T(8,128)(2,1)S(1)} fusion(bf16[1,512]{1,0:T(2,128)(2,1)} %bitcast.8, bf16[128,512]{1,0:T(8,128)(2,1)} %bitcast.6, bf16[144]{0:T(256)(128)(2,1)S(1)} %pad.2.clone), kind=kLoop, calls=%fused_computation | loop fusion | flops 442368 | bytes 279840 | tf_op jit(solution)/shard_map/concatenate | solution.py:278
  2.4 0.0 copy-start
  2.4 0.1 shard_map.76
  2.5 19.3 %all_to_all.20.group_ref = bf16[8,128,512]{2,1,0:T(8,128)(2,1)S(1)} all-to-all(bf16[8,128,512]{2,1,0:T(8,128)(2,1)S(1)} %get-tuple-element.18), channel_id=1, replica_groups=mesh['ylo'=2,'x'=4,'yhi'=2,'z8'=8,'zl'=2,'core'=2] {'ylo','x'}, dimensions={0} | all-to-all | bytes 2097152 | tf_op jit(solution)/shard_map/all_to_all | solution.py:288
  21.8 2.0 %shard_map.77 = (f32[1024,128]{1,0:T(8,128)S(1)}, bf16[2,256,1024]{2,1,0:T(8,128)(2,1)S(1)}, f32[8,8,640]{2,1,0:T(8,128)S(1)}) custom-call(bf16[8,128,512]{2,1,0:T(8,128)(2,1)S(1)} %all_to_all.20.group_ref, bf16[9,512,128]{2,1,0:T(8,128)(2,1)S(1)} %copy-done, bf16[128,512]{1,0:T(8,128)(2,1)S(1)} %copy-done.1, f32[8,128]{1,0:T(8,128)S(1)} %get-tuple-element.19.extra_ref), custom_call_target="tpu_custom_call" | custom-call | flops 1207959552 | tf_op jit(solution)/shard_map/pallas_call | solution.py:289
  23.8 9.4 %all_to_all.21.parts_ref = f32[8,8,640]{2,1,0:T(8,128)S(1)} all-to-all(f32[8,8,640]{2,1,0:T(8,128)S(1)} %get-tuple-element.21), channel_id=1, replica_groups=mesh['ylo'=2,'x'=4,'yhi'=2,'z8'=8,'zl'=2,'core'=2] {'ylo','x'}, dimensions={0} | all-to-all | bytes 327680 | tf_op jit(solution)/shard_map/all_to_all | solution.py:298
  33.3 1.5 %shard_map.78 = (f32[1,512]{1,0:T(1,128)}, bf16[1024,128]{1,0:T(8,128)(2,1)S(1)}, bf16[256,1152]{1,0:T(8,128)(2,1)S(1)}) custom-call(f32[8,8,640]{2,1,0:T(8,128)S(1)} %all_to_all.21.parts_ref, f32[1024,128]{1,0:T(8,128)S(1)} %get-tuple-element.22.slope_ref, bf16[128,512]{1,0:T(8,128)(2,1)S(1)} %copy-done.1, ...), custom_call_target="tpu_custom_call" | custom-call | flops 603979776 | tf_op jit(solution)/shard_map/pallas_call | solution.py:300
  34.8 1.9 %collective-permute-start.4 = (bf16[256,1152]{1,0:T(8,128)(2,1)S(1)}, bf16[256,1152]{1,0:T(8,128)(2,1)S(1)}, u32[]{:S(2)}, u32[]{:S(2)}) collective-permute-start(bf16[256,1152]{1,0:T(8,128)(2,1)S(1)} %get-tuple-element.31), channel_id=1, source_target_pairs={{0,1},{1,0},{2,3},{3,2},{4,5},{5,4},{6,7},{7,6},{8,9},{9,8},{10,11... | collective-permute-start | bytes 1769480 | tf_op jit(solution)/shard_map/ppermute | solution.py:268
  36.7 2.4 %shard_map.79 = (f32[256,1152]{1,0:T(8,128)S(1)}, bf16[2,128,512]{2,1,0:T(8,128)(2,1)S(1)}, bf16[2,128,512]{2,1,0:T(8,128)(2,1)S(1)}, bf16[2,128,512]{2,1,0:T(8,128)(2,1)S(1)}, bf16[2,128,512]{2,1,0:T(8,128)(2,1)S(1)}) custom-call(bf16[2,256,1024]{2,1,0:T(8,128)(2,1)S(1)} %get-tuple-element.20.turned_ref, bf16[1024,128]{1,0:T(8,128)(2,1)S(1)} %get-tuple-element.23.pre_ref, ...), custom_call_target="tpu_custom_call" | custom-call | flops 1811939328 | tf_op jit(solution)/shard_map/pallas_call | solution.py:310
  39.1 0.9 %shard_map.83 = bf16[4,64,1152]{2,1,0:T(8,128)(2,1)} custom-call(f32[256,1152]{1,0:T(8,128)S(1)} %get-tuple-element.30.kept_ref, bf16[256,1152]{1,0:T(8,128)(2,1)S(1)} %collective-permute-done.4.came_ref), custom_call_target="tpu_custom_call" | custom-call | tf_op jit(solution)/shard_map/pallas_call | solution.py:318
  40.0 5.6 %all-to-all-start.2 = ((bf16[4,64,1152]{2,1,0:T(8,128)(2,1)}), bf16[4,64,1152]{2,1,0:T(8,128)(2,1)S(1)}, u32[]{:S(2)}, u32[]{:S(2)}) async-start(bf16[4,64,1152]{2,1,0:T(8,128)(2,1)} %shard_map.83), calls=%async_computation.2 | async-start | bytes 1179648 | tf_op jit(solution)/shard_map/all_to_all | solution.py:324
  45.6 2.2 %collective-permute-start = (bf16[2,128,512]{2,1,0:T(8,128)(2,1)S(1)}, bf16[2,128,512]{2,1,0:T(8,128)(2,1)S(1)}, u32[]{:S(2)}, u32[]{:S(2)}) collective-permute-start(bf16[2,128,512]{2,1,0:T(8,128)(2,1)S(1)} %get-tuple-element.25), channel_id=1, source_target_pairs={{0,64},{64,0},{128,192},{192,128},{1,65},{65,1},{129,193},{193,129... | collective-permute-start | bytes 786440 | tf_op jit(solution)/shard_map/ppermute | solution.py:336
  47.8 4.4 %collective-permute-start.1 = (bf16[2,128,512]{2,1,0:T(8,128)(2,1)S(1)}, bf16[2,128,512]{2,1,0:T(8,128)(2,1)S(1)}, u32[]{:S(2)}, u32[]{:S(2)}) collective-permute-start(bf16[2,128,512]{2,1,0:T(8,128)(2,1)S(1)} %get-tuple-element.26), channel_id=1, source_target_pairs={{0,192},{64,128},{128,64},{192,0},{1,193},{65,129},{129,65},{193,1... | collective-permute-start | bytes 786440 | tf_op jit(solution)/shard_map/ppermute | solution.py:336
  52.2 3.2 %collective-permute-start.2 = (bf16[2,128,512]{2,1,0:T(8,128)(2,1)S(1)}, bf16[2,128,512]{2,1,0:T(8,128)(2,1)S(1)}, u32[]{:S(2)}, u32[]{:S(2)}) collective-permute-start(bf16[2,128,512]{2,1,0:T(8,128)(2,1)S(1)} %get-tuple-element.27), channel_id=1, source_target_pairs={{0,128},{64,192},{128,0},{192,64},{1,129},{65,193},{129,1},{193,65... | collective-permute-start | bytes 786440 | tf_op jit(solution)/shard_map/ppermute | solution.py:336
  55.4 1.0 %all-to-all-done.2.parts_ref = bf16[4,64,1152]{2,1,0:T(8,128)(2,1)S(1)} async-done(((bf16[4,64,1152]{2,1,0:T(8,128)(2,1)}), bf16[4,64,1152]{2,1,0:T(8,128)(2,1)S(1)}, u32[]{:S(2)}, u32[]{:S(2)}) %all-to-all-start.2) | async-done | bytes 589856 | tf_op jit(solution)/shard_map/all_to_all | solution.py:324
  56.4 0.7 shard_map.84
  57.2 17.5 %all-to-all-start.3 = ((bf16[8,8,1152]{2,1,0:T(8,128)(2,1)}), bf16[8,8,1152]{2,1,0:T(8,128)(2,1)S(1)}, u32[]{:S(2)}, u32[]{:S(2)}) async-start(bf16[8,8,1152]{2,1,0:T(8,128)(2,1)} %bitcast.4), calls=%async_computation.3 | async-start | bytes 294912 | tf_op jit(solution)/shard_map/all_to_all | solution.py:332
  74.7 0.1 shard_map.80.near_ref
  74.8 0.1 shard_map.81
  74.9 2.1 %collective-permute-start.3 = (bf16[128,512]{1,0:T(8,128)(2,1)S(1)}, bf16[128,512]{1,0:T(8,128)(2,1)S(1)}, u32[]{:S(2)}, u32[]{:S(2)}) collective-permute-start(bf16[128,512]{1,0:T(8,128)(2,1)S(1)} %get-tuple-element.29), channel_id=1, source_target_pairs={{0,256},{256,0},{1,257},{257,1},{2,258},{258,2},{3,259},{259,3},{4... | collective-permute-start | bytes 393224 | tf_op jit(solution)/shard_map/ppermute | solution.py:268
  77.0 4.8 %collective-permute-done.3.came_ref = bf16[128,512]{1,0:T(8,128)(2,1)S(1)} collective-permute-done((bf16[128,512]{1,0:T(8,128)(2,1)S(1)}, bf16[128,512]{1,0:T(8,128)(2,1)S(1)}, u32[]{:S(2)}, u32[]{:S(2)}) %collective-permute-start.3) | collective-permute-done | bytes 131104 | tf_op jit(solution)/shard_map/ppermute | solution.py:268
  81.7 0.7 shard_map.82
  82.4 0.6 shard_map.85
  (9 shorter events, 0.0 us)
Async XLA Ops:
  2.4 19.4 %copy-start = (bf16[9,512,128]{2,1,0:T(8,128)(2,1)S(1)}, bf16[9,512,128]{2,1,0:T(8,128)(2,1)}, u32[]{:S(2)}) copy-start(bf16[9,512,128]{2,1,0:T(8,128)(2,1)} %weight_ref.3) | copy-start | bytes 3538948
  2.4 19.4 %copy-start.1 = (bf16[128,512]{1,0:T(8,128)(2,1)S(1)}, bf16[128,512]{1,0:T(8,128)(2,1)}, u32[]{:S(2)}) copy-start(bf16[128,512]{1,0:T(8,128)(2,1)} %projection_ref.3) | copy-start | bytes 393220
  34.8 4.3 %collective-permute-start.4 = (bf16[256,1152]{1,0:T(8,128)(2,1)S(1)}, bf16[256,1152]{1,0:T(8,128)(2,1)S(1)}, u32[]{:S(2)}, u32[]{:S(2)}) collective-permute-start(bf16[256,1152]{1,0:T(8,128)(2,1)S(1)} %get-tuple-element.31), channel_id=1, source_target_pairs={{0,1},{1,0},{2,3},{3,2},{4,5},{5,4},{6,7},{7,6},{8,9},{9,8},{10,11... | collective-permute-start | bytes 1769480 | tf_op jit(solution)/shard_map/ppermute | solution.py:268
  40.0 16.4 %all-to-all-start.2 = ((bf16[4,64,1152]{2,1,0:T(8,128)(2,1)}), bf16[4,64,1152]{2,1,0:T(8,128)(2,1)S(1)}, u32[]{:S(2)}, u32[]{:S(2)}) async-start(bf16[4,64,1152]{2,1,0:T(8,128)(2,1)} %shard_map.83), calls=%async_computation.2 | async-start | bytes 1179648 | tf_op jit(solution)/shard_map/all_to_all | solution.py:324
  45.6 29.1 %collective-permute-start = (bf16[2,128,512]{2,1,0:T(8,128)(2,1)S(1)}, bf16[2,128,512]{2,1,0:T(8,128)(2,1)S(1)}, u32[]{:S(2)}, u32[]{:S(2)}) collective-permute-start(bf16[2,128,512]{2,1,0:T(8,128)(2,1)S(1)} %get-tuple-element.25), channel_id=1, source_target_pairs={{0,64},{64,0},{128,192},{192,128},{1,65},{65,1},{129,193},{193,129... | collective-permute-start | bytes 786440 | tf_op jit(solution)/shard_map/ppermute | solution.py:336
  47.8 26.9 %collective-permute-start.1 = (bf16[2,128,512]{2,1,0:T(8,128)(2,1)S(1)}, bf16[2,128,512]{2,1,0:T(8,128)(2,1)S(1)}, u32[]{:S(2)}, u32[]{:S(2)}) collective-permute-start(bf16[2,128,512]{2,1,0:T(8,128)(2,1)S(1)} %get-tuple-element.26), channel_id=1, source_target_pairs={{0,192},{64,128},{128,64},{192,0},{1,193},{65,129},{129,65},{193,1... | collective-permute-start | bytes 786440 | tf_op jit(solution)/shard_map/ppermute | solution.py:336
  52.2 22.5 %collective-permute-start.2 = (bf16[2,128,512]{2,1,0:T(8,128)(2,1)S(1)}, bf16[2,128,512]{2,1,0:T(8,128)(2,1)S(1)}, u32[]{:S(2)}, u32[]{:S(2)}) collective-permute-start(bf16[2,128,512]{2,1,0:T(8,128)(2,1)S(1)} %get-tuple-element.27), channel_id=1, source_target_pairs={{0,128},{64,192},{128,0},{192,64},{1,129},{65,193},{129,1},{193,65... | collective-permute-start | bytes 786440 | tf_op jit(solution)/shard_map/ppermute | solution.py:336
  57.2 25.3 %all-to-all-start.3 = ((bf16[8,8,1152]{2,1,0:T(8,128)(2,1)}), bf16[8,8,1152]{2,1,0:T(8,128)(2,1)S(1)}, u32[]{:S(2)}, u32[]{:S(2)}) async-start(bf16[8,8,1152]{2,1,0:T(8,128)(2,1)} %bitcast.4), calls=%async_computation.3 | async-start | bytes 294912 | tf_op jit(solution)/shard_map/all_to_all | solution.py:332
  74.9 6.9 %collective-permute-start.3 = (bf16[128,512]{1,0:T(8,128)(2,1)S(1)}, bf16[128,512]{1,0:T(8,128)(2,1)S(1)}, u32[]{:S(2)}, u32[]{:S(2)}) collective-permute-start(bf16[128,512]{1,0:T(8,128)(2,1)S(1)} %get-tuple-element.29), channel_id=1, source_target_pairs={{0,256},{256,0},{1,257},{257,1},{2,258},{258,2},{3,259},{259,3},{4... | collective-permute-start | bytes 393224 | tf_op jit(solution)/shard_map/ppermute | solution.py:268

commit v5 on v4

--- a/solution.py
+++ b/solution.py
@@ -89,13 +89,13 @@
                 low = (2 * yhi + zl) * block
                 turned_ref[core, low : low + block] = rows.astype(bf16)
     out_width = projection_ref.shape[0]
+    weight = jnp.concatenate([weight_ref[tap] for tap in range(weight_ref.shape[0])], axis=1)
+    products = jnp.dot(inputs, weight, preferred_element_type=f32)
     preact = None
     for a in range(3):
-        product = jnp.dot(
-            inputs,
-            jnp.concatenate([weight_ref[3 * a + b] for b in range(3)], axis=1),
-            preferred_element_type=f32,
-        ).reshape(clips, freq, frames, 3 * out_width)
+        product = products[:, 3 * a * out_width : 3 * (a + 1) * out_width].reshape(
+            clips, freq, frames, 3 * out_width
+        )
         low = product[..., :out_width]
         mid = product[..., out_width : 2 * out_width]
         high = product[..., 2 * out_width :]
@@ -253,15 +253,12 @@
     sent_ref[...] = total_ref[1 - side].astype(bf16)
 
 
-def join_kernel(mine_ref, came_ref, out_ref):
-    out_ref[...] = (mine_ref[...] + came_ref[...].astype(f32)).astype(bf16)
-
-
-def final_kernel(group_total, parts_ref, out_ref):
+def final_kernel(group_total, parts_ref, mine_ref, came_ref, weight_out_ref, feature_out_ref):
+    feature_out_ref[...] = (mine_ref[...] + came_ref[...].astype(f32)).astype(bf16)
     total = jnp.sum(parts_ref[...].astype(f32), axis=0) * (1.0 / group_total)
-    taps, _, width = out_ref.shape
+    taps, _, width = weight_out_ref.shape
     for tap in range(taps):
-        out_ref[tap] = total[:, tap * width : (tap + 1) * width]
+        weight_out_ref[tap] = total[:, tap * width : (tap + 1) * width]
 
 
 def swap(values, axis):
@@ -345,11 +342,10 @@
         scratch=[pltpu.VMEM((2, cells, channels), f32)],
         flops=int(3e9),
     )(near, others[1])
-    grad_features = call(join_kernel, shape((cells, channels), bf16))(mine, swap(other, "ylo"))
-    grad_weight = call(
-        functools.partial(final_kernel, heights * 8),
-        shape((taps, quarter // heights, width), f32),
-    )(parts)
+    grad_weight, grad_features = call(
+        functools.partial(final_kernel, 64),
+        (shape((taps, 8, width), f32), shape((cells, channels), bf16)),
+    )(parts, mine, swap(other, "ylo"))
     return (
         grad_features.reshape(features.shape),
         grad_weight,

time: 84.6 us -> 83.7 us (0.989)
  Pallas kernels: 9.1 us -> 8.24 us
  transfers between devices with their start and end apart: 7 -> 7, of which waited for: 2 -> 2; matrix products, arithmetic and copies ran while one was open for 0% -> 0% of each run, Pallas kernels for 5% -> 4%
where the time goes in v5:
time: 83.7 us; the launch traced here: 82.2 us
  starting transfers between devices  36.9 us (44%)
  blocking collectives  28.8 us (34%)
  Pallas kernels  8.24 us (10%)
  waiting for transfers between devices  5.8 us (7%)
  between operations  1.43 us (2%)
  other arithmetic  1.01 us (1%)
    all_to_all x1, blocking collectives, shards(): group = lax.all_to_all(copies, BLK, 0, 0)  19.3 us
    all_to_all x1, starting transfers between devices, shards(): lax.all_to_all(sent.reshape(heights, quarter // heights, wide), FAR, 0, 0...  17.5 us
    ppermute x3, starting transfers between devices, shards(): lax.ppermute(columns_out[d], 'x', [(i, i ^ d) for i in range(columns)])  9.81 us
    all_to_all x1, blocking collectives, shards(): parts = lax.all_to_all(partial, BLK, 0, 0)  9.42 us
    all_to_all x1, starting transfers between devices, shards(): parts = lax.all_to_all(sent, NEAR, 0, 0)  5.58 us
    ppermute x2, waiting for transfers between devices, swap(): return lax.ppermute(values, axis, [(0, 1), (1, 0)])  4.77 us
    ppermute x2, starting transfers between devices, swap(): return lax.ppermute(values, axis, [(0, 1), (1, 0)])  4 us
    pallas_call x1, Pallas kernels, shards(): call(keep_kernel, (shape((half, wide), f32),) + tuple((shape((2, cells, c...  2.39 us
  transfers between devices with their start and end apart: 7, of which 2 were waited for; matrix products, arithmetic and copies ran while one was open for 0% of the time, Pallas kernels for 4%

profile of v5, /device:TPU:6, one launch (start us, length us, event | category | flops | bytes accessed | tf_op | source)
XLA Modules:
  0.0 82.2 jit_solution(6763466675635624862)
XLA Ops:
  1.3 0.1 pad.2.clone
  1.4 1.0 %maximum_maximum_fusion.own_ref = bf16[144,512]{1,0:T(8,128)(2,1)S(1)} fusion(bf16[1,512]{1,0:T(2,128)(2,1)} %bitcast.7, bf16[128,512]{1,0:T(8,128)(2,1)} %bitcast.6, bf16[144]{0:T(256)(128)(2,1)S(1)} %pad.2.clone), kind=kLoop, calls=%fused_computation | loop fusion | flops 442368 | bytes 279840 | tf_op jit(solution)/shard_map/concatenate | solution.py:275
  2.4 0.0 copy-start
  2.4 0.0 copy-start.1
  2.4 0.1 shard_map.76
  2.5 19.3 %all_to_all.20.group_ref = bf16[8,128,512]{2,1,0:T(8,128)(2,1)S(1)} all-to-all(bf16[8,128,512]{2,1,0:T(8,128)(2,1)S(1)} %get-tuple-element.20), channel_id=1, replica_groups=mesh['ylo'=2,'x'=4,'yhi'=2,'z8'=8,'zl'=2,'core'=2] {'ylo','x'}, dimensions={0} | all-to-all | bytes 2097152 | tf_op jit(solution)/shard_map/all_to_all | solution.py:285
  21.8 1.8 %shard_map.77 = (f32[1024,128]{1,0:T(8,128)S(1)}, bf16[2,256,1024]{2,1,0:T(8,128)(2,1)S(1)}, f32[8,8,640]{2,1,0:T(8,128)S(1)}) custom-call(bf16[8,128,512]{2,1,0:T(8,128)(2,1)S(1)} %all_to_all.20.group_ref, bf16[9,512,128]{2,1,0:T(8,128)(2,1)S(1)} %copy-done, bf16[128,512]{1,0:T(8,128)(2,1)S(1)} %copy-done.1, f32[8,128]{1,0:T(8,128)S(1)} %get-tuple-element.21.extra_ref), custom_call_target="tpu_custom_call" | custom-call | flops 1207959552 | tf_op jit(solution)/shard_map/pallas_call | solution.py:286
  23.6 9.4 %all_to_all.21.parts_ref = f32[8,8,640]{2,1,0:T(8,128)S(1)} all-to-all(f32[8,8,640]{2,1,0:T(8,128)S(1)} %get-tuple-element.23), channel_id=1, replica_groups=mesh['ylo'=2,'x'=4,'yhi'=2,'z8'=8,'zl'=2,'core'=2] {'ylo','x'}, dimensions={0} | all-to-all | bytes 327680 | tf_op jit(solution)/shard_map/all_to_all | solution.py:295
  33.0 1.5 %shard_map.78 = (f32[1,512]{1,0:T(1,128)}, bf16[1024,128]{1,0:T(8,128)(2,1)S(1)}, bf16[256,1152]{1,0:T(8,128)(2,1)S(1)}) custom-call(f32[8,8,640]{2,1,0:T(8,128)S(1)} %all_to_all.21.parts_ref, f32[1024,128]{1,0:T(8,128)S(1)} %get-tuple-element.24.slope_ref, bf16[128,512]{1,0:T(8,128)(2,1)S(1)} %copy-done.1, ...), custom_call_target="tpu_custom_call" | custom-call | flops 603979776 | tf_op jit(solution)/shard_map/pallas_call | solution.py:297
  34.5 1.9 %collective-permute-start = (bf16[256,1152]{1,0:T(8,128)(2,1)S(1)}, bf16[256,1152]{1,0:T(8,128)(2,1)S(1)}, u32[]{:S(2)}, u32[]{:S(2)}) collective-permute-start(bf16[256,1152]{1,0:T(8,128)(2,1)S(1)} %get-tuple-element.27), channel_id=1, source_target_pairs={{0,1},{1,0},{2,3},{3,2},{4,5},{5,4},{6,7},{7,6},{8,9},{9,8},{10,11... | collective-permute-start | bytes 1769480 | tf_op jit(solution)/shard_map/ppermute | solution.py:265
  36.5 2.4 %shard_map.79 = (f32[256,1152]{1,0:T(8,128)S(1)}, bf16[2,128,512]{2,1,0:T(8,128)(2,1)S(1)}, bf16[2,128,512]{2,1,0:T(8,128)(2,1)S(1)}, bf16[2,128,512]{2,1,0:T(8,128)(2,1)S(1)}, bf16[2,128,512]{2,1,0:T(8,128)(2,1)S(1)}) custom-call(bf16[2,256,1024]{2,1,0:T(8,128)(2,1)S(1)} %get-tuple-element.22.turned_ref, bf16[1024,128]{1,0:T(8,128)(2,1)S(1)} %get-tuple-element.25.pre_ref, ...), custom_call_target="tpu_custom_call" | custom-call | flops 1811939328 | tf_op jit(solution)/shard_map/pallas_call | solution.py:307
  38.9 0.9 %shard_map.80 = bf16[4,64,1152]{2,1,0:T(8,128)(2,1)} custom-call(f32[256,1152]{1,0:T(8,128)S(1)} %get-tuple-element.26.kept_ref, bf16[256,1152]{1,0:T(8,128)(2,1)S(1)} %collective-permute-done.came_ref), custom_call_target="tpu_custom_call" | custom-call | tf_op jit(solution)/shard_map/pallas_call | solution.py:315
  39.8 5.6 %all-to-all-start.2 = ((bf16[4,64,1152]{2,1,0:T(8,128)(2,1)}), bf16[4,64,1152]{2,1,0:T(8,128)(2,1)S(1)}, u32[]{:S(2)}, u32[]{:S(2)}) async-start(bf16[4,64,1152]{2,1,0:T(8,128)(2,1)} %shard_map.80), calls=%async_computation.2 | async-start | bytes 1179648 | tf_op jit(solution)/shard_map/all_to_all | solution.py:321
  45.3 2.2 %collective-permute-start.1 = (bf16[2,128,512]{2,1,0:T(8,128)(2,1)S(1)}, bf16[2,128,512]{2,1,0:T(8,128)(2,1)S(1)}, u32[]{:S(2)}, u32[]{:S(2)}) collective-permute-start(bf16[2,128,512]{2,1,0:T(8,128)(2,1)S(1)} %get-tuple-element.29), channel_id=1, source_target_pairs={{0,64},{64,0},{128,192},{192,128},{1,65},{65,1},{129,193},{193,129... | collective-permute-start | bytes 786440 | tf_op jit(solution)/shard_map/ppermute | solution.py:333
  47.6 4.4 %collective-permute-start.2 = (bf16[2,128,512]{2,1,0:T(8,128)(2,1)S(1)}, bf16[2,128,512]{2,1,0:T(8,128)(2,1)S(1)}, u32[]{:S(2)}, u32[]{:S(2)}) collective-permute-start(bf16[2,128,512]{2,1,0:T(8,128)(2,1)S(1)} %get-tuple-element.30), channel_id=1, source_target_pairs={{0,192},{64,128},{128,64},{192,0},{1,193},{65,129},{129,65},{193,1... | collective-permute-start | bytes 786440 | tf_op jit(solution)/shard_map/ppermute | solution.py:333
  52.0 3.2 %collective-permute-start.3 = (bf16[2,128,512]{2,1,0:T(8,128)(2,1)S(1)}, bf16[2,128,512]{2,1,0:T(8,128)(2,1)S(1)}, u32[]{:S(2)}, u32[]{:S(2)}) collective-permute-start(bf16[2,128,512]{2,1,0:T(8,128)(2,1)S(1)} %get-tuple-element.31), channel_id=1, source_target_pairs={{0,128},{64,192},{128,0},{192,64},{1,129},{65,193},{129,1},{193,65... | collective-permute-start | bytes 786440 | tf_op jit(solution)/shard_map/ppermute | solution.py:333
  55.2 1.0 %all-to-all-done.2.parts_ref = bf16[4,64,1152]{2,1,0:T(8,128)(2,1)S(1)} async-done(((bf16[4,64,1152]{2,1,0:T(8,128)(2,1)}), bf16[4,64,1152]{2,1,0:T(8,128)(2,1)S(1)}, u32[]{:S(2)}, u32[]{:S(2)}) %all-to-all-start.2) | async-done | bytes 589856 | tf_op jit(solution)/shard_map/all_to_all | solution.py:321
  56.2 0.7 shard_map.81
  56.9 17.5 %all-to-all-start.3 = ((bf16[8,8,1152]{2,1,0:T(8,128)(2,1)}), bf16[8,8,1152]{2,1,0:T(8,128)(2,1)S(1)}, u32[]{:S(2)}, u32[]{:S(2)}) async-start(bf16[8,8,1152]{2,1,0:T(8,128)(2,1)} %bitcast.3), calls=%async_computation.3 | async-start | bytes 294912 | tf_op jit(solution)/shard_map/all_to_all | solution.py:329
  74.4 0.1 shard_map.82.near_ref
  74.5 0.1 shard_map.83
  74.7 2.1 %collective-permute-start.4 = (bf16[128,512]{1,0:T(8,128)(2,1)S(1)}, bf16[128,512]{1,0:T(8,128)(2,1)S(1)}, u32[]{:S(2)}, u32[]{:S(2)}) collective-permute-start(bf16[128,512]{1,0:T(8,128)(2,1)S(1)} %get-tuple-element.33), channel_id=1, source_target_pairs={{0,256},{256,0},{1,257},{257,1},{2,258},{258,2},{3,259},{259,3},{4... | collective-permute-start | bytes 393224 | tf_op jit(solution)/shard_map/ppermute | solution.py:265
  76.7 4.8 %collective-permute-done.4.came_ref = bf16[128,512]{1,0:T(8,128)(2,1)S(1)} collective-permute-done((bf16[128,512]{1,0:T(8,128)(2,1)S(1)}, bf16[128,512]{1,0:T(8,128)(2,1)S(1)}, u32[]{:S(2)}, u32[]{:S(2)}) %collective-permute-start.4) | collective-permute-done | bytes 131104 | tf_op jit(solution)/shard_map/ppermute | solution.py:265
  81.5 0.7 shard_map.84
  (8 shorter events, 0.0 us)
Async XLA Ops:
  2.4 19.4 %copy-start = (bf16[9,512,128]{2,1,0:T(8,128)(2,1)S(1)}, bf16[9,512,128]{2,1,0:T(8,128)(2,1)}, u32[]{:S(2)}) copy-start(bf16[9,512,128]{2,1,0:T(8,128)(2,1)} %weight_ref.3) | copy-start | bytes 3538948
  2.4 19.4 %copy-start.1 = (bf16[128,512]{1,0:T(8,128)(2,1)S(1)}, bf16[128,512]{1,0:T(8,128)(2,1)}, u32[]{:S(2)}) copy-start(bf16[128,512]{1,0:T(8,128)(2,1)} %projection_ref.3) | copy-start | bytes 393220
  34.5 4.3 %collective-permute-start = (bf16[256,1152]{1,0:T(8,128)(2,1)S(1)}, bf16[256,1152]{1,0:T(8,128)(2,1)S(1)}, u32[]{:S(2)}, u32[]{:S(2)}) collective-permute-start(bf16[256,1152]{1,0:T(8,128)(2,1)S(1)} %get-tuple-element.27), channel_id=1, source_target_pairs={{0,1},{1,0},{2,3},{3,2},{4,5},{5,4},{6,7},{7,6},{8,9},{9,8},{10,11... | collective-permute-start | bytes 1769480 | tf_op jit(solution)/shard_map/ppermute | solution.py:265
  39.8 16.4 %all-to-all-start.2 = ((bf16[4,64,1152]{2,1,0:T(8,128)(2,1)}), bf16[4,64,1152]{2,1,0:T(8,128)(2,1)S(1)}, u32[]{:S(2)}, u32[]{:S(2)}) async-start(bf16[4,64,1152]{2,1,0:T(8,128)(2,1)} %shard_map.80), calls=%async_computation.2 | async-start | bytes 1179648 | tf_op jit(solution)/shard_map/all_to_all | solution.py:321
  45.3 29.1 %collective-permute-start.1 = (bf16[2,128,512]{2,1,0:T(8,128)(2,1)S(1)}, bf16[2,128,512]{2,1,0:T(8,128)(2,1)S(1)}, u32[]{:S(2)}, u32[]{:S(2)}) collective-permute-start(bf16[2,128,512]{2,1,0:T(8,128)(2,1)S(1)} %get-tuple-element.29), channel_id=1, source_target_pairs={{0,64},{64,0},{128,192},{192,128},{1,65},{65,1},{129,193},{193,129... | collective-permute-start | bytes 786440 | tf_op jit(solution)/shard_map/ppermute | solution.py:333
  47.6 26.9 %collective-permute-start.2 = (bf16[2,128,512]{2,1,0:T(8,128)(2,1)S(1)}, bf16[2,128,512]{2,1,0:T(8,128)(2,1)S(1)}, u32[]{:S(2)}, u32[]{:S(2)}) collective-permute-start(bf16[2,128,512]{2,1,0:T(8,128)(2,1)S(1)} %get-tuple-element.30), channel_id=1, source_target_pairs={{0,192},{64,128},{128,64},{192,0},{1,193},{65,129},{129,65},{193,1... | collective-permute-start | bytes 786440 | tf_op jit(solution)/shard_map/ppermute | solution.py:333
  52.0 22.5 %collective-permute-start.3 = (bf16[2,128,512]{2,1,0:T(8,128)(2,1)S(1)}, bf16[2,128,512]{2,1,0:T(8,128)(2,1)S(1)}, u32[]{:S(2)}, u32[]{:S(2)}) collective-permute-start(bf16[2,128,512]{2,1,0:T(8,128)(2,1)S(1)} %get-tuple-element.31), channel_id=1, source_target_pairs={{0,128},{64,192},{128,0},{192,64},{1,129},{65,193},{129,1},{193,65... | collective-permute-start | bytes 786440 | tf_op jit(solution)/shard_map/ppermute | solution.py:333
  56.9 24.6 %all-to-all-start.3 = ((bf16[8,8,1152]{2,1,0:T(8,128)(2,1)}), bf16[8,8,1152]{2,1,0:T(8,128)(2,1)S(1)}, u32[]{:S(2)}, u32[]{:S(2)}) async-start(bf16[8,8,1152]{2,1,0:T(8,128)(2,1)} %bitcast.3), calls=%async_computation.3 | async-start | bytes 294912 | tf_op jit(solution)/shard_map/all_to_all | solution.py:329
  74.7 6.9 %collective-permute-start.4 = (bf16[128,512]{1,0:T(8,128)(2,1)S(1)}, bf16[128,512]{1,0:T(8,128)(2,1)S(1)}, u32[]{:S(2)}, u32[]{:S(2)}) collective-permute-start(bf16[128,512]{1,0:T(8,128)(2,1)S(1)} %get-tuple-element.33), channel_id=1, source_target_pairs={{0,256},{256,0},{1,257},{257,1},{2,258},{258,2},{3,259},{259,3},{4... | collective-permute-start | bytes 393224 | tf_op jit(solution)/shard_map/ppermute | solution.py:265

commit v6 on v5

--- a/solution.py
+++ b/solution.py
@@ -12,7 +12,7 @@
 loss_scale = 1024.0
 norm_eps = 1e-06
 
-BLK = ("ylo", "x")
+BLK = "blk"
 NEAR = ("yhi", "zl")
 FAR = "z8"
 f32 = jnp.float32
@@ -23,9 +23,10 @@
 frames = 32
 cells = freq * frames
 columns = 4
+last_member = clips - 1
+blk_order = [last_member - p for p in range(clips)]
 heights = 8
-first_far = 4
-far_order = [(first_far + p) % heights for p in range(heights)]
+far_order = [5, 4, 3, 6, 2, 7, 1, 0]
 vmem_limit = 40 * 1024 * 1024
 HBM = pl.BlockSpec(memory_space=pltpu.HBM)
 VMEM = pl.BlockSpec(memory_space=pltpu.VMEM)
@@ -80,7 +81,7 @@
 ):
     inputs = group_ref[...].reshape(clips * cells, -1)
     turned = inputs.T.astype(f32).reshape(2, heights, 2, 2, 8, clips * cells)
-    turned = jnp.concatenate([turned[:, first_far:], turned[:, :first_far]], axis=1)
+    turned = jnp.concatenate([turned[:, z : z + 1] for z in far_order], axis=1)
     block = heights * 8
     for core in range(2):
         for yhi in range(2):
@@ -173,7 +174,8 @@
     clip_labels = jnp.concatenate(
         [parts_ref[c, clips - 1 :, embed : embed + 1] for c in range(clips)], axis=0
     ).astype(jnp.int32)
-    position = lax.axis_index("ylo") * columns + lax.axis_index("x")
+    member = lax.axis_index(BLK)
+    place = last_member - member
 
     def caption_at(index):
         text_values = jnp.concatenate(
@@ -185,10 +187,12 @@
     audio_grad = jnp.zeros_like(audio_unit)
     for j in range(clips):
         caption, _ = caption_at(j)
-        audio_grad = audio_grad + pair_column(audio_unit, caption, clip_labels, j) * caption
+        audio_grad = (
+            audio_grad + pair_column(audio_unit, caption, clip_labels, last_member - j) * caption
+        )
     audio_grad = logit_scale * audio_grad
-    caption, inv_text = caption_at(position)
-    own_pairs = pair_column(audio_unit, caption, clip_labels, position)
+    caption, inv_text = caption_at(place)
+    own_pairs = pair_column(audio_unit, caption, clip_labels, member)
     caption_grad = logit_scale * jnp.sum(own_pairs * audio_unit, axis=0, keepdims=True)
     text_ref[...] = (caption_grad - caption * row_sum(caption * caption_grad)) * inv_text
     embedding_grad = (
@@ -216,9 +220,9 @@
         shifted, weight, (((1,), (1,)), ((), ())), preferred_element_type=f32
     )
     total_ref[...] = result.astype(bf16).reshape(total_ref.shape)
-    here = lax.axis_index("x")
+    here = lax.axis_index(BLK) % columns
     for d in range(columns):
-        out_refs[d][...] = total_ref[:, here ^ d]
+        out_refs[d][...] = total_ref[:, (columns - 1 - here) ^ d]
 
 
 def pair_sum_kernel(kept_ref, came_ref, sent_ref, sent_buf, sems):
@@ -248,7 +252,7 @@
 
 def column_kernel(near_ref, c_ref, mine_ref, sent_ref, total_ref):
     total_ref[...] = near_ref[...] + c_ref[...].astype(f32)
-    side = lax.axis_index("ylo")
+    side = 1 - lax.axis_index(BLK) // columns
     mine_ref[...] = total_ref[side]
     sent_ref[...] = total_ref[1 - side].astype(bf16)
 
@@ -282,7 +286,7 @@
     copies, extra = call(
         copy_kernel, (shape((clips, cells, channels), bf16), shape((clips, 128), f32))
     )(own)
-    group = lax.all_to_all(copies, BLK, 0, 0)
+    group = lax.all_to_all(copies, BLK, 0, 0, axis_index_groups=[blk_order])
     slope, turned, partial = call(
         forward_kernel,
         (
@@ -292,7 +296,7 @@
         ),
         flops=matmul,
     )(group, conv_weight, projection, extra)
-    parts = lax.all_to_all(partial, BLK, 0, 0)
+    parts = lax.all_to_all(partial, BLK, 0, 0, axis_index_groups=[blk_order])
     shifted_buf = pltpu.VMEM((clips, freq, frames, wide), bf16)
     grad_text, pre, sent = call(
         pair_kernel,
@@ -330,7 +334,7 @@
         sent.reshape(heights, quarter // heights, wide), FAR, 0, 0, axis_index_groups=[far_order]
     )
     others = [
-        lax.ppermute(columns_out[d], "x", [(i, i ^ d) for i in range(columns)])
+        lax.ppermute(columns_out[d], BLK, [(i, i ^ d) for i in range(clips)])
         for d in range(1, columns)
     ]
     near = call(near_kernel, shape((2, cells, channels), f32), flops=int(2e10))(
@@ -345,7 +349,7 @@
     grad_weight, grad_features = call(
         functools.partial(final_kernel, 64),
         (shape((taps, 8, width), f32), shape((cells, channels), bf16)),
-    )(parts, mine, swap(other, "ylo"))
+    )(parts, mine, lax.ppermute(other, BLK, [(i, i ^ columns) for i in range(clips)]))
     return (
         grad_features.reshape(features.shape),
         grad_weight,
@@ -354,7 +358,7 @@
 
 
 def solution(mesh):
-    fine = Mesh(mesh.devices.reshape(2, columns, 2, 8, 2, 2), ("ylo", "x", "yhi", "z8", "zl", "core"))
+    fine = Mesh(mesh.devices.reshape(clips, 2, 8, 2, 2), ("blk", "yhi", "z8", "zl", "core"))
     dp = ("yhi", "z8", "zl", "core")
     placed = (
         P(BLK, dp, None, None, None),

time: 83.7 us -> 81.4 us (0.973)
  starting transfers between devices: 36.9 us -> 35.8 us
  blocking collectives: 28.8 us -> 27.9 us
    ppermute x2 -> x1, waiting for transfers between devices: 4.77 us -> 0.01 us  [swap(): return lax.ppermute(values, axis, [(0, 1), (1, 0)])]
    ppermute x3 -> x4, waiting for transfers between devices: 0.01 us -> 4.09 us  [the longest x1 4.09 us: shards(): lax.ppermute(other, BLK, [(i, i ^ columns) for i in range(clips)])]
    ppermute x3 -> x4, starting transfers between devices: 9.81 us -> 12.6 us  [the longest x3 9.81 us: shards(): lax.ppermute(columns_out[d], BLK, [(i, i ^ d) for i in range(clips)])]
    ppermute x2 -> x1, starting transfers between devices: 4 us -> 1.92 us  [swap(): return lax.ppermute(values, axis, [(0, 1), (1, 0)])]
    all_to_all x1, starting transfers between devices: 17.5 us -> 15.7 us  [shards(): lax.all_to_all(sent.reshape(heights, quarter // heights, wide), FAR, 0, 0...]
  transfers between devices with their start and end apart: 7 -> 7, of which waited for: 2 -> 3; matrix products, arithmetic and copies ran while one was open for 0% -> 0% of each run, Pallas kernels for 4% -> 4%
where the time goes in v6:
time: 81.4 us; the launch traced here: 80.1 us
  starting transfers between devices  35.8 us (44%)
  blocking collectives  27.9 us (34%)
  Pallas kernels  8.21 us (10%)
  waiting for transfers between devices  5.61 us (7%)
  between operations  1.43 us (2%)
  other arithmetic  1.01 us (1%)
    all_to_all x1, blocking collectives, shards(): group = lax.all_to_all(copies, BLK, 0, 0, axis_index_groups=[blk_order])  18.6 us
    all_to_all x1, starting transfers between devices, shards(): lax.all_to_all(sent.reshape(heights, quarter // heights, wide), FAR, 0, 0...  15.7 us
    ppermute x3, starting transfers between devices, shards(): lax.ppermute(columns_out[d], BLK, [(i, i ^ d) for i in range(clips)])  9.81 us
    all_to_all x1, blocking collectives, shards(): parts = lax.all_to_all(partial, BLK, 0, 0, axis_index_groups=[blk_order])  9.29 us
    all_to_all x1, starting transfers between devices, shards(): parts = lax.all_to_all(sent, NEAR, 0, 0)  5.63 us
    ppermute x1, waiting for transfers between devices, shards(): lax.ppermute(other, BLK, [(i, i ^ columns) for i in range(clips)])  4.09 us
    ppermute x1, starting transfers between devices, shards(): lax.ppermute(other, BLK, [(i, i ^ columns) for i in range(clips)])  2.77 us
    pallas_call x1, Pallas kernels, shards(): call(keep_kernel, (shape((half, wide), f32),) + tuple((shape((2, cells, c...  2.37 us
  transfers between devices with their start and end apart: 7, of which 3 were waited for; matrix products, arithmetic and copies ran while one was open for 0% of the time, Pallas kernels for 4%

profile of v6, /device:TPU:6, one launch (start us, length us, event | category | flops | bytes accessed | tf_op | source)
XLA Modules:
  0.0 80.1 jit_solution(10482053156065924862)
XLA Ops:
  1.3 0.1 pad.2.clone
  1.4 1.0 %maximum_maximum_fusion.own_ref = bf16[144,512]{1,0:T(8,128)(2,1)S(1)} fusion(bf16[1,512]{1,0:T(2,128)(2,1)} %bitcast.7, bf16[128,512]{1,0:T(8,128)(2,1)} %bitcast.6, bf16[144]{0:T(256)(128)(2,1)S(1)} %pad.2.clone), kind=kLoop, calls=%fused_computation | loop fusion | flops 442368 | bytes 279840 | tf_op jit(solution)/shard_map/concatenate | solution.py:279
  2.4 0.0 copy-start
  2.4 0.1 shard_map.76
  2.5 18.6 %all_to_all.20.group_ref = bf16[8,128,512]{2,1,0:T(8,128)(2,1)S(1)} all-to-all(bf16[8,128,512]{2,1,0:T(8,128)(2,1)S(1)} %get-tuple-element.20), channel_id=1, replica_groups={{448,384,320,256,192,128,64,0},{449,385,321,257,193,129,65,1},{450,386,..., dimensions={0} | all-to-all | bytes 2097152 | tf_op jit(solution)/shard_map/all_to_all | solution.py:289
  21.1 1.8 %shard_map.77 = (f32[1024,128]{1,0:T(8,128)S(1)}, bf16[2,256,1024]{2,1,0:T(8,128)(2,1)S(1)}, f32[8,8,640]{2,1,0:T(8,128)S(1)}) custom-call(bf16[8,128,512]{2,1,0:T(8,128)(2,1)S(1)} %all_to_all.20.group_ref, bf16[9,512,128]{2,1,0:T(8,128)(2,1)S(1)} %copy-done, bf16[128,512]{1,0:T(8,128)(2,1)S(1)} %copy-done.1, f32[8,128]{1,0:T(8,128)S(1)} %get-tuple-element.21.extra_ref), custom_call_target="tpu_custom_call" | custom-call | flops 1207959552 | tf_op jit(solution)/shard_map/pallas_call | solution.py:290
  22.9 9.3 %all_to_all.21.parts_ref = f32[8,8,640]{2,1,0:T(8,128)S(1)} all-to-all(f32[8,8,640]{2,1,0:T(8,128)S(1)} %get-tuple-element.23), channel_id=1, replica_groups={{448,384,320,256,192,128,64,0},{449,385,321,257,193,129,65,1},{450,386,..., dimensions={0} | all-to-all | bytes 327680 | tf_op jit(solution)/shard_map/all_to_all | solution.py:299
  32.2 1.5 %shard_map.78 = (f32[1,512]{1,0:T(1,128)}, bf16[1024,128]{1,0:T(8,128)(2,1)S(1)}, bf16[256,1152]{1,0:T(8,128)(2,1)S(1)}) custom-call(f32[8,8,640]{2,1,0:T(8,128)S(1)} %all_to_all.21.parts_ref, f32[1024,128]{1,0:T(8,128)S(1)} %get-tuple-element.24.slope_ref, bf16[128,512]{1,0:T(8,128)(2,1)S(1)} %copy-done.1, ...), custom_call_target="tpu_custom_call" | custom-call | flops 603979776 | tf_op jit(solution)/shard_map/pallas_call | solution.py:301
  33.7 1.9 %collective-permute-start = (bf16[256,1152]{1,0:T(8,128)(2,1)S(1)}, bf16[256,1152]{1,0:T(8,128)(2,1)S(1)}, u32[]{:S(2)}, u32[]{:S(2)}) collective-permute-start(bf16[256,1152]{1,0:T(8,128)(2,1)S(1)} %get-tuple-element.27), channel_id=1, source_target_pairs={{0,1},{1,0},{2,3},{3,2},{4,5},{5,4},{6,7},{7,6},{8,9},{9,8},{10,11... | collective-permute-start | bytes 1769480 | tf_op jit(solution)/shard_map/ppermute | solution.py:269
  35.6 2.4 %shard_map.79 = (f32[256,1152]{1,0:T(8,128)S(1)}, bf16[2,128,512]{2,1,0:T(8,128)(2,1)S(1)}, bf16[2,128,512]{2,1,0:T(8,128)(2,1)S(1)}, bf16[2,128,512]{2,1,0:T(8,128)(2,1)S(1)}, bf16[2,128,512]{2,1,0:T(8,128)(2,1)S(1)}) custom-call(bf16[2,256,1024]{2,1,0:T(8,128)(2,1)S(1)} %get-tuple-element.22.turned_ref, bf16[1024,128]{1,0:T(8,128)(2,1)S(1)} %get-tuple-element.25.pre_ref, ...), custom_call_target="tpu_custom_call" | custom-call | flops 1811939328 | tf_op jit(solution)/shard_map/pallas_call | solution.py:311
  38.0 0.9 %shard_map.80 = bf16[4,64,1152]{2,1,0:T(8,128)(2,1)} custom-call(f32[256,1152]{1,0:T(8,128)S(1)} %get-tuple-element.26.kept_ref, bf16[256,1152]{1,0:T(8,128)(2,1)S(1)} %collective-permute-done.came_ref), custom_call_target="tpu_custom_call" | custom-call | tf_op jit(solution)/shard_map/pallas_call | solution.py:319
  38.9 5.6 %all-to-all-start.2 = ((bf16[4,64,1152]{2,1,0:T(8,128)(2,1)}), bf16[4,64,1152]{2,1,0:T(8,128)(2,1)S(1)}, u32[]{:S(2)}, u32[]{:S(2)}) async-start(bf16[4,64,1152]{2,1,0:T(8,128)(2,1)} %shard_map.80), calls=%async_computation.2 | async-start | bytes 1179648 | tf_op jit(solution)/shard_map/all_to_all | solution.py:325
  44.5 2.8 %collective-permute-start.1 = (bf16[2,128,512]{2,1,0:T(8,128)(2,1)S(1)}, bf16[2,128,512]{2,1,0:T(8,128)(2,1)S(1)}, u32[]{:S(2)}, u32[]{:S(2)}) collective-permute-start(bf16[2,128,512]{2,1,0:T(8,128)(2,1)S(1)} %get-tuple-element.29), channel_id=1, source_target_pairs={{0,64},{64,0},{128,192},{192,128},{256,320},{320,256},{384,448},{4... | collective-permute-start | bytes 786440 | tf_op jit(solution)/shard_map/ppermute | solution.py:337
  47.3 2.6 %collective-permute-start.2 = (bf16[2,128,512]{2,1,0:T(8,128)(2,1)S(1)}, bf16[2,128,512]{2,1,0:T(8,128)(2,1)S(1)}, u32[]{:S(2)}, u32[]{:S(2)}) collective-permute-start(bf16[2,128,512]{2,1,0:T(8,128)(2,1)S(1)} %get-tuple-element.30), channel_id=1, source_target_pairs={{0,192},{64,128},{128,64},{192,0},{256,448},{320,384},{384,320},{4... | collective-permute-start | bytes 786440 | tf_op jit(solution)/shard_map/ppermute | solution.py:337
  50.0 4.4 %collective-permute-start.3 = (bf16[2,128,512]{2,1,0:T(8,128)(2,1)S(1)}, bf16[2,128,512]{2,1,0:T(8,128)(2,1)S(1)}, u32[]{:S(2)}, u32[]{:S(2)}) collective-permute-start(bf16[2,128,512]{2,1,0:T(8,128)(2,1)S(1)} %get-tuple-element.31), channel_id=1, source_target_pairs={{0,128},{64,192},{128,0},{192,64},{256,384},{320,448},{384,256},{4... | collective-permute-start | bytes 786440 | tf_op jit(solution)/shard_map/ppermute | solution.py:337
  54.4 1.0 %all-to-all-done.2.parts_ref = bf16[4,64,1152]{2,1,0:T(8,128)(2,1)S(1)} async-done(((bf16[4,64,1152]{2,1,0:T(8,128)(2,1)}), bf16[4,64,1152]{2,1,0:T(8,128)(2,1)S(1)}, u32[]{:S(2)}, u32[]{:S(2)}) %all-to-all-start.2) | async-done | bytes 589856 | tf_op jit(solution)/shard_map/all_to_all | solution.py:325
  55.4 0.7 shard_map.81
  56.1 15.7 %all-to-all-start.3 = ((bf16[8,8,1152]{2,1,0:T(8,128)(2,1)}), bf16[8,8,1152]{2,1,0:T(8,128)(2,1)S(1)}, u32[]{:S(2)}, u32[]{:S(2)}) async-start(bf16[8,8,1152]{2,1,0:T(8,128)(2,1)} %bitcast.3), calls=%async_computation.3 | async-start | bytes 294912 | tf_op jit(solution)/shard_map/all_to_all | solution.py:333
  71.8 0.1 shard_map.82.near_ref
  72.0 0.1 shard_map.83
  72.0 2.8 %collective-permute-start.4 = (bf16[128,512]{1,0:T(8,128)(2,1)S(1)}, bf16[128,512]{1,0:T(8,128)(2,1)S(1)}, u32[]{:S(2)}, u32[]{:S(2)}) collective-permute-start(bf16[128,512]{1,0:T(8,128)(2,1)S(1)} %get-tuple-element.33), channel_id=1, source_target_pairs={{0,256},{64,320},{128,384},{192,448},{256,0},{320,64},{384,128},{4... | collective-permute-start | bytes 393224 | tf_op jit(solution)/shard_map/ppermute | solution.py:352
  74.8 4.1 %collective-permute-done.4.came_ref = bf16[128,512]{1,0:T(8,128)(2,1)S(1)} collective-permute-done((bf16[128,512]{1,0:T(8,128)(2,1)S(1)}, bf16[128,512]{1,0:T(8,128)(2,1)S(1)}, u32[]{:S(2)}, u32[]{:S(2)}) %collective-permute-start.4) | collective-permute-done | bytes 131104 | tf_op jit(solution)/shard_map/ppermute | solution.py:352
  78.9 0.5 all-to-all-done.3.parts_ref
  79.4 0.7 shard_map.84
  (8 shorter events, 0.0 us)
Async XLA Ops:
  2.4 18.7 %copy-start = (bf16[9,512,128]{2,1,0:T(8,128)(2,1)S(1)}, bf16[9,512,128]{2,1,0:T(8,128)(2,1)}, u32[]{:S(2)}) copy-start(bf16[9,512,128]{2,1,0:T(8,128)(2,1)} %weight_ref.3) | copy-start | bytes 3538948
  2.4 18.7 %copy-start.1 = (bf16[128,512]{1,0:T(8,128)(2,1)S(1)}, bf16[128,512]{1,0:T(8,128)(2,1)}, u32[]{:S(2)}) copy-start(bf16[128,512]{1,0:T(8,128)(2,1)} %projection_ref.3) | copy-start | bytes 393220
  33.7 4.3 %collective-permute-start = (bf16[256,1152]{1,0:T(8,128)(2,1)S(1)}, bf16[256,1152]{1,0:T(8,128)(2,1)S(1)}, u32[]{:S(2)}, u32[]{:S(2)}) collective-permute-start(bf16[256,1152]{1,0:T(8,128)(2,1)S(1)} %get-tuple-element.27), channel_id=1, source_target_pairs={{0,1},{1,0},{2,3},{3,2},{4,5},{5,4},{6,7},{7,6},{8,9},{9,8},{10,11... | collective-permute-start | bytes 1769480 | tf_op jit(solution)/shard_map/ppermute | solution.py:269
  38.9 16.5 %all-to-all-start.2 = ((bf16[4,64,1152]{2,1,0:T(8,128)(2,1)}), bf16[4,64,1152]{2,1,0:T(8,128)(2,1)S(1)}, u32[]{:S(2)}, u32[]{:S(2)}) async-start(bf16[4,64,1152]{2,1,0:T(8,128)(2,1)} %shard_map.80), calls=%async_computation.2 | async-start | bytes 1179648 | tf_op jit(solution)/shard_map/all_to_all | solution.py:325
  44.5 27.3 %collective-permute-start.1 = (bf16[2,128,512]{2,1,0:T(8,128)(2,1)S(1)}, bf16[2,128,512]{2,1,0:T(8,128)(2,1)S(1)}, u32[]{:S(2)}, u32[]{:S(2)}) collective-permute-start(bf16[2,128,512]{2,1,0:T(8,128)(2,1)S(1)} %get-tuple-element.29), channel_id=1, source_target_pairs={{0,64},{64,0},{128,192},{192,128},{256,320},{320,256},{384,448},{4... | collective-permute-start | bytes 786440 | tf_op jit(solution)/shard_map/ppermute | solution.py:337
  47.3 24.5 %collective-permute-start.2 = (bf16[2,128,512]{2,1,0:T(8,128)(2,1)S(1)}, bf16[2,128,512]{2,1,0:T(8,128)(2,1)S(1)}, u32[]{:S(2)}, u32[]{:S(2)}) collective-permute-start(bf16[2,128,512]{2,1,0:T(8,128)(2,1)S(1)} %get-tuple-element.30), channel_id=1, source_target_pairs={{0,192},{64,128},{128,64},{192,0},{256,448},{320,384},{384,320},{4... | collective-permute-start | bytes 786440 | tf_op jit(solution)/shard_map/ppermute | solution.py:337
  50.0 22.0 %collective-permute-start.3 = (bf16[2,128,512]{2,1,0:T(8,128)(2,1)S(1)}, bf16[2,128,512]{2,1,0:T(8,128)(2,1)S(1)}, u32[]{:S(2)}, u32[]{:S(2)}) collective-permute-start(bf16[2,128,512]{2,1,0:T(8,128)(2,1)S(1)} %get-tuple-element.31), channel_id=1, source_target_pairs={{0,128},{64,192},{128,0},{192,64},{256,384},{320,448},{384,256},{4... | collective-permute-start | bytes 786440 | tf_op jit(solution)/shard_map/ppermute | solution.py:337
  56.1 23.3 %all-to-all-start.3 = ((bf16[8,8,1152]{2,1,0:T(8,128)(2,1)}), bf16[8,8,1152]{2,1,0:T(8,128)(2,1)S(1)}, u32[]{:S(2)}, u32[]{:S(2)}) async-start(bf16[8,8,1152]{2,1,0:T(8,128)(2,1)} %bitcast.3), calls=%async_computation.3 | async-start | bytes 294912 | tf_op jit(solution)/shard_map/all_to_all | solution.py:333
  72.0 6.9 %collective-permute-start.4 = (bf16[128,512]{1,0:T(8,128)(2,1)S(1)}, bf16[128,512]{1,0:T(8,128)(2,1)S(1)}, u32[]{:S(2)}, u32[]{:S(2)}) collective-permute-start(bf16[128,512]{1,0:T(8,128)(2,1)S(1)} %get-tuple-element.33), channel_id=1, source_target_pairs={{0,256},{64,320},{128,384},{192,448},{256,0},{320,64},{384,128},{4... | collective-permute-start | bytes 393224 | tf_op jit(solution)/shard_map/ppermute | solution.py:352

commit v7 on v6

--- a/solution.py
+++ b/solution.py
@@ -26,7 +26,7 @@
 last_member = clips - 1
 blk_order = [last_member - p for p in range(clips)]
 heights = 8
-far_order = [5, 4, 3, 6, 2, 7, 1, 0]
+far_order = [5, 4, 3, 2, 1, 0, 7, 6]
 vmem_limit = 40 * 1024 * 1024
 HBM = pl.BlockSpec(memory_space=pltpu.HBM)
 VMEM = pl.BlockSpec(memory_space=pltpu.VMEM)
@@ -161,9 +161,8 @@
     projection_ref,
     turned_ref,
     text_ref,
-    pre_ref,
+    shifted_ref,
     sent_ref,
-    shifted_ref,
 ):
     core = lax.axis_index("core")
     embed = projection_ref.shape[1]
@@ -205,15 +204,14 @@
     scaled = pooled_grad * (1.0 / cells)
     pre_grad = (scaled[:, None, :] * slope_ref[...].reshape(clips, cells, width)).astype(bf16)
     pre_grad = pre_grad.astype(f32).reshape(clips * cells, width)
-    pre_ref[...] = pre_grad.astype(bf16)
     shifted = shift_all(pre_grad, shifted_ref)
     sent_ref[...] = jnp.dot(turned_ref[1 - core], shifted, preferred_element_type=f32).astype(bf16)
 
 
-def keep_kernel(turned_ref, pre_ref, weight_ref, kept_ref, *rest):
-    out_refs, total_ref, shifted_ref = rest[:columns], rest[columns], rest[columns + 1]
+def keep_kernel(turned_ref, shifted_ref, weight_ref, kept_ref, *rest):
+    out_refs, total_ref = rest[:columns], rest[columns]
     core = lax.axis_index("core")
-    shifted = shift_all(pre_ref[...].astype(f32), shifted_ref)
+    shifted = shifted_ref[...].reshape(clips * cells, -1)
     kept_ref[...] = jnp.dot(turned_ref[core], shifted, preferred_element_type=f32)
     weight = jnp.concatenate([weight_ref[tap] for tap in range(weight_ref.shape[0])], axis=1)
     result = lax.dot_general(
@@ -297,24 +295,22 @@
         flops=matmul,
     )(group, conv_weight, projection, extra)
     parts = lax.all_to_all(partial, BLK, 0, 0, axis_index_groups=[blk_order])
-    shifted_buf = pltpu.VMEM((clips, freq, frames, wide), bf16)
-    grad_text, pre, sent = call(
+    grad_text, shifted, sent = call(
         pair_kernel,
         (
             shape((1, embed), f32),
-            shape((clips * cells, width), bf16),
+            shape((clips, freq, frames, wide), bf16),
             shape((half, wide), bf16),
         ),
-        scratch=[shifted_buf],
         flops=matmul // 2,
     )(parts, slope, projection, turned)
     kept, *columns_out = call(
         keep_kernel,
         (shape((half, wide), f32),)
         + tuple(shape((2, cells, channels), bf16) for _ in range(columns)),
-        scratch=[pltpu.VMEM((2, columns, cells, channels), bf16), shifted_buf],
+        scratch=[pltpu.VMEM((2, columns, cells, channels), bf16)],
         flops=matmul + matmul // 2,
-    )(turned, pre, conv_weight)
+    )(turned, shifted, conv_weight)
     came = swap(sent, "core")
     sent = call(
         pair_sum_kernel,

time: 81.4 us -> 80.6 us (level)
  no operation moved by 1% of the time
where the time goes in v7:
time: 80.6 us; the launch traced here: 80.1 us
  starting transfers between devices  35.8 us (44%)
  blocking collectives  27.9 us (35%)
  Pallas kernels  8.12 us (10%)
  waiting for transfers between devices  5.69 us (7%)
  between operations  1.43 us (2%)
  other arithmetic  1.01 us (1%)
    all_to_all x1, blocking collectives, shards(): group = lax.all_to_all(copies, BLK, 0, 0, axis_index_groups=[blk_order])  18.6 us
    all_to_all x1, starting transfers between devices, shards(): lax.all_to_all(sent.reshape(heights, quarter // heights, wide), FAR, 0, 0...  15.7 us
    ppermute x3, starting transfers between devices, shards(): lax.ppermute(columns_out[d], BLK, [(i, i ^ d) for i in range(clips)])  9.81 us
    all_to_all x1, blocking collectives, shards(): parts = lax.all_to_all(partial, BLK, 0, 0, axis_index_groups=[blk_order])  9.29 us
    all_to_all x1, starting transfers between devices, shards(): parts = lax.all_to_all(sent, NEAR, 0, 0)  5.63 us
    ppermute x1, waiting for transfers between devices, shards(): lax.ppermute(other, BLK, [(i, i ^ columns) for i in range(clips)])  4.09 us
    ppermute x1, starting transfers between devices, shards(): lax.ppermute(other, BLK, [(i, i ^ columns) for i in range(clips)])  2.77 us
    pallas_call x1, Pallas kernels, shards(): call(keep_kernel, (shape((half, wide), f32),) + tuple((shape((2, cells, c...  2.27 us
  transfers between devices with their start and end apart: 7, of which 3 were waited for; matrix products, arithmetic and copies ran while one was open for 0% of the time, Pallas kernels for 4%

profile of v7, /device:TPU:6, one launch (start us, length us, event | category | flops | bytes accessed | tf_op | source)
XLA Modules:
  0.0 80.1 jit_solution(4510271467979690451)
XLA Ops:
  1.3 0.1 pad.2.clone
  1.4 1.0 %maximum_maximum_fusion.own_ref = bf16[144,512]{1,0:T(8,128)(2,1)S(1)} fusion(bf16[1,512]{1,0:T(2,128)(2,1)} %bitcast.7, bf16[128,512]{1,0:T(8,128)(2,1)} %bitcast.6, bf16[144]{0:T(256)(128)(2,1)S(1)} %pad.2.clone), kind=kLoop, calls=%fused_computation | loop fusion | flops 442368 | bytes 279840 | tf_op jit(solution)/shard_map/concatenate | solution.py:277
  2.4 0.0 copy-start
  2.4 0.1 shard_map.76
  2.5 18.6 %all_to_all.20.group_ref = bf16[8,128,512]{2,1,0:T(8,128)(2,1)S(1)} all-to-all(bf16[8,128,512]{2,1,0:T(8,128)(2,1)S(1)} %get-tuple-element.20), channel_id=1, replica_groups={{448,384,320,256,192,128,64,0},{449,385,321,257,193,129,65,1},{450,386,..., dimensions={0} | all-to-all | bytes 2097152 | tf_op jit(solution)/shard_map/all_to_all | solution.py:287
  21.1 1.8 %shard_map.77 = (f32[1024,128]{1,0:T(8,128)S(1)}, bf16[2,256,1024]{2,1,0:T(8,128)(2,1)S(1)}, f32[8,8,640]{2,1,0:T(8,128)S(1)}) custom-call(bf16[8,128,512]{2,1,0:T(8,128)(2,1)S(1)} %all_to_all.20.group_ref, bf16[9,512,128]{2,1,0:T(8,128)(2,1)S(1)} %copy-done, bf16[128,512]{1,0:T(8,128)(2,1)S(1)} %copy-done.1, f32[8,128]{1,0:T(8,128)S(1)} %get-tuple-element.21.extra_ref), custom_call_target="tpu_custom_call" | custom-call | flops 1207959552 | tf_op jit(solution)/shard_map/pallas_call | solution.py:288
  22.9 9.3 %all_to_all.21.parts_ref = f32[8,8,640]{2,1,0:T(8,128)S(1)} all-to-all(f32[8,8,640]{2,1,0:T(8,128)S(1)} %get-tuple-element.23), channel_id=1, replica_groups={{448,384,320,256,192,128,64,0},{449,385,321,257,193,129,65,1},{450,386,..., dimensions={0} | all-to-all | bytes 327680 | tf_op jit(solution)/shard_map/all_to_all | solution.py:297
  32.2 1.5 %shard_map.78 = (f32[1,512]{1,0:T(1,128)}, bf16[8,4,32,1152]{3,2,1,0:T(8,128)(2,1)S(1)}, bf16[256,1152]{1,0:T(8,128)(2,1)S(1)}) custom-call(f32[8,8,640]{2,1,0:T(8,128)S(1)} %all_to_all.21.parts_ref, f32[1024,128]{1,0:T(8,128)S(1)} %get-tuple-element.24.slope_ref, bf16[128,512]{1,0:T(8,128)(2,1)S(1)} %copy-done.1, ...), custom_call_target="tpu_custom_call" | custom-call | flops 603979776 | tf_op jit(solution)/shard_map/pallas_call | solution.py:298
  33.7 1.9 %collective-permute-start = (bf16[256,1152]{1,0:T(8,128)(2,1)S(1)}, bf16[256,1152]{1,0:T(8,128)(2,1)S(1)}, u32[]{:S(2)}, u32[]{:S(2)}) collective-permute-start(bf16[256,1152]{1,0:T(8,128)(2,1)S(1)} %get-tuple-element.27), channel_id=1, source_target_pairs={{0,1},{1,0},{2,3},{3,2},{4,5},{5,4},{6,7},{7,6},{8,9},{9,8},{10,11... | collective-permute-start | bytes 1769480 | tf_op jit(solution)/shard_map/ppermute | solution.py:267
  35.6 2.3 %shard_map.79 = (f32[256,1152]{1,0:T(8,128)S(1)}, bf16[2,128,512]{2,1,0:T(8,128)(2,1)S(1)}, bf16[2,128,512]{2,1,0:T(8,128)(2,1)S(1)}, bf16[2,128,512]{2,1,0:T(8,128)(2,1)S(1)}, bf16[2,128,512]{2,1,0:T(8,128)(2,1)S(1)}) custom-call(bf16[2,256,1024]{2,1,0:T(8,128)(2,1)S(1)} %get-tuple-element.22.turned_ref, ...), custom_call_target="tpu_custom_call" | custom-call | flops 1811939328 | tf_op jit(solution)/shard_map/pallas_call | solution.py:307
  37.9 0.9 %shard_map.80 = bf16[4,64,1152]{2,1,0:T(8,128)(2,1)} custom-call(f32[256,1152]{1,0:T(8,128)S(1)} %get-tuple-element.26.kept_ref, bf16[256,1152]{1,0:T(8,128)(2,1)S(1)} %collective-permute-done.came_ref), custom_call_target="tpu_custom_call" | custom-call | tf_op jit(solution)/shard_map/pallas_call | solution.py:315
  38.8 5.6 %all-to-all-start.2 = ((bf16[4,64,1152]{2,1,0:T(8,128)(2,1)}), bf16[4,64,1152]{2,1,0:T(8,128)(2,1)S(1)}, u32[]{:S(2)}, u32[]{:S(2)}) async-start(bf16[4,64,1152]{2,1,0:T(8,128)(2,1)} %shard_map.80), calls=%async_computation.2 | async-start | bytes 1179648 | tf_op jit(solution)/shard_map/all_to_all | solution.py:321
  44.5 2.8 %collective-permute-start.1 = (bf16[2,128,512]{2,1,0:T(8,128)(2,1)S(1)}, bf16[2,128,512]{2,1,0:T(8,128)(2,1)S(1)}, u32[]{:S(2)}, u32[]{:S(2)}) collective-permute-start(bf16[2,128,512]{2,1,0:T(8,128)(2,1)S(1)} %get-tuple-element.29), channel_id=1, source_target_pairs={{0,64},{64,0},{128,192},{192,128},{256,320},{320,256},{384,448},{4... | collective-permute-start | bytes 786440 | tf_op jit(solution)/shard_map/ppermute | solution.py:333
  47.2 2.6 %collective-permute-start.2 = (bf16[2,128,512]{2,1,0:T(8,128)(2,1)S(1)}, bf16[2,128,512]{2,1,0:T(8,128)(2,1)S(1)}, u32[]{:S(2)}, u32[]{:S(2)}) collective-permute-start(bf16[2,128,512]{2,1,0:T(8,128)(2,1)S(1)} %get-tuple-element.30), channel_id=1, source_target_pairs={{0,192},{64,128},{128,64},{192,0},{256,448},{320,384},{384,320},{4... | collective-permute-start | bytes 786440 | tf_op jit(solution)/shard_map/ppermute | solution.py:333
  49.9 4.4 %collective-permute-start.3 = (bf16[2,128,512]{2,1,0:T(8,128)(2,1)S(1)}, bf16[2,128,512]{2,1,0:T(8,128)(2,1)S(1)}, u32[]{:S(2)}, u32[]{:S(2)}) collective-permute-start(bf16[2,128,512]{2,1,0:T(8,128)(2,1)S(1)} %get-tuple-element.31), channel_id=1, source_target_pairs={{0,128},{64,192},{128,0},{192,64},{256,384},{320,448},{384,256},{4... | collective-permute-start | bytes 786440 | tf_op jit(solution)/shard_map/ppermute | solution.py:333
  54.3 1.0 %all-to-all-done.2.parts_ref = bf16[4,64,1152]{2,1,0:T(8,128)(2,1)S(1)} async-done(((bf16[4,64,1152]{2,1,0:T(8,128)(2,1)}), bf16[4,64,1152]{2,1,0:T(8,128)(2,1)S(1)}, u32[]{:S(2)}, u32[]{:S(2)}) %all-to-all-start.2) | async-done | bytes 589856 | tf_op jit(solution)/shard_map/all_to_all | solution.py:321
  55.3 0.7 shard_map.81
  56.0 15.7 %all-to-all-start.3 = ((bf16[8,8,1152]{2,1,0:T(8,128)(2,1)}), bf16[8,8,1152]{2,1,0:T(8,128)(2,1)S(1)}, u32[]{:S(2)}, u32[]{:S(2)}) async-start(bf16[8,8,1152]{2,1,0:T(8,128)(2,1)} %bitcast.3), calls=%async_computation.3 | async-start | bytes 294912 | tf_op jit(solution)/shard_map/all_to_all | solution.py:329
  71.8 0.1 shard_map.82.near_ref
  71.9 0.1 shard_map.83
  72.0 2.8 %collective-permute-start.4 = (bf16[128,512]{1,0:T(8,128)(2,1)S(1)}, bf16[128,512]{1,0:T(8,128)(2,1)S(1)}, u32[]{:S(2)}, u32[]{:S(2)}) collective-permute-start(bf16[128,512]{1,0:T(8,128)(2,1)S(1)} %get-tuple-element.33), channel_id=1, source_target_pairs={{0,256},{64,320},{128,384},{192,448},{256,0},{320,64},{384,128},{4... | collective-permute-start | bytes 393224 | tf_op jit(solution)/shard_map/ppermute | solution.py:348
  74.7 4.1 %collective-permute-done.4.came_ref = bf16[128,512]{1,0:T(8,128)(2,1)S(1)} collective-permute-done((bf16[128,512]{1,0:T(8,128)(2,1)S(1)}, bf16[128,512]{1,0:T(8,128)(2,1)S(1)}, u32[]{:S(2)}, u32[]{:S(2)}) %collective-permute-start.4) | collective-permute-done | bytes 131104 | tf_op jit(solution)/shard_map/ppermute | solution.py:348
  78.8 0.6 all-to-all-done.3.parts_ref
  79.4 0.7 shard_map.84
  (8 shorter events, 0.0 us)
Async XLA Ops:
  2.4 18.7 %copy-start = (bf16[9,512,128]{2,1,0:T(8,128)(2,1)S(1)}, bf16[9,512,128]{2,1,0:T(8,128)(2,1)}, u32[]{:S(2)}) copy-start(bf16[9,512,128]{2,1,0:T(8,128)(2,1)} %weight_ref.3) | copy-start | bytes 3538948
  2.4 18.7 %copy-start.1 = (bf16[128,512]{1,0:T(8,128)(2,1)S(1)}, bf16[128,512]{1,0:T(8,128)(2,1)}, u32[]{:S(2)}) copy-start(bf16[128,512]{1,0:T(8,128)(2,1)} %projection_ref.3) | copy-start | bytes 393220
  33.7 4.2 %collective-permute-start = (bf16[256,1152]{1,0:T(8,128)(2,1)S(1)}, bf16[256,1152]{1,0:T(8,128)(2,1)S(1)}, u32[]{:S(2)}, u32[]{:S(2)}) collective-permute-start(bf16[256,1152]{1,0:T(8,128)(2,1)S(1)} %get-tuple-element.27), channel_id=1, source_target_pairs={{0,1},{1,0},{2,3},{3,2},{4,5},{5,4},{6,7},{7,6},{8,9},{9,8},{10,11... | collective-permute-start | bytes 1769480 | tf_op jit(solution)/shard_map/ppermute | solution.py:267
  38.8 16.5 %all-to-all-start.2 = ((bf16[4,64,1152]{2,1,0:T(8,128)(2,1)}), bf16[4,64,1152]{2,1,0:T(8,128)(2,1)S(1)}, u32[]{:S(2)}, u32[]{:S(2)}) async-start(bf16[4,64,1152]{2,1,0:T(8,128)(2,1)} %shard_map.80), calls=%async_computation.2 | async-start | bytes 1179648 | tf_op jit(solution)/shard_map/all_to_all | solution.py:321
  44.5 27.3 %collective-permute-start.1 = (bf16[2,128,512]{2,1,0:T(8,128)(2,1)S(1)}, bf16[2,128,512]{2,1,0:T(8,128)(2,1)S(1)}, u32[]{:S(2)}, u32[]{:S(2)}) collective-permute-start(bf16[2,128,512]{2,1,0:T(8,128)(2,1)S(1)} %get-tuple-element.29), channel_id=1, source_target_pairs={{0,64},{64,0},{128,192},{192,128},{256,320},{320,256},{384,448},{4... | collective-permute-start | bytes 786440 | tf_op jit(solution)/shard_map/ppermute | solution.py:333
  47.2 24.5 %collective-permute-start.2 = (bf16[2,128,512]{2,1,0:T(8,128)(2,1)S(1)}, bf16[2,128,512]{2,1,0:T(8,128)(2,1)S(1)}, u32[]{:S(2)}, u32[]{:S(2)}) collective-permute-start(bf16[2,128,512]{2,1,0:T(8,128)(2,1)S(1)} %get-tuple-element.30), channel_id=1, source_target_pairs={{0,192},{64,128},{128,64},{192,0},{256,448},{320,384},{384,320},{4... | collective-permute-start | bytes 786440 | tf_op jit(solution)/shard_map/ppermute | solution.py:333
  49.9 22.0 %collective-permute-start.3 = (bf16[2,128,512]{2,1,0:T(8,128)(2,1)S(1)}, bf16[2,128,512]{2,1,0:T(8,128)(2,1)S(1)}, u32[]{:S(2)}, u32[]{:S(2)}) collective-permute-start(bf16[2,128,512]{2,1,0:T(8,128)(2,1)S(1)} %get-tuple-element.31), channel_id=1, source_target_pairs={{0,128},{64,192},{128,0},{192,64},{256,384},{320,448},{384,256},{4... | collective-permute-start | bytes 786440 | tf_op jit(solution)/shard_map/ppermute | solution.py:333
  56.0 23.4 %all-to-all-start.3 = ((bf16[8,8,1152]{2,1,0:T(8,128)(2,1)}), bf16[8,8,1152]{2,1,0:T(8,128)(2,1)S(1)}, u32[]{:S(2)}, u32[]{:S(2)}) async-start(bf16[8,8,1152]{2,1,0:T(8,128)(2,1)} %bitcast.3), calls=%async_computation.3 | async-start | bytes 294912 | tf_op jit(solution)/shard_map/all_to_all | solution.py:329
  72.0 6.9 %collective-permute-start.4 = (bf16[128,512]{1,0:T(8,128)(2,1)S(1)}, bf16[128,512]{1,0:T(8,128)(2,1)S(1)}, u32[]{:S(2)}, u32[]{:S(2)}) collective-permute-start(bf16[128,512]{1,0:T(8,128)(2,1)S(1)} %get-tuple-element.33), channel_id=1, source_target_pairs={{0,256},{64,320},{128,384},{192,448},{256,0},{320,64},{384,128},{4... | collective-permute-start | bytes 393224 | tf_op jit(solution)/shard_map/ppermute | solution.py:348

commit v8 on v7

--- a/solution.py
+++ b/solution.py
@@ -48,14 +48,9 @@
     )
 
 
-def copy_kernel(own_ref, copies_ref, extra_ref):
-    copies_ref[...] = jnp.broadcast_to(own_ref[:cells][None], copies_ref.shape)
-    last = own_ref[cells:].astype(f32)
-    lanes = extra_ref.shape[1]
-    pieces = last.shape[1] // lanes
-    for piece in range(pieces):
-        extra_ref[piece : piece + 1, :] = last[:1, piece * lanes : (piece + 1) * lanes]
-    extra_ref[pieces:, :] = last[8 : 8 + clips - pieces, :lanes]
+def copy_kernel(own_ref, given_ref, copies_ref, label_ref):
+    copies_ref[...] = jnp.broadcast_to(own_ref[...][None], copies_ref.shape)
+    label_ref[...] = given_ref[...]
 
 
 def frame_index(count):
@@ -74,7 +69,8 @@
     group_ref,
     weight_ref,
     projection_ref,
-    extra_ref,
+    caption_ref,
+    label_ref,
     slope_ref,
     turned_ref,
     partial_ref,
@@ -121,8 +117,16 @@
     partial = jnp.dot(pooled, projection_ref[...], preferred_element_type=f32)
     embed = partial.shape[1]
     partial_ref[:, :, :embed] = jnp.broadcast_to(partial[None], (clips, clips, embed))
-    partial_ref[:, :, embed:] = jnp.broadcast_to(
-        extra_ref[...][None], (clips, clips, extra_ref.shape[1])
+    caption = caption_ref[...].astype(f32)
+    lanes = partial_ref.shape[2] - embed
+    pieces = embed // lanes
+    for piece in range(pieces):
+        part = caption[:, piece * lanes : (piece + 1) * lanes]
+        partial_ref[:, piece : piece + 1, embed:] = jnp.broadcast_to(
+            part[None], (clips, 1, lanes)
+        )
+    partial_ref[:, pieces:, embed:] = jnp.broadcast_to(
+        label_ref[pieces:][None], (clips, clips - pieces, lanes)
     )
 
 
@@ -274,16 +278,9 @@
     half = channels // 2
     quarter = half // 4
     matmul = 2 * clips * cells * channels * wide
-    own = jnp.concatenate(
-        [
-            features.reshape(cells, channels),
-            text.reshape(1, channels),
-            jnp.broadcast_to(labels.astype(bf16), (15, channels)),
-        ]
-    )
-    copies, extra = call(
+    copies, label = call(
         copy_kernel, (shape((clips, cells, channels), bf16), shape((clips, 128), f32))
-    )(own)
+    )(features.reshape(cells, channels), jnp.broadcast_to(labels.astype(f32), (clips, 128)))
     group = lax.all_to_all(copies, BLK, 0, 0, axis_index_groups=[blk_order])
     slope, turned, partial = call(
         forward_kernel,
@@ -293,7 +290,7 @@
             shape((clips, clips, embed + 128), f32),
         ),
         flops=matmul,
-    )(group, conv_weight, projection, extra)
+    )(group, conv_weight, projection, text.reshape(1, embed), label)
     parts = lax.all_to_all(partial, BLK, 0, 0, axis_index_groups=[blk_order])
     grad_text, shifted, sent = call(
         pair_kernel,

time: 80.6 us -> 80.5 us (level)
  other arithmetic: 1.01 us -> 0 us
  local copies, waits for them, and re-layouts: 0.09 us -> 0.91 us
    concatenate x1 -> x0, other arithmetic: 1.01 us -> none  [shards(): jnp.concatenate([features.reshape(cells, channels), text.reshape(1, chann...]
    unnamed x4 -> x8, local copies, waits for them, and re-layouts: 0.01 us -> 0.91 us
where the time goes in v8:
time: 80.5 us; the launch traced here: 79.9 us
  starting transfers between devices  35.8 us (44%)
  blocking collectives  27.9 us (35%)
  Pallas kernels  8.14 us (10%)
  waiting for transfers between devices  5.69 us (7%)
  between operations  1.43 us (2%)
  local copies, waits for them, and re-layouts  0.91 us (1%)
    all_to_all x1, blocking collectives, shards(): group = lax.all_to_all(copies, BLK, 0, 0, axis_index_groups=[blk_order])  18.6 us
    all_to_all x1, starting transfers between devices, shards(): lax.all_to_all(sent.reshape(heights, quarter // heights, wide), FAR, 0, 0...  15.7 us
    ppermute x3, starting transfers between devices, shards(): lax.ppermute(columns_out[d], BLK, [(i, i ^ d) for i in range(clips)])  9.81 us
    all_to_all x1, blocking collectives, shards(): parts = lax.all_to_all(partial, BLK, 0, 0, axis_index_groups=[blk_order])  9.29 us
    all_to_all x1, starting transfers between devices, shards(): parts = lax.all_to_all(sent, NEAR, 0, 0)  5.63 us
    ppermute x1, waiting for transfers between devices, shards(): lax.ppermute(other, BLK, [(i, i ^ columns) for i in range(clips)])  4.09 us
    ppermute x1, starting transfers between devices, shards(): lax.ppermute(other, BLK, [(i, i ^ columns) for i in range(clips)])  2.76 us
    pallas_call x1, Pallas kernels, shards(): call(keep_kernel, (shape((half, wide), f32),) + tuple((shape((2, cells, c...  2.27 us
  transfers between devices with their start and end apart: 7, of which 3 were waited for; matrix products, arithmetic and copies ran while one was open for 0% of the time, Pallas kernels for 4%

profile of v8, /device:TPU:6, one launch (start us, length us, event | category | flops | bytes accessed | tf_op | source)
XLA Modules:
  0.0 79.9 jit_solution(18167473415652147713)
XLA Ops:
  1.3 0.0 copy-start
  1.3 0.9 %copy-done = bf16[1,1,4,32,512]{4,3,2,1,0:T(8,128)(2,1)S(1)} copy-done((bf16[1,1,4,32,512]{4,3,2,1,0:T(8,128)(2,1)S(1)}, bf16[1,1,4,32,512]{4,3,2,1,0:T(8,128)(2,1)}, u32[]{:S(2)}) %copy-start) | copy-done | bytes 131096
  2.2 0.1 shard_map.76
  2.3 18.6 %all_to_all.20.group_ref = bf16[8,128,512]{2,1,0:T(8,128)(2,1)S(1)} all-to-all(bf16[8,128,512]{2,1,0:T(8,128)(2,1)S(1)} %get-tuple-element.20), channel_id=1, replica_groups={{448,384,320,256,192,128,64,0},{449,385,321,257,193,129,65,1},{450,386,..., dimensions={0} | all-to-all | bytes 2097152 | tf_op jit(solution)/shard_map/all_to_all | solution.py:284
  20.9 1.8 %shard_map.77 = (f32[1024,128]{1,0:T(8,128)S(1)}, bf16[2,256,1024]{2,1,0:T(8,128)(2,1)S(1)}, f32[8,8,640]{2,1,0:T(8,128)S(1)}) custom-call(bf16[8,128,512]{2,1,0:T(8,128)(2,1)S(1)} %all_to_all.20.group_ref, bf16[9,512,128]{2,1,0:T(8,128)(2,1)S(1)} %copy-done.1, bf16[128,512]{1,0:T(8,128)(2,1)S(1)} %copy-done.2, bf16[1,512]{1,0:T(2,128)(2,1)S(1)} %bitcast.7, ...), custom_call_target="tpu_custom_call" | custom-call | flops 1207959552 | tf_op jit(solution)/shard_map/pallas_call | solution.py:285
  22.7 9.3 %all_to_all.21.parts_ref = f32[8,8,640]{2,1,0:T(8,128)S(1)} all-to-all(f32[8,8,640]{2,1,0:T(8,128)S(1)} %get-tuple-element.23), channel_id=1, replica_groups={{448,384,320,256,192,128,64,0},{449,385,321,257,193,129,65,1},{450,386,..., dimensions={0} | all-to-all | bytes 327680 | tf_op jit(solution)/shard_map/all_to_all | solution.py:294
  32.0 1.5 %shard_map.78 = (f32[1,512]{1,0:T(1,128)}, bf16[8,4,32,1152]{3,2,1,0:T(8,128)(2,1)S(1)}, bf16[256,1152]{1,0:T(8,128)(2,1)S(1)}) custom-call(f32[8,8,640]{2,1,0:T(8,128)S(1)} %all_to_all.21.parts_ref, f32[1024,128]{1,0:T(8,128)S(1)} %get-tuple-element.24.slope_ref, bf16[128,512]{1,0:T(8,128)(2,1)S(1)} %copy-done.2, ...), custom_call_target="tpu_custom_call" | custom-call | flops 603979776 | tf_op jit(solution)/shard_map/pallas_call | solution.py:295
  33.5 1.9 %collective-permute-start = (bf16[256,1152]{1,0:T(8,128)(2,1)S(1)}, bf16[256,1152]{1,0:T(8,128)(2,1)S(1)}, u32[]{:S(2)}, u32[]{:S(2)}) collective-permute-start(bf16[256,1152]{1,0:T(8,128)(2,1)S(1)} %get-tuple-element.27), channel_id=1, source_target_pairs={{0,1},{1,0},{2,3},{3,2},{4,5},{5,4},{6,7},{7,6},{8,9},{9,8},{10,11... | collective-permute-start | bytes 1769480 | tf_op jit(solution)/shard_map/ppermute | solution.py:271
  35.5 2.3 %shard_map.79 = (f32[256,1152]{1,0:T(8,128)S(1)}, bf16[2,128,512]{2,1,0:T(8,128)(2,1)S(1)}, bf16[2,128,512]{2,1,0:T(8,128)(2,1)S(1)}, bf16[2,128,512]{2,1,0:T(8,128)(2,1)S(1)}, bf16[2,128,512]{2,1,0:T(8,128)(2,1)S(1)}) custom-call(bf16[2,256,1024]{2,1,0:T(8,128)(2,1)S(1)} %get-tuple-element.22.turned_ref, ...), custom_call_target="tpu_custom_call" | custom-call | flops 1811939328 | tf_op jit(solution)/shard_map/pallas_call | solution.py:304
  37.7 0.0 collective-permute-done.came_ref
  37.8 0.9 %shard_map.80 = bf16[4,64,1152]{2,1,0:T(8,128)(2,1)} custom-call(f32[256,1152]{1,0:T(8,128)S(1)} %get-tuple-element.26.kept_ref, bf16[256,1152]{1,0:T(8,128)(2,1)S(1)} %collective-permute-done.came_ref), custom_call_target="tpu_custom_call" | custom-call | tf_op jit(solution)/shard_map/pallas_call | solution.py:312
  38.7 5.6 %all-to-all-start.2 = ((bf16[4,64,1152]{2,1,0:T(8,128)(2,1)}), bf16[4,64,1152]{2,1,0:T(8,128)(2,1)S(1)}, u32[]{:S(2)}, u32[]{:S(2)}) async-start(bf16[4,64,1152]{2,1,0:T(8,128)(2,1)} %shard_map.80), calls=%async_computation.2 | async-start | bytes 1179648 | tf_op jit(solution)/shard_map/all_to_all | solution.py:318
  44.3 2.7 %collective-permute-start.1 = (bf16[2,128,512]{2,1,0:T(8,128)(2,1)S(1)}, bf16[2,128,512]{2,1,0:T(8,128)(2,1)S(1)}, u32[]{:S(2)}, u32[]{:S(2)}) collective-permute-start(bf16[2,128,512]{2,1,0:T(8,128)(2,1)S(1)} %get-tuple-element.29), channel_id=1, source_target_pairs={{0,64},{64,0},{128,192},{192,128},{256,320},{320,256},{384,448},{4... | collective-permute-start | bytes 786440 | tf_op jit(solution)/shard_map/ppermute | solution.py:330
  47.0 2.6 %collective-permute-start.2 = (bf16[2,128,512]{2,1,0:T(8,128)(2,1)S(1)}, bf16[2,128,512]{2,1,0:T(8,128)(2,1)S(1)}, u32[]{:S(2)}, u32[]{:S(2)}) collective-permute-start(bf16[2,128,512]{2,1,0:T(8,128)(2,1)S(1)} %get-tuple-element.30), channel_id=1, source_target_pairs={{0,192},{64,128},{128,64},{192,0},{256,448},{320,384},{384,320},{4... | collective-permute-start | bytes 786440 | tf_op jit(solution)/shard_map/ppermute | solution.py:330
  49.7 4.4 %collective-permute-start.3 = (bf16[2,128,512]{2,1,0:T(8,128)(2,1)S(1)}, bf16[2,128,512]{2,1,0:T(8,128)(2,1)S(1)}, u32[]{:S(2)}, u32[]{:S(2)}) collective-permute-start(bf16[2,128,512]{2,1,0:T(8,128)(2,1)S(1)} %get-tuple-element.31), channel_id=1, source_target_pairs={{0,128},{64,192},{128,0},{192,64},{256,384},{320,448},{384,256},{4... | collective-permute-start | bytes 786440 | tf_op jit(solution)/shard_map/ppermute | solution.py:330
  54.1 1.0 %all-to-all-done.2.parts_ref = bf16[4,64,1152]{2,1,0:T(8,128)(2,1)S(1)} async-done(((bf16[4,64,1152]{2,1,0:T(8,128)(2,1)}), bf16[4,64,1152]{2,1,0:T(8,128)(2,1)S(1)}, u32[]{:S(2)}, u32[]{:S(2)}) %all-to-all-start.2) | async-done | bytes 589856 | tf_op jit(solution)/shard_map/all_to_all | solution.py:318
  55.1 0.8 shard_map.81
  55.9 15.7 %all-to-all-start.3 = ((bf16[8,8,1152]{2,1,0:T(8,128)(2,1)}), bf16[8,8,1152]{2,1,0:T(8,128)(2,1)S(1)}, u32[]{:S(2)}, u32[]{:S(2)}) async-start(bf16[8,8,1152]{2,1,0:T(8,128)(2,1)} %bitcast.3), calls=%async_computation.3 | async-start | bytes 294912 | tf_op jit(solution)/shard_map/all_to_all | solution.py:326
  71.6 0.1 shard_map.82.near_ref
  71.7 0.1 shard_map.83
  71.8 2.8 %collective-permute-start.4 = (bf16[128,512]{1,0:T(8,128)(2,1)S(1)}, bf16[128,512]{1,0:T(8,128)(2,1)S(1)}, u32[]{:S(2)}, u32[]{:S(2)}) collective-permute-start(bf16[128,512]{1,0:T(8,128)(2,1)S(1)} %get-tuple-element.33), channel_id=1, source_target_pairs={{0,256},{64,320},{128,384},{192,448},{256,0},{320,64},{384,128},{4... | collective-permute-start | bytes 393224 | tf_op jit(solution)/shard_map/ppermute | solution.py:345
  74.6 4.1 %collective-permute-done.4.came_ref = bf16[128,512]{1,0:T(8,128)(2,1)S(1)} collective-permute-done((bf16[128,512]{1,0:T(8,128)(2,1)S(1)}, bf16[128,512]{1,0:T(8,128)(2,1)S(1)}, u32[]{:S(2)}, u32[]{:S(2)}) %collective-permute-start.4) | collective-permute-done | bytes 131104 | tf_op jit(solution)/shard_map/ppermute | solution.py:345
  78.7 0.6 all-to-all-done.3.parts_ref
  79.2 0.7 shard_map.84
  (10 shorter events, 0.0 us)
Async XLA Ops:
  0.6 20.3 %copy-start.3 = (bf16[1,1,512]{2,1,0:T(2,128)(2,1)S(1)}, bf16[1,1,512]{2,1,0:T(2,128)(2,1)}, u32[]{:S(2)}) copy-start(bf16[1,1,512]{2,1,0:T(2,128)(2,1)} %param.8) | copy-start | bytes 3076
  1.3 0.9 %copy-start = (bf16[1,1,4,32,512]{4,3,2,1,0:T(8,128)(2,1)S(1)}, bf16[1,1,4,32,512]{4,3,2,1,0:T(8,128)(2,1)}, u32[]{:S(2)}) copy-start(bf16[1,1,4,32,512]{4,3,2,1,0:T(8,128)(2,1)} %param.5) | copy-start | bytes 393220
  2.2 18.7 %copy-start.1 = (bf16[9,512,128]{2,1,0:T(8,128)(2,1)S(1)}, bf16[9,512,128]{2,1,0:T(8,128)(2,1)}, u32[]{:S(2)}) copy-start(bf16[9,512,128]{2,1,0:T(8,128)(2,1)} %weight_ref.3) | copy-start | bytes 3538948
  2.2 18.7 %copy-start.2 = (bf16[128,512]{1,0:T(8,128)(2,1)S(1)}, bf16[128,512]{1,0:T(8,128)(2,1)}, u32[]{:S(2)}) copy-start(bf16[128,512]{1,0:T(8,128)(2,1)} %projection_ref.3) | copy-start | bytes 393220
  33.5 4.2 %collective-permute-start = (bf16[256,1152]{1,0:T(8,128)(2,1)S(1)}, bf16[256,1152]{1,0:T(8,128)(2,1)S(1)}, u32[]{:S(2)}, u32[]{:S(2)}) collective-permute-start(bf16[256,1152]{1,0:T(8,128)(2,1)S(1)} %get-tuple-element.27), channel_id=1, source_target_pairs={{0,1},{1,0},{2,3},{3,2},{4,5},{5,4},{6,7},{7,6},{8,9},{9,8},{10,11... | collective-permute-start | bytes 1769480 | tf_op jit(solution)/shard_map/ppermute | solution.py:271
  38.7 16.5 %all-to-all-start.2 = ((bf16[4,64,1152]{2,1,0:T(8,128)(2,1)}), bf16[4,64,1152]{2,1,0:T(8,128)(2,1)S(1)}, u32[]{:S(2)}, u32[]{:S(2)}) async-start(bf16[4,64,1152]{2,1,0:T(8,128)(2,1)} %shard_map.80), calls=%async_computation.2 | async-start | bytes 1179648 | tf_op jit(solution)/shard_map/all_to_all | solution.py:318
  44.3 27.3 %collective-permute-start.1 = (bf16[2,128,512]{2,1,0:T(8,128)(2,1)S(1)}, bf16[2,128,512]{2,1,0:T(8,128)(2,1)S(1)}, u32[]{:S(2)}, u32[]{:S(2)}) collective-permute-start(bf16[2,128,512]{2,1,0:T(8,128)(2,1)S(1)} %get-tuple-element.29), channel_id=1, source_target_pairs={{0,64},{64,0},{128,192},{192,128},{256,320},{320,256},{384,448},{4... | collective-permute-start | bytes 786440 | tf_op jit(solution)/shard_map/ppermute | solution.py:330
  47.0 24.6 %collective-permute-start.2 = (bf16[2,128,512]{2,1,0:T(8,128)(2,1)S(1)}, bf16[2,128,512]{2,1,0:T(8,128)(2,1)S(1)}, u32[]{:S(2)}, u32[]{:S(2)}) collective-permute-start(bf16[2,128,512]{2,1,0:T(8,128)(2,1)S(1)} %get-tuple-element.30), channel_id=1, source_target_pairs={{0,192},{64,128},{128,64},{192,0},{256,448},{320,384},{384,320},{4... | collective-permute-start | bytes 786440 | tf_op jit(solution)/shard_map/ppermute | solution.py:330
  49.7 22.0 %collective-permute-start.3 = (bf16[2,128,512]{2,1,0:T(8,128)(2,1)S(1)}, bf16[2,128,512]{2,1,0:T(8,128)(2,1)S(1)}, u32[]{:S(2)}, u32[]{:S(2)}) collective-permute-start(bf16[2,128,512]{2,1,0:T(8,128)(2,1)S(1)} %get-tuple-element.31), channel_id=1, source_target_pairs={{0,128},{64,192},{128,0},{192,64},{256,384},{320,448},{384,256},{4... | collective-permute-start | bytes 786440 | tf_op jit(solution)/shard_map/ppermute | solution.py:330
  55.9 23.4 %all-to-all-start.3 = ((bf16[8,8,1152]{2,1,0:T(8,128)(2,1)}), bf16[8,8,1152]{2,1,0:T(8,128)(2,1)S(1)}, u32[]{:S(2)}, u32[]{:S(2)}) async-start(bf16[8,8,1152]{2,1,0:T(8,128)(2,1)} %bitcast.3), calls=%async_computation.3 | async-start | bytes 294912 | tf_op jit(solution)/shard_map/all_to_all | solution.py:326
  71.8 6.9 %collective-permute-start.4 = (bf16[128,512]{1,0:T(8,128)(2,1)S(1)}, bf16[128,512]{1,0:T(8,128)(2,1)S(1)}, u32[]{:S(2)}, u32[]{:S(2)}) collective-permute-start(bf16[128,512]{1,0:T(8,128)(2,1)S(1)} %get-tuple-element.33), channel_id=1, source_target_pairs={{0,256},{64,320},{128,384},{192,448},{256,0},{320,64},{384,128},{4... | collective-permute-start | bytes 393224 | tf_op jit(solution)/shard_map/ppermute | solution.py:345

commit v9 on v8

--- a/solution.py
+++ b/solution.py
@@ -25,6 +25,7 @@
 columns = 4
 last_member = clips - 1
 blk_order = [last_member - p for p in range(clips)]
+gather_order = [6, 7, 5, 4, 2, 3, 1, 0]
 heights = 8
 far_order = [5, 4, 3, 2, 1, 0, 7, 6]
 vmem_limit = 40 * 1024 * 1024
@@ -75,7 +76,7 @@
     turned_ref,
     partial_ref,
 ):
-    inputs = group_ref[...].reshape(clips * cells, -1)
+    inputs = jnp.concatenate([group_ref[gather_order.index(member)] for member in blk_order])
     turned = inputs.T.astype(f32).reshape(2, heights, 2, 2, 8, clips * cells)
     turned = jnp.concatenate([turned[:, z : z + 1] for z in far_order], axis=1)
     block = heights * 8
@@ -281,7 +282,7 @@
     copies, label = call(
         copy_kernel, (shape((clips, cells, channels), bf16), shape((clips, 128), f32))
     )(features.reshape(cells, channels), jnp.broadcast_to(labels.astype(f32), (clips, 128)))
-    group = lax.all_to_all(copies, BLK, 0, 0, axis_index_groups=[blk_order])
+    group = lax.all_to_all(copies, BLK, 0, 0, axis_index_groups=[gather_order])
     slope, turned, partial = call(
         forward_kernel,
         (

time: 80.5 us -> 80.1 us (level)
  no operation moved by 1% of the time
where the time goes in v9:
time: 80.1 us; the launch traced here: 79.6 us
  starting transfers between devices  35.8 us (45%)
  blocking collectives  27.6 us (34%)
  Pallas kernels  8.14 us (10%)
  waiting for transfers between devices  5.69 us (7%)
  between operations  1.43 us (2%)
  local copies, waits for them, and re-layouts  0.91 us (1%)
    all_to_all x1, blocking collectives, shards(): group = lax.all_to_all(copies, BLK, 0, 0, axis_index_groups=[gather_order])  18.3 us
    all_to_all x1, starting transfers between devices, shards(): lax.all_to_all(sent.reshape(heights, quarter // heights, wide), FAR, 0, 0...  15.7 us
    ppermute x3, starting transfers between devices, shards(): lax.ppermute(columns_out[d], BLK, [(i, i ^ d) for i in range(clips)])  9.81 us
    all_to_all x1, blocking collectives, shards(): parts = lax.all_to_all(partial, BLK, 0, 0, axis_index_groups=[blk_order])  9.3 us
    all_to_all x1, starting transfers between devices, shards(): parts = lax.all_to_all(sent, NEAR, 0, 0)  5.63 us
    ppermute x1, waiting for transfers between devices, shards(): lax.ppermute(other, BLK, [(i, i ^ columns) for i in range(clips)])  4.08 us
    ppermute x1, starting transfers between devices, shards(): lax.ppermute(other, BLK, [(i, i ^ columns) for i in range(clips)])  2.77 us
    pallas_call x1, Pallas kernels, shards(): call(keep_kernel, (shape((half, wide), f32),) + tuple((shape((2, cells, c...  2.27 us
  transfers between devices with their start and end apart: 7, of which 3 were waited for; matrix products, arithmetic and copies ran while one was open for 0% of the time, Pallas kernels for 4%

profile of v9, /device:TPU:6, one launch (start us, length us, event | category | flops | bytes accessed | tf_op | source)
XLA Modules:
  0.0 79.6 jit_solution(5162312108812460573)
XLA Ops:
  1.3 0.0 copy-start
  1.3 0.9 %copy-done = bf16[1,1,4,32,512]{4,3,2,1,0:T(8,128)(2,1)S(1)} copy-done((bf16[1,1,4,32,512]{4,3,2,1,0:T(8,128)(2,1)S(1)}, bf16[1,1,4,32,512]{4,3,2,1,0:T(8,128)(2,1)}, u32[]{:S(2)}) %copy-start) | copy-done | bytes 131096
  2.2 0.1 shard_map.76
  2.3 18.3 %all_to_all.20.group_ref = bf16[8,128,512]{2,1,0:T(8,128)(2,1)S(1)} all-to-all(bf16[8,128,512]{2,1,0:T(8,128)(2,1)S(1)} %get-tuple-element.20), channel_id=1, replica_groups={{384,448,320,256,128,192,64,0},{385,449,321,257,129,193,65,1},{386,450,..., dimensions={0} | all-to-all | bytes 2097152 | tf_op jit(solution)/shard_map/all_to_all | solution.py:285
  20.6 1.8 %shard_map.77 = (f32[1024,128]{1,0:T(8,128)S(1)}, bf16[2,256,1024]{2,1,0:T(8,128)(2,1)S(1)}, f32[8,8,640]{2,1,0:T(8,128)S(1)}) custom-call(bf16[8,128,512]{2,1,0:T(8,128)(2,1)S(1)} %all_to_all.20.group_ref, bf16[9,512,128]{2,1,0:T(8,128)(2,1)S(1)} %copy-done.1, bf16[128,512]{1,0:T(8,128)(2,1)S(1)} %copy-done.2, bf16[1,512]{1,0:T(2,128)(2,1)S(1)} %bitcast.7, ...), custom_call_target="tpu_custom_call" | custom-call | flops 1207959552 | tf_op jit(solution)/shard_map/pallas_call | solution.py:286
  22.4 9.3 %all_to_all.21.parts_ref = f32[8,8,640]{2,1,0:T(8,128)S(1)} all-to-all(f32[8,8,640]{2,1,0:T(8,128)S(1)} %get-tuple-element.23), channel_id=1, replica_groups={{448,384,320,256,192,128,64,0},{449,385,321,257,193,129,65,1},{450,386,..., dimensions={0} | all-to-all | bytes 327680 | tf_op jit(solution)/shard_map/all_to_all | solution.py:295
  31.7 1.5 %shard_map.78 = (f32[1,512]{1,0:T(1,128)}, bf16[8,4,32,1152]{3,2,1,0:T(8,128)(2,1)S(1)}, bf16[256,1152]{1,0:T(8,128)(2,1)S(1)}) custom-call(f32[8,8,640]{2,1,0:T(8,128)S(1)} %all_to_all.21.parts_ref, f32[1024,128]{1,0:T(8,128)S(1)} %get-tuple-element.24.slope_ref, bf16[128,512]{1,0:T(8,128)(2,1)S(1)} %copy-done.2, ...), custom_call_target="tpu_custom_call" | custom-call | flops 603979776 | tf_op jit(solution)/shard_map/pallas_call | solution.py:296
  33.2 1.9 %collective-permute-start = (bf16[256,1152]{1,0:T(8,128)(2,1)S(1)}, bf16[256,1152]{1,0:T(8,128)(2,1)S(1)}, u32[]{:S(2)}, u32[]{:S(2)}) collective-permute-start(bf16[256,1152]{1,0:T(8,128)(2,1)S(1)} %get-tuple-element.27), channel_id=1, source_target_pairs={{0,1},{1,0},{2,3},{3,2},{4,5},{5,4},{6,7},{7,6},{8,9},{9,8},{10,11... | collective-permute-start | bytes 1769480 | tf_op jit(solution)/shard_map/ppermute | solution.py:272
  35.1 2.3 %shard_map.79 = (f32[256,1152]{1,0:T(8,128)S(1)}, bf16[2,128,512]{2,1,0:T(8,128)(2,1)S(1)}, bf16[2,128,512]{2,1,0:T(8,128)(2,1)S(1)}, bf16[2,128,512]{2,1,0:T(8,128)(2,1)S(1)}, bf16[2,128,512]{2,1,0:T(8,128)(2,1)S(1)}) custom-call(bf16[2,256,1024]{2,1,0:T(8,128)(2,1)S(1)} %get-tuple-element.22.turned_ref, ...), custom_call_target="tpu_custom_call" | custom-call | flops 1811939328 | tf_op jit(solution)/shard_map/pallas_call | solution.py:305
  37.4 0.0 collective-permute-done.came_ref
  37.4 0.9 %shard_map.80 = bf16[4,64,1152]{2,1,0:T(8,128)(2,1)} custom-call(f32[256,1152]{1,0:T(8,128)S(1)} %get-tuple-element.26.kept_ref, bf16[256,1152]{1,0:T(8,128)(2,1)S(1)} %collective-permute-done.came_ref), custom_call_target="tpu_custom_call" | custom-call | tf_op jit(solution)/shard_map/pallas_call | solution.py:313
  38.3 5.6 %all-to-all-start.2 = ((bf16[4,64,1152]{2,1,0:T(8,128)(2,1)}), bf16[4,64,1152]{2,1,0:T(8,128)(2,1)S(1)}, u32[]{:S(2)}, u32[]{:S(2)}) async-start(bf16[4,64,1152]{2,1,0:T(8,128)(2,1)} %shard_map.80), calls=%async_computation.2 | async-start | bytes 1179648 | tf_op jit(solution)/shard_map/all_to_all | solution.py:319
  43.9 2.7 %collective-permute-start.1 = (bf16[2,128,512]{2,1,0:T(8,128)(2,1)S(1)}, bf16[2,128,512]{2,1,0:T(8,128)(2,1)S(1)}, u32[]{:S(2)}, u32[]{:S(2)}) collective-permute-start(bf16[2,128,512]{2,1,0:T(8,128)(2,1)S(1)} %get-tuple-element.29), channel_id=1, source_target_pairs={{0,64},{64,0},{128,192},{192,128},{256,320},{320,256},{384,448},{4... | collective-permute-start | bytes 786440 | tf_op jit(solution)/shard_map/ppermute | solution.py:331
  46.7 2.6 %collective-permute-start.2 = (bf16[2,128,512]{2,1,0:T(8,128)(2,1)S(1)}, bf16[2,128,512]{2,1,0:T(8,128)(2,1)S(1)}, u32[]{:S(2)}, u32[]{:S(2)}) collective-permute-start(bf16[2,128,512]{2,1,0:T(8,128)(2,1)S(1)} %get-tuple-element.30), channel_id=1, source_target_pairs={{0,192},{64,128},{128,64},{192,0},{256,448},{320,384},{384,320},{4... | collective-permute-start | bytes 786440 | tf_op jit(solution)/shard_map/ppermute | solution.py:331
  49.3 4.4 %collective-permute-start.3 = (bf16[2,128,512]{2,1,0:T(8,128)(2,1)S(1)}, bf16[2,128,512]{2,1,0:T(8,128)(2,1)S(1)}, u32[]{:S(2)}, u32[]{:S(2)}) collective-permute-start(bf16[2,128,512]{2,1,0:T(8,128)(2,1)S(1)} %get-tuple-element.31), channel_id=1, source_target_pairs={{0,128},{64,192},{128,0},{192,64},{256,384},{320,448},{384,256},{4... | collective-permute-start | bytes 786440 | tf_op jit(solution)/shard_map/ppermute | solution.py:331
  53.8 1.0 %all-to-all-done.2.parts_ref = bf16[4,64,1152]{2,1,0:T(8,128)(2,1)S(1)} async-done(((bf16[4,64,1152]{2,1,0:T(8,128)(2,1)}), bf16[4,64,1152]{2,1,0:T(8,128)(2,1)S(1)}, u32[]{:S(2)}, u32[]{:S(2)}) %all-to-all-start.2) | async-done | bytes 589856 | tf_op jit(solution)/shard_map/all_to_all | solution.py:319
  54.8 0.8 shard_map.81
  55.5 15.7 %all-to-all-start.3 = ((bf16[8,8,1152]{2,1,0:T(8,128)(2,1)}), bf16[8,8,1152]{2,1,0:T(8,128)(2,1)S(1)}, u32[]{:S(2)}, u32[]{:S(2)}) async-start(bf16[8,8,1152]{2,1,0:T(8,128)(2,1)} %bitcast.3), calls=%async_computation.3 | async-start | bytes 294912 | tf_op jit(solution)/shard_map/all_to_all | solution.py:327
  71.2 0.1 shard_map.82.near_ref
  71.4 0.1 shard_map.83
  71.5 2.8 %collective-permute-start.4 = (bf16[128,512]{1,0:T(8,128)(2,1)S(1)}, bf16[128,512]{1,0:T(8,128)(2,1)S(1)}, u32[]{:S(2)}, u32[]{:S(2)}) collective-permute-start(bf16[128,512]{1,0:T(8,128)(2,1)S(1)} %get-tuple-element.33), channel_id=1, source_target_pairs={{0,256},{64,320},{128,384},{192,448},{256,0},{320,64},{384,128},{4... | collective-permute-start | bytes 393224 | tf_op jit(solution)/shard_map/ppermute | solution.py:346
  74.2 4.1 %collective-permute-done.4.came_ref = bf16[128,512]{1,0:T(8,128)(2,1)S(1)} collective-permute-done((bf16[128,512]{1,0:T(8,128)(2,1)S(1)}, bf16[128,512]{1,0:T(8,128)(2,1)S(1)}, u32[]{:S(2)}, u32[]{:S(2)}) %collective-permute-start.4) | collective-permute-done | bytes 131104 | tf_op jit(solution)/shard_map/ppermute | solution.py:346
  78.3 0.6 all-to-all-done.3.parts_ref
  78.9 0.7 shard_map.84
  (10 shorter events, 0.0 us)
Async XLA Ops:
  0.6 20.0 %copy-start.3 = (bf16[1,1,512]{2,1,0:T(2,128)(2,1)S(1)}, bf16[1,1,512]{2,1,0:T(2,128)(2,1)}, u32[]{:S(2)}) copy-start(bf16[1,1,512]{2,1,0:T(2,128)(2,1)} %param.8) | copy-start | bytes 3076
  1.3 0.9 %copy-start = (bf16[1,1,4,32,512]{4,3,2,1,0:T(8,128)(2,1)S(1)}, bf16[1,1,4,32,512]{4,3,2,1,0:T(8,128)(2,1)}, u32[]{:S(2)}) copy-start(bf16[1,1,4,32,512]{4,3,2,1,0:T(8,128)(2,1)} %param.5) | copy-start | bytes 393220
  2.2 18.4 %copy-start.1 = (bf16[9,512,128]{2,1,0:T(8,128)(2,1)S(1)}, bf16[9,512,128]{2,1,0:T(8,128)(2,1)}, u32[]{:S(2)}) copy-start(bf16[9,512,128]{2,1,0:T(8,128)(2,1)} %weight_ref.3) | copy-start | bytes 3538948
  2.2 18.4 %copy-start.2 = (bf16[128,512]{1,0:T(8,128)(2,1)S(1)}, bf16[128,512]{1,0:T(8,128)(2,1)}, u32[]{:S(2)}) copy-start(bf16[128,512]{1,0:T(8,128)(2,1)} %projection_ref.3) | copy-start | bytes 393220
  33.2 4.2 %collective-permute-start = (bf16[256,1152]{1,0:T(8,128)(2,1)S(1)}, bf16[256,1152]{1,0:T(8,128)(2,1)S(1)}, u32[]{:S(2)}, u32[]{:S(2)}) collective-permute-start(bf16[256,1152]{1,0:T(8,128)(2,1)S(1)} %get-tuple-element.27), channel_id=1, source_target_pairs={{0,1},{1,0},{2,3},{3,2},{4,5},{5,4},{6,7},{7,6},{8,9},{9,8},{10,11... | collective-permute-start | bytes 1769480 | tf_op jit(solution)/shard_map/ppermute | solution.py:272
  38.3 16.5 %all-to-all-start.2 = ((bf16[4,64,1152]{2,1,0:T(8,128)(2,1)}), bf16[4,64,1152]{2,1,0:T(8,128)(2,1)S(1)}, u32[]{:S(2)}, u32[]{:S(2)}) async-start(bf16[4,64,1152]{2,1,0:T(8,128)(2,1)} %shard_map.80), calls=%async_computation.2 | async-start | bytes 1179648 | tf_op jit(solution)/shard_map/all_to_all | solution.py:319
  43.9 27.3 %collective-permute-start.1 = (bf16[2,128,512]{2,1,0:T(8,128)(2,1)S(1)}, bf16[2,128,512]{2,1,0:T(8,128)(2,1)S(1)}, u32[]{:S(2)}, u32[]{:S(2)}) collective-permute-start(bf16[2,128,512]{2,1,0:T(8,128)(2,1)S(1)} %get-tuple-element.29), channel_id=1, source_target_pairs={{0,64},{64,0},{128,192},{192,128},{256,320},{320,256},{384,448},{4... | collective-permute-start | bytes 786440 | tf_op jit(solution)/shard_map/ppermute | solution.py:331
  46.7 24.5 %collective-permute-start.2 = (bf16[2,128,512]{2,1,0:T(8,128)(2,1)S(1)}, bf16[2,128,512]{2,1,0:T(8,128)(2,1)S(1)}, u32[]{:S(2)}, u32[]{:S(2)}) collective-permute-start(bf16[2,128,512]{2,1,0:T(8,128)(2,1)S(1)} %get-tuple-element.30), channel_id=1, source_target_pairs={{0,192},{64,128},{128,64},{192,0},{256,448},{320,384},{384,320},{4... | collective-permute-start | bytes 786440 | tf_op jit(solution)/shard_map/ppermute | solution.py:331
  49.3 22.0 %collective-permute-start.3 = (bf16[2,128,512]{2,1,0:T(8,128)(2,1)S(1)}, bf16[2,128,512]{2,1,0:T(8,128)(2,1)S(1)}, u32[]{:S(2)}, u32[]{:S(2)}) collective-permute-start(bf16[2,128,512]{2,1,0:T(8,128)(2,1)S(1)} %get-tuple-element.31), channel_id=1, source_target_pairs={{0,128},{64,192},{128,0},{192,64},{256,384},{320,448},{384,256},{4... | collective-permute-start | bytes 786440 | tf_op jit(solution)/shard_map/ppermute | solution.py:331
  55.5 23.3 %all-to-all-start.3 = ((bf16[8,8,1152]{2,1,0:T(8,128)(2,1)}), bf16[8,8,1152]{2,1,0:T(8,128)(2,1)S(1)}, u32[]{:S(2)}, u32[]{:S(2)}) async-start(bf16[8,8,1152]{2,1,0:T(8,128)(2,1)} %bitcast.3), calls=%async_computation.3 | async-start | bytes 294912 | tf_op jit(solution)/shard_map/all_to_all | solution.py:327
  71.5 6.9 %collective-permute-start.4 = (bf16[128,512]{1,0:T(8,128)(2,1)S(1)}, bf16[128,512]{1,0:T(8,128)(2,1)S(1)}, u32[]{:S(2)}, u32[]{:S(2)}) collective-permute-start(bf16[128,512]{1,0:T(8,128)(2,1)S(1)} %get-tuple-element.33), channel_id=1, source_target_pairs={{0,256},{64,320},{128,384},{192,448},{256,0},{320,64},{384,128},{4... | collective-permute-start | bytes 393224 | tf_op jit(solution)/shard_map/ppermute | solution.py:346
